TPU v7x, 256 devices: a whole 4x4x8 slice. The times are simulated.
256 devices in a mesh: ind: 32 (over y, x, core), snp: 8 (over z).
Axes of the slice: x: 4, y: 4, z: 8, core: 2. Of those that a mesh axis runs over, the one named last changes fastest.
Arguments:
- genotypes: int32 [65536, 4096], P('ind', 'snp'), may hold values from 0 to 2, as said below
- targets: float32 [65536, 32], P('ind'), may hold values from -16 to 16
- ridge: float32 [1], replicated, may hold values from 0.5 to 2
- held_out: int32 [32], replicated, may hold values from 0 to 65535
Outputs:
- solution: float32 [65536, 32], P('ind')
- held_values: float32 [32], replicated
Inputs may be any that keep to these rules, and one draw needn't show every extreme that they name: `held_out`: row indices of individuals. `genotypes`: each entry counts copies of one allele.
All inputs are finite; a program needn't handle non-finite values.
Results may differ from a plain program's by a relative error of at most 0.0003.
Values sent between devices are 32-bit elements; how exact they have to be, the bound alone decides.
No kernel may reach another device: no remote copies, remote signals or barrier semaphores. Data moves between devices by JAX's collectives and lax.ppermute only.
A program may use at most 64 MiB of HBM per device.

v0:
```python
import jax
import jax.numpy as jnp
from jax import lax
from jax.sharding import PartitionSpec as P

ITERS = 4


def chol_solve(gram, right):
    lower = jnp.linalg.cholesky(gram)
    inner = lax.linalg.triangular_solve(lower, right, left_side=True, lower=True)
    return lax.linalg.triangular_solve(lower, inner, left_side=True, lower=True, transpose_a=True)


def matmul(left, right):
    return jnp.dot(left, right, precision=lax.Precision.HIGHEST, preferred_element_type=jnp.float32)


def symmetric(matrix):
    return 0.5 * (matrix + matrix.T)


def shards(genotypes, targets, ridge, held_out):
    rows, cols = genotypes.shape
    total_rows = rows * lax.axis_size("ind")
    width = cols * lax.axis_size("snp")
    values = genotypes.astype(jnp.float32)
    stats = lax.psum(jnp.stack([jnp.sum(values, axis=0), jnp.sum(values * values, axis=0)]), "ind")
    mean = stats[0] / total_rows
    scale = 1.0 / jnp.sqrt(stats[1] / total_rows - mean * mean + 1e-05)
    zmat = (values - mean) * scale
    lam = ridge[0]
    resid = targets

    def grams(parts):
        return lax.psum((parts[0],), "ind")

    solution = jnp.zeros_like(resid)
    direction = resid
    norm_now = symmetric(grams((matmul(resid.T, resid),))[0])
    for step in range(ITERS):
        term = matmul(zmat, lax.psum(matmul(zmat.T, direction), "ind"))
        image = lax.psum(term, "snp") / width + lam * direction
        curvature = grams((matmul(direction.T, image),))[0]
        alpha = chol_solve(symmetric(curvature), norm_now)
        solution = solution + matmul(direction, alpha)
        resid = resid - matmul(image, alpha)
        norm_next = symmetric(grams((matmul(resid.T, resid),))[0])
        beta = chol_solve(norm_now, norm_next)
        direction = resid + matmul(direction, beta)
        norm_now = norm_next
    indices = lax.axis_index("ind") * rows + lax.broadcasted_iota(jnp.int32, (rows, 1), 0)
    selected = (indices == held_out[None, :]).astype(jnp.float32)
    held_values = lax.psum(jnp.sum(selected * solution, axis=0), "ind")
    return (solution, held_values)


def solution(mesh):
    return jax.shard_map(
        shards,
        mesh=mesh,
        in_specs=(P("ind", "snp"), P("ind", None), P(), P()),
        out_specs=(P("ind", None), P()),
        check_vma=False,
    )
```

profile of v0, /device:TPU:22, one launch (start us, length us, event | category | flops | bytes accessed | tf_op | source)
XLA Modules:
  0.0 1830.2 jit_solution(3204445344569510111)
XLA Ops:
  7.2 2.8 convert_reduce_fusion
  10.1 50.1 %psum.126 = f32[2,512]{1,0:T(2,128)S(1)} all-reduce(f32[2,512]{1,0:T(2,128)S(1)} %pad_maximum_fusion), channel_id=1, replica_groups=mesh['ind'=32,'snp'=8] {'ind'}, use_global_device_ids=true, to_apply=%region_2.0 | all-reduce | flops 1024 | bytes 8192 | tf_op jit(solution)/shard_map/psum | solution.py:28
  60.2 9.6 fusion.11
  69.8 124.3 %all-reduce.10.cloned.1.call-done = f32[512,32]{1,0:T(8,128)} async-done(((f32[512,32]{1,0:T(8,128)}), f32[512,32]{1,0:T(8,128)}) %all-reduce.10.cloned.1.call-update) | async-done | bytes 65552 | tf_op jit(solution)/shard_map/psum | solution.py:42
  194.1 7.1 fusion.10
  202.2 73.4 %all-reduce.12.cloned.1.call-done = f32[2048,32]{0,1:T(8,128)} async-done(((f32[2048,32]{0,1:T(8,128)}), f32[2048,32]{0,1:T(8,128)}) %all-reduce.12.cloned.1.call-update) | async-done | bytes 262160 | tf_op jit(solution)/shard_map/psum | solution.py:43
  275.6 1.3 convolution_bitcast_fusion.2
  276.9 99.5 %all-reduce = (f32[32,32]{1,0:T(8,128)S(1)}, f32[32,32]{1,0:T(8,128)S(1)}) all-reduce(f32[32,32]{1,0:T(8,128)S(1)} %fusion.96, f32[32,32]{1,0:T(8,128)S(1)} %convolution_bitcast_fusion.2), channel_id=1, replica_groups=mesh['ind'=32,'snp'=8] {'ind'}, use_global_device_ids=true, to_apply=%region_8.0 | all-reduce | flops 2048 | bytes 16384 | tf_op jit(solution)/shard_map/psum | solution.py:36
  376.7 2.9 cholesky.119
  380.9 2.4 custom-call.21
  383.8 1.4 convolution_subtract_fusion.2
  385.6 123.2 %psum.131 = f32[32,32]{1,0:T(8,128)S(1)} all-reduce(f32[32,32]{1,0:T(8,128)S(1)} %fusion.97), channel_id=1, replica_groups=mesh['ind'=32,'snp'=8] {'ind'}, use_global_device_ids=true, to_apply=%region_9.13 | all-reduce | flops 1024 | bytes 8192 | tf_op jit(solution)/shard_map/psum | solution.py:36
  509.0 2.9 cholesky.152
  511.9 2.9 cholesky.130
  516.2 2.4 custom-call.23
  519.4 9.6 fusion.9
  529.1 128.2 %all-reduce.14.cloned.1.call-done = f32[512,32]{1,0:T(8,128)} async-done(((f32[512,32]{1,0:T(8,128)}), f32[512,32]{1,0:T(8,128)}) %all-reduce.14.cloned.1.call-update) | async-done | bytes 65552 | tf_op jit(solution)/shard_map/psum | solution.py:42
  657.2 7.1 fusion.8
  665.7 2.4 custom-call.27
  668.1 70.7 %all-reduce.16.cloned.1.call-done = f32[2048,32]{0,1:T(8,128)} async-done(((f32[2048,32]{0,1:T(8,128)}), f32[2048,32]{0,1:T(8,128)}) %all-reduce.16.cloned.1.call-update) | async-done | bytes 262160 | tf_op jit(solution)/shard_map/psum | solution.py:43
  738.8 1.3 fusion.18
  740.1 99.1 %psum.134 = f32[32,32]{1,0:T(8,128)S(1)} all-reduce(f32[32,32]{1,0:T(8,128)S(1)} %fusion.18), channel_id=1, replica_groups=mesh['ind'=32,'snp'=8] {'ind'}, use_global_device_ids=true, to_apply=%region_12.16 | all-reduce | flops 1024 | bytes 8192 | tf_op jit(solution)/shard_map/psum | solution.py:36
  839.4 2.9 cholesky.141
  843.6 2.4 custom-call.25
  846.5 1.4 convolution_subtract_fusion.1
  848.2 123.4 %psum.135 = f32[32,32]{1,0:T(8,128)S(1)} all-reduce(f32[32,32]{1,0:T(8,128)S(1)} %fusion.99), channel_id=1, replica_groups=mesh['ind'=32,'snp'=8] {'ind'}, use_global_device_ids=true, to_apply=%region_13.17 | all-reduce | flops 1024 | bytes 8192 | tf_op jit(solution)/shard_map/psum | solution.py:36
  971.8 2.9 cholesky.174
  975.5 9.6 fusion.7
  985.2 128.2 %all-reduce.18.cloned.1.call-done = f32[512,32]{1,0:T(8,128)} async-done(((f32[512,32]{1,0:T(8,128)}), f32[512,32]{1,0:T(8,128)}) %all-reduce.18.cloned.1.call-update) | async-done | bytes 65552 | tf_op jit(solution)/shard_map/psum | solution.py:42
  1113.4 7.1 fusion.6
  1121.8 2.4 custom-call.31
  1124.3 70.7 %all-reduce.20.cloned.1.call-done = f32[2048,32]{0,1:T(8,128)} async-done(((f32[2048,32]{0,1:T(8,128)}), f32[2048,32]{0,1:T(8,128)}) %all-reduce.20.cloned.1.call-update) | async-done | bytes 262160 | tf_op jit(solution)/shard_map/psum | solution.py:43
  1195.0 1.3 fusion.19
  1196.3 99.3 %psum.138 = f32[32,32]{1,0:T(8,128)S(1)} all-reduce(f32[32,32]{1,0:T(8,128)S(1)} %fusion.19), channel_id=1, replica_groups=mesh['ind'=32,'snp'=8] {'ind'}, use_global_device_ids=true, to_apply=%region_16.20 | all-reduce | flops 1024 | bytes 8192 | tf_op jit(solution)/shard_map/psum | solution.py:36
  1295.8 2.9 cholesky.163
  1300.0 2.4 custom-call.29
  1302.8 1.4 convolution_subtract_fusion
  1304.6 123.3 %psum.139 = f32[32,32]{1,0:T(8,128)S(1)} all-reduce(f32[32,32]{1,0:T(8,128)S(1)} %fusion.101), channel_id=1, replica_groups=mesh['ind'=32,'snp'=8] {'ind'}, use_global_device_ids=true, to_apply=%region_17.21 | all-reduce | flops 1024 | bytes 8192 | tf_op jit(solution)/shard_map/psum | solution.py:36
  1428.7 9.6 fusion.5
  1438.6 127.9 %all-reduce.22.cloned.1.call-done = f32[512,32]{1,0:T(8,128)} async-done(((f32[512,32]{1,0:T(8,128)}), f32[512,32]{1,0:T(8,128)}) %all-reduce.22.cloned.1.call-update) | async-done | bytes 65552 | tf_op jit(solution)/shard_map/psum | solution.py:42
  1566.5 7.1 fusion.4
  1574.5 73.6 %all-reduce.24.cloned.1.call-done = f32[2048,32]{0,1:T(8,128)} async-done(((f32[2048,32]{0,1:T(8,128)}), f32[2048,32]{0,1:T(8,128)}) %all-reduce.24.cloned.1.call-update) | async-done | bytes 262160 | tf_op jit(solution)/shard_map/psum | solution.py:43
  1648.0 1.3 fusion.12
  1649.4 99.1 %psum.142 = f32[32,32]{1,0:T(8,128)S(1)} all-reduce(f32[32,32]{1,0:T(8,128)S(1)} %fusion.12), channel_id=1, replica_groups=mesh['ind'=32,'snp'=8] {'ind'}, use_global_device_ids=true, to_apply=%region_20.24 | all-reduce | flops 1024 | bytes 8192 | tf_op jit(solution)/shard_map/psum | solution.py:36
  1748.6 2.9 cholesky.185
  1752.9 2.4 custom-call.33
  1756.2 1.3 select_reduce_fusion
  1757.4 65.5 %psum.143 = f32[32]{0:T(128)} all-reduce(f32[32]{0:T(128)S(1)} %get-tuple-element.11), channel_id=1, replica_groups=mesh['ind'=32,'snp'=8] {'ind'}, use_global_device_ids=true, to_apply=%region_22.26 | all-reduce | flops 32 | bytes 256 | tf_op jit(solution)/shard_map/psum | solution.py:54
  (96 shorter events, 17.8 us)
Async XLA Ops:
  7.2 53.0 %copy-start = (f32[2048,32]{0,1:T(8,128)S(1)}, f32[2048,32]{0,1:T(8,128)}, u32[]{:S(2)}) copy-start(f32[2048,32]{0,1:T(8,128)} %param.10) | copy-start | bytes 786436
  7.2 186.9 %all-reduce.10.cloned.1.call-start = ((), (), s32[]{:S(2)}) async-start(), calls=%async_computation | async-start | bytes 524288 | tf_op jit(solution)/shard_map/psum | solution.py:42
  69.8 205.9 %all-reduce.12.cloned.1.call-start = ((), (), s32[]{:S(2)}) async-start(), calls=%async_computation.1 | async-start | bytes 524288 | tf_op jit(solution)/shard_map/psum | solution.py:43
  201.2 456.1 %all-reduce.14.cloned.1.call-start = ((), (), s32[]{:S(2)}) async-start(), calls=%async_computation.2 | async-start | bytes 524288 | tf_op jit(solution)/shard_map/psum | solution.py:42
  529.0 209.8 %all-reduce.16.cloned.1.call-start = ((), (), s32[]{:S(2)}) async-start(), calls=%async_computation.3 | async-start | bytes 524288 | tf_op jit(solution)/shard_map/psum | solution.py:43
  664.3 449.0 %all-reduce.18.cloned.1.call-start = ((), (), s32[]{:S(2)}) async-start(), calls=%async_computation.4 | async-start | bytes 524288 | tf_op jit(solution)/shard_map/psum | solution.py:42
  985.1 209.8 %all-reduce.20.cloned.1.call-start = ((), (), s32[]{:S(2)}) async-start(), calls=%async_computation.5 | async-start | bytes 524288 | tf_op jit(solution)/shard_map/psum | solution.py:43
  1120.5 446.1 %all-reduce.22.cloned.1.call-start = ((), (), s32[]{:S(2)}) async-start(), calls=%async_computation.6 | async-start | bytes 524288 | tf_op jit(solution)/shard_map/psum | solution.py:42
  1438.3 317.9 %copy-start.1 = (s32[32]{0:T(128)S(1)}, s32[32]{0:T(128)}, u32[]{:S(2)}) copy-start(s32[32]{0:T(128)} %param.12) | copy-start | bytes 388
  1438.3 209.7 %all-reduce.24.cloned.1.call-start = ((), (), s32[]{:S(2)}) async-start(), calls=%async_computation.7 | async-start | bytes 524288 | tf_op jit(solution)/shard_map/psum | solution.py:43
Sparse Core Ops, SparseCore 0:
  69.9 124.1 all-reduce.9
  201.3 74.3 all-reduce.11
  529.1 128.0 all-reduce.13
  664.5 74.3 all-reduce.15
  985.3 128.0 all-reduce.17
  1120.6 74.3 all-reduce.19
  1438.4 128.0 all-reduce.21
  1573.7 74.2 all-reduce.23
where the time goes:
time: 1860 us; the launch traced here: 1830 us
  blocking collectives  883 us (47%)
  waiting for transfers between devices  797 us (43%)
  matrix products  83.7 us (4%)
  other arithmetic  49.8 us (3%)
    psum x7, blocking collectives, grams(): return lax.psum((parts[0],), 'ind')  767 us
    psum x4, waiting for transfers between devices, shards(): term = matmul(zmat, lax.psum(matmul(zmat.T, direction), 'ind'))  509 us
    psum x4, waiting for transfers between devices, shards(): image = lax.psum(term, 'snp') / width + lam * direction  288 us
    dot_general x26, matrix products, matmul(): jnp.dot(left, right, precision=lax.Precision.HIGHEST, preferred_element_t...  81.2 us
    psum x1, blocking collectives, shards(): held_values = lax.psum(jnp.sum(selected * solution, axis=0), 'ind')  65.5 us
    psum x1, blocking collectives, shards(): lax.psum(jnp.stack([jnp.sum(values, axis=0), jnp.sum(values * values, axi...  50.1 us
  transfers between devices with their start and end apart: 8, of which 8 were waited for; matrix products, arithmetic and copies ran while one was open for 0% of the time, Pallas kernels for 0%

commit v1 on v0

v1 whole, which is shorter than its diff:
```python
import functools

import jax
import jax.numpy as jnp
from jax import lax
from jax.experimental import pallas as pl
from jax.experimental.pallas import tpu as pltpu
from jax.sharding import PartitionSpec as P

ITERS = 4
RHS = 32
XSIZE, YSIZE, CORES = 4, 4, 2
F32, BF16 = jnp.float32, jnp.bfloat16
NT = (((1,), (1,)), ((), ()))
PARAMS = pltpu.CompilerParams(vmem_limit_bytes=40 * 1024 * 1024)


def split(x):
    high = x.astype(BF16)
    rest = x - high.astype(F32)
    mid = rest.astype(BF16)
    low = (rest - mid.astype(F32)).astype(BF16)
    return high, mid, low


def stacked(x):
    return jnp.concatenate(split(x), axis=0)


def fold(x):
    n = x.shape[0] // 3
    return x[:n] + (x[n:2 * n] + x[2 * n:])


def gram(left, right):
    full = fold(lax.dot_general(left, right, NT, preferred_element_type=F32))
    n = full.shape[1] // 3
    return full[:, :n] + (full[:, n:2 * n] + full[:, 2 * n:])


def small_dot(left, right):
    lh, lm, ll = split(left)
    rh, rm, rl = split(right)
    lhs = jnp.concatenate([lh, lh, lm, lm, lh, ll], axis=1)
    rhs = jnp.concatenate([rh, rm, rh, rm, rl, rh], axis=0)
    return jnp.dot(lhs, rhs, preferred_element_type=F32)


def symmetric(x):
    return 0.5 * (x + x.T)


def right_divide(gram_, top):
    n = gram_.shape[0]
    m = jnp.concatenate([gram_, top], axis=0)
    lane = lax.broadcasted_iota(jnp.int32, m.shape, 1)
    for k in range(n):
        row = m[k:k + 1, :]
        col = m[:, k:k + 1] * (1.0 / m[k:k + 1, k:k + 1])
        m = jnp.where(lane == k, col, m - col * row)
    return m[n:]


def prep_kernel(geno_ref, rhs_ref, codes_ref, pay_ref, all_ref):
    step = pl.program_id(0)
    rows, cols = geno_ref.shape
    centred = (geno_ref[...] - 1).astype(F32)
    codes = centred.astype(BF16)
    codes_ref[...] = codes
    all_ref[pl.ds(pl.multiple_of(step * rows, rows), rows), :] = codes
    squares = jnp.sum(centred * centred, axis=0, keepdims=True)

    @pl.when(step == 0)
    def _():
        pay_ref[...] = jnp.zeros_like(pay_ref)
        pay_ref[33:34, :cols] = squares

    @pl.when(step > 0)
    def _():
        pay_ref[33:34, :cols] += squares

    @pl.when(step == pl.num_programs(0) - 1)
    def _():
        rhs = rhs_ref[...]
        pieces = stacked(rhs)
        lhs = jnp.concatenate([pieces, jnp.ones((32, pieces.shape[1]), BF16)], axis=0)
        acc = jnp.dot(lhs, all_ref[...], preferred_element_type=F32)
        pay_ref[0:RHS, :cols] = fold(acc[:96])
        pay_ref[32:33, :cols] = acc[96:97]
        pay_ref[0:RHS, cols:cols + 32] = gram(pieces, pieces)
        pay_ref[0:RHS, cols + 32:cols + 33] = jnp.sum(rhs, axis=1, keepdims=True)


def prep(genotypes, rhs):
    rows, cols = genotypes.shape
    block = 256
    return pl.pallas_call(
        prep_kernel,
        grid=(rows // block,),
        in_specs=[pl.BlockSpec((block, cols), lambda i: (i, 0)), pl.BlockSpec((RHS, rows), lambda i: (0, 0))],
        out_specs=[pl.BlockSpec((block, cols), lambda i: (i, 0)), pl.BlockSpec((40, cols + 128), lambda i: (0, 0))],
        out_shape=[jax.ShapeDtypeStruct((rows, cols), BF16), jax.ShapeDtypeStruct((40, cols + 128), F32)],
        scratch_shapes=[pltpu.VMEM((rows, cols), BF16)],
        compiler_params=PARAMS,
        name="prep",
    )(genotypes, rhs)


def panel_kernel(total, first, last, parts, *refs):
    if first:
        red_ref, codes_ref, resid_ref, u_ref, stat_ref, norm_ref, pp_ref, dir_ref, out_ref = refs
    else:
        (red_ref, codes_ref, resid_ref, olddir_ref, oldu_ref, stat_in_ref, inv_ref, oldpp_ref,
         u_ref, norm_ref, pp_ref, dir_ref, beta_ref, out_ref) = refs
    cols = codes_ref.shape[1]
    if first:
        mean = red_ref[32:33, :cols] * (1.0 / total)
        scale = 1.0 / jnp.sqrt(red_ref[33:34, :cols] * (1.0 / total) - mean * mean + 1e-05)
        stat_ref[0:1, :] = mean
        stat_ref[1:2, :] = scale
    else:
        mean, scale = stat_in_ref[0:1, :], stat_in_ref[1:2, :]
    side = red_ref[0:RHS, cols:cols + 128]
    norm = symmetric(side[:, :32])
    u = (red_ref[0:RHS, :cols] - side[:, 32:33] * mean) * scale
    norm_ref[...] = norm
    if first:
        pp = norm
        dir_ref[...] = resid_ref[...]
    else:
        beta = small_dot(norm, inv_ref[...])
        u = u + small_dot(beta, oldu_ref[...])
        cross = small_dot(beta, side[:, 64:96])
        pp = norm + (cross + cross.T) + symmetric(small_dot(small_dot(beta, oldpp_ref[...]), beta.T))
        dir_ref[...] = resid_ref[...] + small_dot(beta, olddir_ref[...])
        beta_ref[...] = beta
    pp_ref[...] = pp
    u_ref[...] = u
    pieces = stacked(u)
    uu = gram(pieces, pieces)
    if last:
        for j in range(parts):
            out_ref[j, :, :] = jnp.zeros(out_ref.shape[1:], F32)
            out_ref[j, :, 0:32] = uu
        return
    weight = u * scale
    image = fold(lax.dot_general(stacked(weight), codes_ref[...], NT, preferred_element_type=F32))
    image = image - jnp.sum(weight * mean, axis=1, keepdims=True)
    width = image.shape[1] // parts
    for j in range(parts):
        out_ref[j, :, 0:width] = image[:, j * width:(j + 1) * width]
        out_ref[j, :, width:] = jnp.zeros((RHS, 128), F32)
        out_ref[j, :, width:width + 32] = uu


def panel(total, first, last, parts, *args):
    rows, cols = args[1].shape
    small = jax.ShapeDtypeStruct((RHS, RHS), F32)
    outs = [jax.ShapeDtypeStruct((RHS, cols), F32)]
    if first:
        outs.append(jax.ShapeDtypeStruct((8, cols), F32))
    outs += [small, small, jax.ShapeDtypeStruct((RHS, rows), F32)]
    if not first:
        outs.append(small)
    outs.append(jax.ShapeDtypeStruct((parts, RHS, (0 if last else rows // parts) + 128), F32))
    return pl.pallas_call(
        functools.partial(panel_kernel, total, first, last, parts),
        out_shape=outs,
        compiler_params=PARAMS,
        name="panel",
    )(*args)


def step_kernel(markers, first, held_too, *refs):
    it = iter(refs)
    ridge_ref, image_ref, uu_ref, pp_ref, norm_ref, resid_ref, dir_ref = [next(it) for _ in range(7)]
    sol_in = None if first else next(it)
    codes_ref = next(it)
    held_ref = next(it) if held_too else None
    sol_ref, newres_ref, inv_ref, pay_ref = [next(it) for _ in range(4)]
    cols = codes_ref.shape[1]
    lam = ridge_ref[0]
    norm = norm_ref[...]
    eye = (lax.broadcasted_iota(jnp.int32, norm.shape, 0) == lax.broadcasted_iota(jnp.int32, norm.shape, 1)).astype(F32)
    alpha = right_divide(symmetric(uu_ref[...] * (1.0 / markers) + lam * pp_ref[...]), norm)
    inv_ref[...] = right_divide(norm, eye)
    direction = dir_ref[...]
    image = jnp.concatenate([image_ref[j] for j in range(image_ref.shape[0])], axis=1)
    image = image * (1.0 / markers) + lam * direction
    resid = resid_ref[...] - small_dot(alpha, image)
    sol = small_dot(alpha, direction)
    if not first:
        sol = sol_in[...] + sol
    sol_ref[...] = sol
    newres_ref[...] = resid
    pieces = stacked(resid)
    dpieces = stacked(direction)
    pay_ref[:, :cols] = fold(jnp.dot(pieces, codes_ref[...], preferred_element_type=F32))
    pay_ref[:, cols:] = jnp.zeros((RHS, pay_ref.shape[1] - cols), F32)
    pay_ref[:, cols:cols + 32] = gram(pieces, pieces)
    pay_ref[:, cols + 32:cols + 33] = jnp.sum(resid, axis=1, keepdims=True)
    pay_ref[:, cols + 64:cols + 96] = gram(dpieces, pieces)
    if held_too:
        place = lax.broadcasted_iota(jnp.int32, resid.shape, 1)
        chosen = (place == held_ref[...]).astype(BF16)
        pay_ref[:, cols + 128:cols + 160] = fold(lax.dot_general(pieces, chosen, NT, preferred_element_type=F32))
        pay_ref[:, cols + 160:cols + 192] = fold(lax.dot_general(dpieces, chosen, NT, preferred_element_type=F32))
        pay_ref[:, cols + 192:cols + 224] = fold(lax.dot_general(stacked(sol), chosen, NT, preferred_element_type=F32))


def step(markers, first, held_too, *args):
    codes = args[-2] if held_too else args[-1]
    rows, cols = codes.shape
    vmem = pl.BlockSpec(memory_space=pltpu.VMEM)
    long = jax.ShapeDtypeStruct((RHS, rows), F32)
    return pl.pallas_call(
        functools.partial(step_kernel, markers, first, held_too),
        in_specs=[pl.BlockSpec(memory_space=pltpu.SMEM)] + [vmem] * (len(args) - 1),
        out_shape=[long, long, jax.ShapeDtypeStruct((RHS, RHS), F32),
                   jax.ShapeDtypeStruct((RHS, cols + (256 if held_too else 128)), F32)],
        compiler_params=PARAMS,
        name="step",
    )(*args)


def last_kernel(markers, cols, ridge_ref, uu_ref, pp_ref, norm_ref, dir_ref, sol_ref, red_ref, beta_ref, out_ref, held_ref):
    alpha = right_divide(symmetric(uu_ref[...] * (1.0 / markers) + ridge_ref[0] * pp_ref[...]), norm_ref[...])
    out_ref[...] = sol_ref[...] + small_dot(alpha, dir_ref[...])
    side = red_ref[:, cols + 128:cols + 256]
    direction = side[:, 0:32] + small_dot(beta_ref[...], side[:, 32:64])
    rows = side[:, 64:96] + small_dot(alpha, direction)
    eye = lax.broadcasted_iota(jnp.int32, rows.shape, 0) == lax.broadcasted_iota(jnp.int32, rows.shape, 1)
    held_ref[...] = jnp.sum(jnp.where(eye, rows, 0.0), axis=0, keepdims=True)


def last_step(markers, cols, *args):
    vmem = pl.BlockSpec(memory_space=pltpu.VMEM)
    return pl.pallas_call(
        functools.partial(last_kernel, markers, cols),
        in_specs=[pl.BlockSpec(memory_space=pltpu.SMEM)] + [vmem] * (len(args) - 1),
        out_shape=[jax.ShapeDtypeStruct(args[4].shape, F32), jax.ShapeDtypeStruct((1, RHS), F32)],
        compiler_params=PARAMS,
        name="last",
    )(*args)


def on_ind(move):
    pairs = []
    for y in range(YSIZE):
        for x in range(XSIZE):
            for c in range(CORES):
                ty, tx, tc = move(y, x, c)
                pairs.append(((y * XSIZE + x) * CORES + c, (ty * XSIZE + tx) * CORES + tc))
    return pairs


def sum_ind(value):
    for along in ("x", "y"):
        moved = []
        for d in (1, 2, 3):
            if along == "x":
                pairs = on_ind(lambda y, x, c, d=d: (y, (x + d) % XSIZE, c))
            else:
                pairs = on_ind(lambda y, x, c, d=d: ((y + d) % YSIZE, x, c))
            moved.append(lax.ppermute(value, "ind", pairs))
        value = (value + moved[1]) + (moved[0] + moved[2])
    return value + lax.ppermute(value, "ind", on_ind(lambda y, x, c: (y, x, 1 - c)))


def exchange(value):
    return lax.all_to_all(value, "snp", 0, 0)


def shards(genotypes, targets, ridge, held_out):
    rows, cols = genotypes.shape
    parts = lax.axis_size("snp")
    total = rows * lax.axis_size("ind")
    markers = cols * parts
    width = rows // parts
    place = (held_out - lax.axis_index("ind") * rows)[:, None]

    resid = targets.T
    codes, pay = prep(genotypes, resid)
    sol = None
    for k in range(ITERS):
        first, last = k == 0, k == ITERS - 1
        red = sum_ind(pay)
        if first:
            u, stat, norm, pp, direction, out = panel(total, True, False, parts, red, codes, resid)
        else:
            u, norm, pp, direction, beta, out = panel(
                total, False, last, parts, red, codes, resid, direction, u, stat, inv, pp)
        got = jnp.sum(exchange(out), axis=0)
        if last:
            break
        uu = got[:, width:width + RHS]
        image = exchange(jnp.broadcast_to(got[None, :, :width], (parts, RHS, width)))
        args = [ridge, image, uu, pp, norm, resid, direction]
        if not first:
            args.append(sol)
        args.append(codes)
        held_too = k == ITERS - 2
        if held_too:
            args.append(place)
        sol, resid, inv, pay = step(markers, first, held_too, *args)
    sol, held = last_step(markers, cols, ridge, got[:, :RHS], pp, norm, direction, sol, red, beta)
    return sol.T, held[0]


def solution(mesh):
    return jax.shard_map(
        shards,
        mesh=mesh,
        in_specs=(P("ind", "snp"), P("ind", None), P(), P()),
        out_specs=(P("ind", None), P()),
        check_vma=False,
    )
```

time: 1860 us -> 235 us (0.13); the launches traced: 1830 us -> 230 us
  blocking collectives: 883 us -> 72 us
  waiting for transfers between devices: 797 us -> 80.1 us
  matrix products: 83.7 us -> 0 us
  other arithmetic: 49.8 us -> 2.96 us
  starting transfers between devices: 0.58 us -> 42.9 us
  Pallas kernels: 0 us -> 24.6 us
    psum x9 -> x0, blocking collectives: 883 us -> none  [the longest x7 767 us: grams(): return lax.psum((parts[0],), 'ind')]
    psum x8 -> x0, waiting for transfers between devices: 797 us -> none  [the longest x4 509 us: shards(): term = matmul(zmat, lax.psum(matmul(zmat.T, direction), 'ind'))]
    dot_general x26 -> x0, matrix products: 81.2 us -> none  [matmul(): jnp.dot(left, right, precision=lax.Precision.HIGHEST, preferred_element_t...]
    all_to_all x0 -> x4, blocking collectives: none -> 72 us  [exchange(): return lax.all_to_all(value, 'snp', 0, 0)]
    another operation x36 -> x0, other arithmetic: 46.8 us -> none  [the longest x21 25.3 us: chol_solve(): lower = jnp.linalg.cholesky(gram)]
    ppermute x0 -> x28, waiting for transfers between devices: none -> 46 us  [the longest x24 40.9 us: sum_ind(): moved.append(lax.ppermute(value, 'ind', pairs))]
    all_to_all x0 -> x3, waiting for transfers between devices: none -> 34.2 us  [exchange(): return lax.all_to_all(value, 'snp', 0, 0)]
    ppermute x0 -> x28, starting transfers between devices: none -> 32.7 us  [the longest x24 32.3 us: sum_ind(): moved.append(lax.ppermute(value, 'ind', pairs))]
  transfers between devices with their start and end apart: 8 -> 31, of which waited for: 8 -> 30; matrix products, arithmetic and copies ran while one was open for 0% -> 0% of each run, Pallas kernels for 0% -> 0%
where the time goes in v1:
time: 235 us; the launch traced here: 230 us
  waiting for transfers between devices  80.1 us (34%)
  blocking collectives  72 us (31%)
  starting transfers between devices  42.9 us (18%)
  Pallas kernels  24.6 us (10%)
  local copies, waits for them, and re-layouts  6.06 us (3%)
  other arithmetic  2.96 us (1%)
    all_to_all x4, blocking collectives, exchange(): return lax.all_to_all(value, 'snp', 0, 0)  72 us
    ppermute x24, waiting for transfers between devices, sum_ind(): moved.append(lax.ppermute(value, 'ind', pairs))  40.9 us
    all_to_all x3, waiting for transfers between devices, exchange(): return lax.all_to_all(value, 'snp', 0, 0)  34.2 us
    ppermute x24, starting transfers between devices, sum_ind(): moved.append(lax.ppermute(value, 'ind', pairs))  32.3 us
    pallas_call x3, Pallas kernels, step(): pl.pallas_call(functools.partial(step_kernel, markers, first, held_too),...  14.5 us
    all_to_all x3, starting transfers between devices, exchange(): return lax.all_to_all(value, 'snp', 0, 0)  10.2 us
    ppermute x4, waiting for transfers between devices, sum_ind(): lax.ppermute(value, 'ind', on_ind(lambda y, x, c: (y, x, 1 - c)))  5.11 us
    pallas_call x4, Pallas kernels, panel(): pl.pallas_call(functools.partial(panel_kernel, total, first, last, parts)...  4.81 us
  transfers between devices with their start and end apart: 31, of which 30 were waited for; matrix products, arithmetic and copies ran while one was open for 0% of the time, Pallas kernels for 0%

profile of v1, /device:TPU:22, one launch (start us, length us, event | category | flops | bytes accessed | tf_op | source)
XLA Modules:
  0.0 230.3 jit_solution(3085372006180650388)
XLA Ops:
  0.6 2.2 copy-done
  3.8 1.5 prep.1
  6.2 2.4 %collective-permute-start.1 = (f32[40,640]{1,0:T(8,128)S(1)}, f32[40,640]{1,0:T(8,128)S(1)}, u32[]{:S(2)}, u32[]{:S(2)}) collective-permute-start(f32[40,640]{1,0:T(8,128)S(1)} %get-tuple-element.39), channel_id=1, source_target_pairs={{0,16},{8,24},{16,32},{24,40},{32,48},{40,56},{48,0},{56,8},{64,80... | collective-permute-start | bytes 307208 | tf_op jit(solution)/shard_map/ppermute | solution.py:265
  8.8 2.4 %collective-permute-done.2 = f32[40,640]{1,0:T(8,128)S(1)} collective-permute-done((f32[40,640]{1,0:T(8,128)S(1)}, f32[40,640]{1,0:T(8,128)S(1)}, u32[]{:S(2)}, u32[]{:S(2)}) %collective-permute-start.2) | collective-permute-done | bytes 102432 | tf_op jit(solution)/shard_map/ppermute | solution.py:265
  11.2 1.5 collective-permute-done.1
  12.7 2.1 collective-permute-done
  15.3 1.6 collective-permute-start.4
  16.9 1.3 collective-permute-start.3
  18.2 1.8 collective-permute-done.5
  20.7 2.3 %collective-permute-done.3 = f32[40,640]{1,0:T(8,128)S(1)} collective-permute-done((f32[40,640]{1,0:T(8,128)S(1)}, f32[40,640]{1,0:T(8,128)S(1)}, u32[]{:S(2)}, u32[]{:S(2)}) %collective-permute-start.3) | collective-permute-done | bytes 102432 | tf_op jit(solution)/shard_map/ppermute | solution.py:265
  23.2 1.3 collective-permute-done.6
  25.4 23.3 %all_to_all.35 = f32[8,32,384]{2,1,0:T(8,128)S(1)} all-to-all(f32[8,32,384]{2,1,0:T(8,128)S(1)} %get-tuple-element.41), channel_id=1, replica_groups=mesh['ind'=32,'snp'=8] {'snp'}, dimensions={0} | all-to-all | bytes 786432 | tf_op jit(solution)/shard_map/all_to_all | solution.py:271
  49.4 3.4 %all-to-all-start.1 = ((f32[8,32,256]{2,1,0:T(8,128)}), f32[8,32,256]{2,1,0:T(8,128)S(1)}, u32[]{:S(2)}, u32[]{:S(2)}) async-start(f32[8,32,256]{2,1,0:T(8,128)} %broadcast_in_dim.8), calls=%async_computation.1 | async-start | bytes 524288 | tf_op jit(solution)/shard_map/all_to_all | solution.py:271
  53.5 10.4 %all-to-all-done.1.refs_1_ = f32[8,32,256]{2,1,0:T(8,128)S(1)} async-done(((f32[8,32,256]{2,1,0:T(8,128)}), f32[8,32,256]{2,1,0:T(8,128)S(1)}, u32[]{:S(2)}, u32[]{:S(2)}) %all-to-all-start.1) | async-done | bytes 262176 | tf_op jit(solution)/shard_map/all_to_all | solution.py:271
  63.9 4.7 %step.3 = (f32[32,2048]{1,0:T(8,128)S(1)}, f32[32,2048]{1,0:T(8,128)S(1)}, f32[32,32]{1,0:T(8,128)S(1)}, f32[32,640]{1,0:T(8,128)S(1)}) custom-call(f32[1]{0:T(128)S(6)} %copy.7.refs_0_.ridge_ref, f32[8,32,256]{2,1,0:T(8,128)S(1)} %all-to-all-done.1.refs_1_, f32[32,32]{1,0:T(8,128)S(1)} %slice.29.refs_2_, f32[32,32]{1,0:T(8,128)S(1)} %get-tuple-element.42.refs_3_.refs_7_, ...), custom_call_target="tpu_custom_call" | custom-call | tf_op jit(solution)/shard_map/step/pallas_call | solution.py:216
  68.6 3.2 %collective-permute-start.8 = (f32[32,640]{1,0:T(8,128)S(1)}, f32[32,640]{1,0:T(8,128)S(1)}, u32[]{:S(2)}, u32[]{:S(2)}) collective-permute-start(f32[32,640]{1,0:T(8,128)S(1)} %get-tuple-element.45), channel_id=1, source_target_pairs={{0,16},{8,24},{16,32},{24,40},{32,48},{40,56},{48,0},{56,8},{64,80... | collective-permute-start | bytes 245768 | tf_op jit(solution)/shard_map/ppermute | solution.py:265
  71.9 2.8 %collective-permute-done.9 = f32[32,640]{1,0:T(8,128)S(1)} collective-permute-done((f32[32,640]{1,0:T(8,128)S(1)}, f32[32,640]{1,0:T(8,128)S(1)}, u32[]{:S(2)}, u32[]{:S(2)}) %collective-permute-start.9) | collective-permute-done | bytes 81952 | tf_op jit(solution)/shard_map/ppermute | solution.py:265
  74.7 3.1 %collective-permute-done.7 = f32[32,640]{1,0:T(8,128)S(1)} collective-permute-done((f32[32,640]{1,0:T(8,128)S(1)}, f32[32,640]{1,0:T(8,128)S(1)}, u32[]{:S(2)}, u32[]{:S(2)}) %collective-permute-start.7) | collective-permute-done | bytes 81952 | tf_op jit(solution)/shard_map/ppermute | solution.py:265
  78.4 2.1 collective-permute-start.11
  80.5 2.0 collective-permute-start.10
  83.0 3.4 %collective-permute-done.10 = f32[32,640]{1,0:T(8,128)S(1)} collective-permute-done((f32[32,640]{1,0:T(8,128)S(1)}, f32[32,640]{1,0:T(8,128)S(1)}, u32[]{:S(2)}, u32[]{:S(2)}) %collective-permute-start.10) | collective-permute-done | bytes 81952 | tf_op jit(solution)/shard_map/ppermute | solution.py:265
  87.9 1.4 panel.5
  89.9 18.3 %all_to_all.36 = f32[8,32,384]{2,1,0:T(8,128)} all-to-all(f32[8,32,384]{2,1,0:T(8,128)S(1)} %get-tuple-element.50), channel_id=1, replica_groups=mesh['ind'=32,'snp'=8] {'snp'}, dimensions={0} | all-to-all | bytes 786432 | tf_op jit(solution)/shard_map/all_to_all | solution.py:271
  110.0 3.4 %all-to-all-start.3 = ((f32[8,32,256]{2,1,0:T(8,128)}), f32[8,32,256]{2,1,0:T(8,128)S(1)}, u32[]{:S(2)}, u32[]{:S(2)}) async-start(f32[8,32,256]{2,1,0:T(8,128)} %broadcast_in_dim.9), calls=%async_computation.3 | async-start | bytes 524288 | tf_op jit(solution)/shard_map/all_to_all | solution.py:271
  113.4 12.3 %all-to-all-done.3.refs_1_ = f32[8,32,256]{2,1,0:T(8,128)S(1)} async-done(((f32[8,32,256]{2,1,0:T(8,128)}), f32[8,32,256]{2,1,0:T(8,128)S(1)}, u32[]{:S(2)}, u32[]{:S(2)}) %all-to-all-start.3) | async-done | bytes 262176 | tf_op jit(solution)/shard_map/all_to_all | solution.py:271
  125.7 4.7 %step.4 = (f32[32,2048]{1,0:T(8,128)S(1)}, f32[32,2048]{1,0:T(8,128)S(1)}, f32[32,32]{1,0:T(8,128)S(1)}, f32[32,640]{1,0:T(8,128)S(1)}) custom-call(f32[1]{0:T(128)S(6)} %copy.7.refs_0_.ridge_ref, f32[8,32,256]{2,1,0:T(8,128)S(1)} %all-to-all-done.3.refs_1_, f32[32,32]{1,0:T(8,128)S(1)} %slice.31.refs_2_, f32[32,32]{1,0:T(8,128)S(1)} %get-tuple-element.51.refs_3_.refs_7_, ...), custom_call_target="tpu_custom_call" | custom-call | tf_op jit(solution)/shard_map/step/pallas_call | solution.py:216
  130.5 3.2 %collective-permute-start.15 = (f32[32,640]{1,0:T(8,128)S(1)}, f32[32,640]{1,0:T(8,128)S(1)}, u32[]{:S(2)}, u32[]{:S(2)}) collective-permute-start(f32[32,640]{1,0:T(8,128)S(1)} %get-tuple-element.55), channel_id=1, source_target_pairs={{0,16},{8,24},{16,32},{24,40},{32,48},{40,56},{48,0},{56,8},{64,80... | collective-permute-start | bytes 245768 | tf_op jit(solution)/shard_map/ppermute | solution.py:265
  133.7 2.4 %collective-permute-done.16 = f32[32,640]{1,0:T(8,128)S(1)} collective-permute-done((f32[32,640]{1,0:T(8,128)S(1)}, f32[32,640]{1,0:T(8,128)S(1)}, u32[]{:S(2)}, u32[]{:S(2)}) %collective-permute-start.16) | collective-permute-done | bytes 81952 | tf_op jit(solution)/shard_map/ppermute | solution.py:265
  137.0 2.6 %collective-permute-done.14 = f32[32,640]{1,0:T(8,128)S(1)} collective-permute-done((f32[32,640]{1,0:T(8,128)S(1)}, f32[32,640]{1,0:T(8,128)S(1)}, u32[]{:S(2)}, u32[]{:S(2)}) %collective-permute-start.14) | collective-permute-done | bytes 81952 | tf_op jit(solution)/shard_map/ppermute | solution.py:265
  140.8 2.2 collective-permute-start.18
  143.0 2.0 collective-permute-start.17
  146.2 2.8 %collective-permute-done.17 = f32[32,640]{1,0:T(8,128)S(1)} collective-permute-done((f32[32,640]{1,0:T(8,128)S(1)}, f32[32,640]{1,0:T(8,128)S(1)}, u32[]{:S(2)}, u32[]{:S(2)}) %collective-permute-start.17) | collective-permute-done | bytes 81952 | tf_op jit(solution)/shard_map/ppermute | solution.py:265
  150.3 1.4 panel.6
  151.8 18.3 %all_to_all.37 = f32[8,32,384]{2,1,0:T(8,128)} all-to-all(f32[8,32,384]{2,1,0:T(8,128)S(1)} %get-tuple-element.59), channel_id=1, replica_groups=mesh['ind'=32,'snp'=8] {'snp'}, dimensions={0} | all-to-all | bytes 786432 | tf_op jit(solution)/shard_map/all_to_all | solution.py:271
  171.9 3.4 %all-to-all-start.5 = ((f32[8,32,256]{2,1,0:T(8,128)}), f32[8,32,256]{2,1,0:T(8,128)S(1)}, u32[]{:S(2)}, u32[]{:S(2)}) async-start(f32[8,32,256]{2,1,0:T(8,128)} %broadcast_in_dim.10), calls=%async_computation.5 | async-start | bytes 524288 | tf_op jit(solution)/shard_map/all_to_all | solution.py:271
  176.0 11.5 %all-to-all-done.5.refs_1_ = f32[8,32,256]{2,1,0:T(8,128)S(1)} async-done(((f32[8,32,256]{2,1,0:T(8,128)}), f32[8,32,256]{2,1,0:T(8,128)S(1)}, u32[]{:S(2)}, u32[]{:S(2)}) %all-to-all-start.5) | async-done | bytes 262176 | tf_op jit(solution)/shard_map/all_to_all | solution.py:271
  187.6 5.1 %step.5 = (f32[32,2048]{1,0:T(8,128)S(1)}, f32[32,2048]{1,0:T(8,128)S(1)}, f32[32,32]{1,0:T(8,128)S(1)}, f32[32,768]{1,0:T(8,128)S(1)}) custom-call(f32[1]{0:T(128)S(6)} %copy.7.refs_0_.ridge_ref, f32[8,32,256]{2,1,0:T(8,128)S(1)} %all-to-all-done.5.refs_1_, f32[32,32]{1,0:T(8,128)S(1)} %slice.33.refs_2_, f32[32,32]{1,0:T(8,128)S(1)} %get-tuple-element.60.refs_3_.refs_7_, ...), custom_call_target="tpu_custom_call" | custom-call | tf_op jit(solution)/shard_map/step/pallas_call | solution.py:216
  193.0 3.2 %collective-permute-start.22 = (f32[32,768]{1,0:T(8,128)S(1)}, f32[32,768]{1,0:T(8,128)S(1)}, u32[]{:S(2)}, u32[]{:S(2)}) collective-permute-start(f32[32,768]{1,0:T(8,128)S(1)} %get-tuple-element.64), channel_id=1, source_target_pairs={{0,16},{8,24},{16,32},{24,40},{32,48},{40,56},{48,0},{56,8},{64,80... | collective-permute-start | bytes 294920 | tf_op jit(solution)/shard_map/ppermute | solution.py:265
  196.2 2.6 %collective-permute-done.23 = f32[32,768]{1,0:T(8,128)S(1)} collective-permute-done((f32[32,768]{1,0:T(8,128)S(1)}, f32[32,768]{1,0:T(8,128)S(1)}, u32[]{:S(2)}, u32[]{:S(2)}) %collective-permute-start.23) | collective-permute-done | bytes 98336 | tf_op jit(solution)/shard_map/ppermute | solution.py:265
  198.8 1.4 collective-permute-done.22
  200.2 2.1 collective-permute-done.21
  203.5 2.2 collective-permute-start.25
  205.7 2.0 collective-permute-start.24
  207.7 1.4 collective-permute-done.26
  209.2 2.6 %collective-permute-done.24 = f32[32,768]{1,0:T(8,128)S(1)} collective-permute-done((f32[32,768]{1,0:T(8,128)S(1)}, f32[32,768]{1,0:T(8,128)S(1)}, u32[]{:S(2)}, u32[]{:S(2)}) %collective-permute-start.24) | collective-permute-done | bytes 98336 | tf_op jit(solution)/shard_map/ppermute | solution.py:265
  211.9 1.3 collective-permute-done.27
  214.4 12.0 %all_to_all.38 = f32[8,32,128]{2,1,0:T(8,128)S(1)} all-to-all(f32[8,32,128]{2,1,0:T(8,128)S(1)} %get-tuple-element.68), channel_id=1, replica_groups=mesh['ind'=32,'snp'=8] {'snp'}, dimensions={0} | all-to-all | bytes 262144 | tf_op jit(solution)/shard_map/all_to_all | solution.py:271
  226.4 3.9 %last.1 = (f32[32,2048]{1,0:T(8,128)}, f32[1,32]{1,0:T(1,128)}) custom-call(f32[1]{0:T(128)S(6)} %copy.7.refs_0_.ridge_ref, f32[32,32]{1,0:T(8,128)S(1)} %bitcast.9, f32[32,32]{1,0:T(8,128)S(1)} %get-tuple-element.69.pp_ref, f32[32,32]{1,0:T(8,128)S(1)} %get-tuple-element.70.norm_ref, f32[32,2048]{1,0:T(8,128)S(1)} %get-tuple-element.71.dir_ref, ...), custom_call_target="tpu_custom_call" | custom-call | tf_op jit(solution)/shard_map/last/pallas_call | solution.py:238
  (72 shorter events, 20.3 us)
Async XLA Ops:
  0.6 2.2 copy-start
  2.8 0.9 copy-start.1
  3.8 60.1 %copy-start.2 = (f32[2048,32]{0,1:T(8,128)S(1)}, f32[2048,32]{0,1:T(8,128)}, u32[]{:S(2)}) copy-start(f32[2048,32]{0,1:T(8,128)} %param.5) | copy-start | bytes 786436
  5.3 5.9 %collective-permute-start.2 = (f32[40,640]{1,0:T(8,128)S(1)}, f32[40,640]{1,0:T(8,128)S(1)}, u32[]{:S(2)}, u32[]{:S(2)}) collective-permute-start(f32[40,640]{1,0:T(8,128)S(1)} %get-tuple-element.39), channel_id=1, source_target_pairs={{0,48},{8,56},{16,0},{24,8},{32,16},{40,24},{48,32},{56,40},{64,11... | collective-permute-start | bytes 307208 | tf_op jit(solution)/shard_map/ppermute | solution.py:265
  6.2 6.5 %collective-permute-start.1 = (f32[40,640]{1,0:T(8,128)S(1)}, f32[40,640]{1,0:T(8,128)S(1)}, u32[]{:S(2)}, u32[]{:S(2)}) collective-permute-start(f32[40,640]{1,0:T(8,128)S(1)} %get-tuple-element.39), channel_id=1, source_target_pairs={{0,16},{8,24},{16,32},{24,40},{32,48},{40,56},{48,0},{56,8},{64,80... | collective-permute-start | bytes 307208 | tf_op jit(solution)/shard_map/ppermute | solution.py:265
  8.6 6.2 %collective-permute-start = (f32[40,640]{1,0:T(8,128)S(1)}, f32[40,640]{1,0:T(8,128)S(1)}, u32[]{:S(2)}, u32[]{:S(2)}) collective-permute-start(f32[40,640]{1,0:T(8,128)S(1)} %get-tuple-element.39), channel_id=1, source_target_pairs={{0,32},{8,40},{16,48},{24,56},{32,0},{40,8},{48,16},{56,24},{64,96... | collective-permute-start | bytes 307208 | tf_op jit(solution)/shard_map/ppermute | solution.py:265
  14.8 5.2 %collective-permute-start.5 = (f32[40,640]{1,0:T(8,128)S(1)}, f32[40,640]{1,0:T(8,128)S(1)}, u32[]{:S(2)}, u32[]{:S(2)}) collective-permute-start(f32[40,640]{1,0:T(8,128)S(1)} %add_add_fusion.1), channel_id=1, source_target_pairs={{0,192},{8,200},{16,208},{24,216},{32,224},{40,232},{48,240},{56,2... | collective-permute-start | bytes 307208 | tf_op jit(solution)/shard_map/ppermute | solution.py:265
  15.3 5.4 %collective-permute-start.4 = (f32[40,640]{1,0:T(8,128)S(1)}, f32[40,640]{1,0:T(8,128)S(1)}, u32[]{:S(2)}, u32[]{:S(2)}) collective-permute-start(f32[40,640]{1,0:T(8,128)S(1)} %add_add_fusion.1), channel_id=1, source_target_pairs={{0,64},{8,72},{16,80},{24,88},{32,96},{40,104},{48,112},{56,120},{... | collective-permute-start | bytes 307208 | tf_op jit(solution)/shard_map/ppermute | solution.py:265
  16.9 6.2 %collective-permute-start.3 = (f32[40,640]{1,0:T(8,128)S(1)}, f32[40,640]{1,0:T(8,128)S(1)}, u32[]{:S(2)}, u32[]{:S(2)}) collective-permute-start(f32[40,640]{1,0:T(8,128)S(1)} %add_add_fusion.1), channel_id=1, source_target_pairs={{0,128},{8,136},{16,144},{24,152},{32,160},{40,168},{48,176},{56,1... | collective-permute-start | bytes 307208 | tf_op jit(solution)/shard_map/ppermute | solution.py:265
  23.1 1.4 collective-permute-start.6
  49.4 14.5 %all-to-all-start.1 = ((f32[8,32,256]{2,1,0:T(8,128)}), f32[8,32,256]{2,1,0:T(8,128)S(1)}, u32[]{:S(2)}, u32[]{:S(2)}) async-start(f32[8,32,256]{2,1,0:T(8,128)} %broadcast_in_dim.8), calls=%async_computation.1 | async-start | bytes 524288 | tf_op jit(solution)/shard_map/all_to_all | solution.py:271
  68.5 19.3 %copy-start.5 = (f32[32,2048]{1,0:T(8,128)}, f32[32,2048]{1,0:T(8,128)S(1)}, u32[]{:S(2)}) copy-start(f32[32,2048]{1,0:T(8,128)S(1)} %get-tuple-element.54.refs_7_) | copy-start | bytes 786436
  68.5 6.1 %collective-permute-start.9 = (f32[32,640]{1,0:T(8,128)S(1)}, f32[32,640]{1,0:T(8,128)S(1)}, u32[]{:S(2)}, u32[]{:S(2)}) collective-permute-start(f32[32,640]{1,0:T(8,128)S(1)} %get-tuple-element.45), channel_id=1, source_target_pairs={{0,48},{8,56},{16,0},{24,8},{32,16},{40,24},{48,32},{56,40},{64,11... | collective-permute-start | bytes 245768 | tf_op jit(solution)/shard_map/ppermute | solution.py:265
  68.6 6.0 %collective-permute-start.8 = (f32[32,640]{1,0:T(8,128)S(1)}, f32[32,640]{1,0:T(8,128)S(1)}, u32[]{:S(2)}, u32[]{:S(2)}) collective-permute-start(f32[32,640]{1,0:T(8,128)S(1)} %get-tuple-element.45), channel_id=1, source_target_pairs={{0,16},{8,24},{16,32},{24,40},{32,48},{40,56},{48,0},{56,8},{64,80... | collective-permute-start | bytes 245768 | tf_op jit(solution)/shard_map/ppermute | solution.py:265
  71.9 5.9 %collective-permute-start.7 = (f32[32,640]{1,0:T(8,128)S(1)}, f32[32,640]{1,0:T(8,128)S(1)}, u32[]{:S(2)}, u32[]{:S(2)}) collective-permute-start(f32[32,640]{1,0:T(8,128)S(1)} %get-tuple-element.45), channel_id=1, source_target_pairs={{0,32},{8,40},{16,48},{24,56},{32,0},{40,8},{48,16},{56,24},{64,96... | collective-permute-start | bytes 245768 | tf_op jit(solution)/shard_map/ppermute | solution.py:265
  77.8 5.0 %collective-permute-start.12 = (f32[32,640]{1,0:T(8,128)S(1)}, f32[32,640]{1,0:T(8,128)S(1)}, u32[]{:S(2)}, u32[]{:S(2)}) collective-permute-start(f32[32,640]{1,0:T(8,128)S(1)} %add_add_fusion.7), channel_id=1, source_target_pairs={{0,192},{8,200},{16,208},{24,216},{32,224},{40,232},{48,240},{56,2... | collective-permute-start | bytes 245768 | tf_op jit(solution)/shard_map/ppermute | solution.py:265
  78.4 4.7 %collective-permute-start.11 = (f32[32,640]{1,0:T(8,128)S(1)}, f32[32,640]{1,0:T(8,128)S(1)}, u32[]{:S(2)}, u32[]{:S(2)}) collective-permute-start(f32[32,640]{1,0:T(8,128)S(1)} %add_add_fusion.7), channel_id=1, source_target_pairs={{0,64},{8,72},{16,80},{24,88},{32,96},{40,104},{48,112},{56,120},{... | collective-permute-start | bytes 245768 | tf_op jit(solution)/shard_map/ppermute | solution.py:265
  80.5 5.9 %collective-permute-start.10 = (f32[32,640]{1,0:T(8,128)S(1)}, f32[32,640]{1,0:T(8,128)S(1)}, u32[]{:S(2)}, u32[]{:S(2)}) collective-permute-start(f32[32,640]{1,0:T(8,128)S(1)} %add_add_fusion.7), channel_id=1, source_target_pairs={{0,128},{8,136},{16,144},{24,152},{32,160},{40,168},{48,176},{56,1... | collective-permute-start | bytes 245768 | tf_op jit(solution)/shard_map/ppermute | solution.py:265
  86.5 1.4 collective-permute-start.13
  87.8 37.8 %copy-start.6 = (f32[32,2048]{1,0:T(8,128)S(1)}, f32[32,2048]{1,0:T(8,128)}, u32[]{:S(2)}) copy-start(f32[32,2048]{1,0:T(8,128)} %copy-done.5) | copy-start | bytes 786436
  89.3 0.6 copy-start.7
  110.0 15.7 %all-to-all-start.3 = ((f32[8,32,256]{2,1,0:T(8,128)}), f32[8,32,256]{2,1,0:T(8,128)S(1)}, u32[]{:S(2)}, u32[]{:S(2)}) async-start(f32[8,32,256]{2,1,0:T(8,128)} %broadcast_in_dim.9), calls=%async_computation.3 | async-start | bytes 524288 | tf_op jit(solution)/shard_map/all_to_all | solution.py:271
  125.7 24.6 %copy-start.8 = (f32[32,512]{1,0:T(8,128)S(1)}, f32[32,512]{1,0:T(8,128)}, u32[]{:S(2)}) copy-start(f32[32,512]{1,0:T(8,128)} %copy-done.7) | copy-start | bytes 196612
  130.4 20.0 %copy-start.3 = (f32[32,2048]{1,0:T(8,128)}, f32[32,2048]{1,0:T(8,128)S(1)}, u32[]{:S(2)}) copy-start(f32[32,2048]{1,0:T(8,128)S(1)} %get-tuple-element.63.refs_7_) | copy-start | bytes 786436
  130.4 5.7 %collective-permute-start.16 = (f32[32,640]{1,0:T(8,128)S(1)}, f32[32,640]{1,0:T(8,128)S(1)}, u32[]{:S(2)}, u32[]{:S(2)}) collective-permute-start(f32[32,640]{1,0:T(8,128)S(1)} %get-tuple-element.55), channel_id=1, source_target_pairs={{0,48},{8,56},{16,0},{24,8},{32,16},{40,24},{48,32},{56,40},{64,11... | collective-permute-start | bytes 245768 | tf_op jit(solution)/shard_map/ppermute | solution.py:265
  130.5 6.5 %collective-permute-start.15 = (f32[32,640]{1,0:T(8,128)S(1)}, f32[32,640]{1,0:T(8,128)S(1)}, u32[]{:S(2)}, u32[]{:S(2)}) collective-permute-start(f32[32,640]{1,0:T(8,128)S(1)} %get-tuple-element.55), channel_id=1, source_target_pairs={{0,16},{8,24},{16,32},{24,40},{32,48},{40,56},{48,0},{56,8},{64,80... | collective-permute-start | bytes 245768 | tf_op jit(solution)/shard_map/ppermute | solution.py:265
  133.7 5.9 %collective-permute-start.14 = (f32[32,640]{1,0:T(8,128)S(1)}, f32[32,640]{1,0:T(8,128)S(1)}, u32[]{:S(2)}, u32[]{:S(2)}) collective-permute-start(f32[32,640]{1,0:T(8,128)S(1)} %get-tuple-element.55), channel_id=1, source_target_pairs={{0,32},{8,40},{16,48},{24,56},{32,0},{40,8},{48,16},{56,24},{64,96... | collective-permute-start | bytes 245768 | tf_op jit(solution)/shard_map/ppermute | solution.py:265
  139.7 6.3 %collective-permute-start.19 = (f32[32,640]{1,0:T(8,128)S(1)}, f32[32,640]{1,0:T(8,128)S(1)}, u32[]{:S(2)}, u32[]{:S(2)}) collective-permute-start(f32[32,640]{1,0:T(8,128)S(1)} %add_add_fusion.5), channel_id=1, source_target_pairs={{0,192},{8,200},{16,208},{24,216},{32,224},{40,232},{48,240},{56,2... | collective-permute-start | bytes 245768 | tf_op jit(solution)/shard_map/ppermute | solution.py:265
  140.8 5.3 %collective-permute-start.18 = (f32[32,640]{1,0:T(8,128)S(1)}, f32[32,640]{1,0:T(8,128)S(1)}, u32[]{:S(2)}, u32[]{:S(2)}) collective-permute-start(f32[32,640]{1,0:T(8,128)S(1)} %add_add_fusion.5), channel_id=1, source_target_pairs={{0,64},{8,72},{16,80},{24,88},{32,96},{40,104},{48,112},{56,120},{... | collective-permute-start | bytes 245768 | tf_op jit(solution)/shard_map/ppermute | solution.py:265
  143.0 5.9 %collective-permute-start.17 = (f32[32,640]{1,0:T(8,128)S(1)}, f32[32,640]{1,0:T(8,128)S(1)}, u32[]{:S(2)}, u32[]{:S(2)}) collective-permute-start(f32[32,640]{1,0:T(8,128)S(1)} %add_add_fusion.5), channel_id=1, source_target_pairs={{0,128},{8,136},{16,144},{24,152},{32,160},{40,168},{48,176},{56,1... | collective-permute-start | bytes 245768 | tf_op jit(solution)/shard_map/ppermute | solution.py:265
  148.9 1.4 collective-permute-start.20
  150.3 37.2 %copy-start.4 = (f32[32,2048]{1,0:T(8,128)S(1)}, f32[32,2048]{1,0:T(8,128)}, u32[]{:S(2)}) copy-start(f32[32,2048]{1,0:T(8,128)} %copy-done.3) | copy-start | bytes 786436
  171.9 15.7 %all-to-all-start.5 = ((f32[8,32,256]{2,1,0:T(8,128)}), f32[8,32,256]{2,1,0:T(8,128)S(1)}, u32[]{:S(2)}, u32[]{:S(2)}) async-start(f32[8,32,256]{2,1,0:T(8,128)} %broadcast_in_dim.10), calls=%async_computation.5 | async-start | bytes 524288 | tf_op jit(solution)/shard_map/all_to_all | solution.py:271
  192.7 6.1 %collective-permute-start.23 = (f32[32,768]{1,0:T(8,128)S(1)}, f32[32,768]{1,0:T(8,128)S(1)}, u32[]{:S(2)}, u32[]{:S(2)}) collective-permute-start(f32[32,768]{1,0:T(8,128)S(1)} %get-tuple-element.64), channel_id=1, source_target_pairs={{0,48},{8,56},{16,0},{24,8},{32,16},{40,24},{48,32},{56,40},{64,11... | collective-permute-start | bytes 294920 | tf_op jit(solution)/shard_map/ppermute | solution.py:265
  193.0 7.2 %collective-permute-start.22 = (f32[32,768]{1,0:T(8,128)S(1)}, f32[32,768]{1,0:T(8,128)S(1)}, u32[]{:S(2)}, u32[]{:S(2)}) collective-permute-start(f32[32,768]{1,0:T(8,128)S(1)} %get-tuple-element.64), channel_id=1, source_target_pairs={{0,16},{8,24},{16,32},{24,40},{32,48},{40,56},{48,0},{56,8},{64,80... | collective-permute-start | bytes 294920 | tf_op jit(solution)/shard_map/ppermute | solution.py:265
  196.2 6.1 %collective-permute-start.21 = (f32[32,768]{1,0:T(8,128)S(1)}, f32[32,768]{1,0:T(8,128)S(1)}, u32[]{:S(2)}, u32[]{:S(2)}) collective-permute-start(f32[32,768]{1,0:T(8,128)S(1)} %get-tuple-element.64), channel_id=1, source_target_pairs={{0,32},{8,40},{16,48},{24,56},{32,0},{40,8},{48,16},{56,24},{64,96... | collective-permute-start | bytes 294920 | tf_op jit(solution)/shard_map/ppermute | solution.py:265
  202.4 6.7 %collective-permute-start.26 = (f32[32,768]{1,0:T(8,128)S(1)}, f32[32,768]{1,0:T(8,128)S(1)}, u32[]{:S(2)}, u32[]{:S(2)}) collective-permute-start(f32[32,768]{1,0:T(8,128)S(1)} %add_add_fusion.3), channel_id=1, source_target_pairs={{0,192},{8,200},{16,208},{24,216},{32,224},{40,232},{48,240},{56,2... | collective-permute-start | bytes 294920 | tf_op jit(solution)/shard_map/ppermute | solution.py:265
  203.5 5.7 %collective-permute-start.25 = (f32[32,768]{1,0:T(8,128)S(1)}, f32[32,768]{1,0:T(8,128)S(1)}, u32[]{:S(2)}, u32[]{:S(2)}) collective-permute-start(f32[32,768]{1,0:T(8,128)S(1)} %add_add_fusion.3), channel_id=1, source_target_pairs={{0,64},{8,72},{16,80},{24,88},{32,96},{40,104},{48,112},{56,120},{... | collective-permute-start | bytes 294920 | tf_op jit(solution)/shard_map/ppermute | solution.py:265
  205.7 6.1 %collective-permute-start.24 = (f32[32,768]{1,0:T(8,128)S(1)}, f32[32,768]{1,0:T(8,128)S(1)}, u32[]{:S(2)}, u32[]{:S(2)}) collective-permute-start(f32[32,768]{1,0:T(8,128)S(1)} %add_add_fusion.3), channel_id=1, source_target_pairs={{0,128},{8,136},{16,144},{24,152},{32,160},{40,168},{48,176},{56,1... | collective-permute-start | bytes 294920 | tf_op jit(solution)/shard_map/ppermute | solution.py:265
  211.8 1.4 collective-permute-start.27

commit v2 on v1

v2 whole, which is shorter than its diff:
```python
import functools

import jax
import jax.numpy as jnp
from jax import lax
from jax.experimental import pallas as pl
from jax.experimental.pallas import tpu as pltpu
from jax.sharding import PartitionSpec as P

ITERS = 4
RHS = 32
XSIZE, YSIZE, CORES = 4, 4, 2
F32, BF16 = jnp.float32, jnp.bfloat16
NT = (((1,), (1,)), ((), ()))
PARAMS = pltpu.CompilerParams(vmem_limit_bytes=12 * 1024 * 1024)


def split(x):
    high = x.astype(BF16)
    rest = x - high.astype(F32)
    mid = rest.astype(BF16)
    low = (rest - mid.astype(F32)).astype(BF16)
    return high, mid, low


def stacked(x):
    return jnp.concatenate(split(x), axis=0)


def fold(x):
    n = x.shape[0] // 3
    return x[:n] + (x[n:2 * n] + x[2 * n:])


def gram(left, right):
    full = fold(lax.dot_general(left, right, NT, preferred_element_type=F32))
    n = full.shape[1] // 3
    return full[:, :n] + (full[:, n:2 * n] + full[:, 2 * n:])


def small_dot(left, right):
    lh, lm, ll = split(left)
    rh, rm, rl = split(right)
    lhs = jnp.concatenate([lh, lh, lm, lm, lh, ll], axis=1)
    rhs = jnp.concatenate([rh, rm, rh, rm, rl, rh], axis=0)
    return jnp.dot(lhs, rhs, preferred_element_type=F32)


def symmetric(x):
    return 0.5 * (x + x.T)


def left_divide(gram_, right):
    n = gram_.shape[0]
    diag = lax.broadcasted_iota(jnp.int32, (n, n), 0) == lax.broadcasted_iota(jnp.int32, (n, n), 1)
    only = jnp.where(diag, gram_, 0.0)
    down = lax.rsqrt(jnp.sum(only, axis=1, keepdims=True))
    across = lax.rsqrt(jnp.sum(only, axis=0, keepdims=True))
    m = jnp.concatenate([gram_ * across, right], axis=1) * down
    sub = lax.broadcasted_iota(jnp.int32, (n, 1), 0)
    for k in range(0, n, 2):
        c0 = jnp.broadcast_to(m[:, k:k + 1], m.shape)
        c1 = jnp.broadcast_to(m[:, k + 1:k + 2], m.shape)
        r0, r1 = m[k:k + 1, :], m[k + 1:k + 2, :]
        p, q, r = c0[k:k + 1, :], c0[k + 1:k + 2, :], c1[k + 1:k + 2, :]
        inverse = 1.0 / (p * r - q * q)
        n0 = (r * r0 - q * r1) * inverse
        n1 = (p * r1 - q * r0) * inverse
        m = jnp.where(sub == k, n0, jnp.where(sub == k + 1, n1, m - c0 * n0 - c1 * n1))
    return m[:, n:] * down


SIDE = {"norm": (0, 0), "sums": (0, 32), "held_resid": (0, 64), "cross": (1, 0), "held_dir": (1, 32), "held_sol": (1, 64)}


def put(ref, name, value):
    half, lane = SIDE[name]
    lane += ref.shape[2] - 128
    ref[half, 0:RHS, lane:lane + value.shape[1]] = value


def take(ref, name, lanes=RHS):
    half, lane = SIDE[name]
    lane += ref.shape[2] - 128
    return ref[half, 0:RHS, lane:lane + lanes]


QUARTERS = 4


def prep_kernel(geno_hbm, rhs_hbm, codes_ref, pay_ref, geno_ref, rhs_ref, sems):
    rows, cols = geno_ref.shape
    half, chunk = cols // 2, rows // QUARTERS
    rhs_copy = pltpu.make_async_copy(rhs_hbm, rhs_ref, sems.at[QUARTERS])
    rhs_copy.start()
    copies = []
    for q in range(QUARTERS):
        part = pl.ds(q * chunk, chunk)
        copies.append(pltpu.make_async_copy(geno_hbm.at[part, :], geno_ref.at[part, :], sems.at[q]))
        copies[-1].start()
    rhs_copy.wait()
    rhs = rhs_ref[...]
    pieces = stacked(rhs)
    pay_ref[...] = jnp.zeros_like(pay_ref)
    put(pay_ref, "norm", gram(pieces, pieces))
    put(pay_ref, "sums", jnp.sum(rhs, axis=1, keepdims=True))
    lhs = jnp.concatenate([pieces, jnp.ones((32, rows), BF16)], axis=0)
    panel_, sums, squares = 0.0, 0.0, 0.0
    for q in range(QUARTERS):
        copies[q].wait()
        centred = (geno_ref[q * chunk:(q + 1) * chunk, :] - 1).astype(F32)
        codes = centred.astype(BF16)
        codes_ref[q * chunk:(q + 1) * chunk, :] = codes
        squares = squares + jnp.sum(centred * centred, axis=0, keepdims=True)
        acc = jnp.dot(lhs[:, q * chunk:(q + 1) * chunk], codes, preferred_element_type=F32)
        panel_ = panel_ + fold(acc[:96])
        sums = sums + acc[96:97]
    for c in range(2):
        part = slice(c * half, (c + 1) * half)
        pay_ref[c, 0:RHS, :half] = panel_[:, part]
        pay_ref[c, 32:33, :half] = sums[:, part]
        pay_ref[c, 33:34, :half] = squares[:, part]


def prep(genotypes, rhs):
    rows, cols = genotypes.shape
    hbm = pl.BlockSpec(memory_space=pltpu.HBM)
    return pl.pallas_call(
        prep_kernel,
        in_specs=[hbm, hbm],
        out_shape=[jax.ShapeDtypeStruct((rows, cols), BF16), jax.ShapeDtypeStruct((2, 40, cols // 2 + 128), F32)],
        scratch_shapes=[pltpu.VMEM((rows, cols), jnp.int32), pltpu.VMEM((RHS, rows), F32),
                        pltpu.SemaphoreType.DMA((QUARTERS + 1,))],
        compiler_params=PARAMS,
        name="prep",
    )(pltpu.with_memory_space_constraint(genotypes, pltpu.HBM), pltpu.with_memory_space_constraint(rhs, pltpu.HBM))


def panel_kernel(total, first, last, parts, *refs):
    if first:
        red_ref, codes_ref, u_ref, stat_ref, norm_ref, pp_ref, out_ref = refs
    else:
        red_ref, codes_ref, oldu_ref, stat_in_ref, inv_ref, oldpp_ref, u_ref, norm_ref, pp_ref, beta_ref, out_ref = refs
    half = red_ref.shape[2] - 128

    def row(i):
        return jnp.concatenate([red_ref[0, i:i + 1, :half], red_ref[1, i:i + 1, :half]], axis=1)

    if first:
        mean = row(32) * (1.0 / total)
        scale = 1.0 / jnp.sqrt(row(33) * (1.0 / total) - mean * mean + 1e-05)
        stat_ref[0:1, :] = mean
        stat_ref[1:2, :] = scale
    else:
        mean, scale = stat_in_ref[0:1, :], stat_in_ref[1:2, :]
    norm = symmetric(take(red_ref, "norm"))
    u = jnp.concatenate([red_ref[0, 0:RHS, :half], red_ref[1, 0:RHS, :half]], axis=1)
    u = (u - take(red_ref, "sums", 1) * mean) * scale
    norm_ref[...] = norm
    if first:
        pp = norm
    else:
        beta = small_dot(norm, inv_ref[...])
        u = u + small_dot(beta, oldu_ref[...])
        cross = small_dot(beta, take(red_ref, "cross"))
        pp = norm + (cross + cross.T) + symmetric(small_dot(small_dot(beta, oldpp_ref[...]), beta.T))
        beta_ref[...] = beta
    pp_ref[...] = pp
    u_ref[...] = u
    pieces = stacked(u)
    uu = gram(pieces, pieces)
    packed = jnp.concatenate([uu[4 * i:4 * i + 4] for i in range(8)], axis=1)
    if last:
        for j in range(parts):
            out_ref[j, :, :] = packed
        return
    weight = u * scale
    image = fold(lax.dot_general(stacked(weight), codes_ref[...], NT, preferred_element_type=F32))
    image = image - jnp.sum(weight * mean, axis=1, keepdims=True)
    width = image.shape[1] // parts
    for j in range(parts):
        out_ref[j, 0:RHS, :] = image[:, j * width:(j + 1) * width]
        out_ref[j, RHS:, :] = packed


def unpack(block):
    return jnp.concatenate([block[0:4, 32 * i:32 * i + 32] for i in range(8)], axis=0)


def panel(total, first, last, parts, *args):
    rows, cols = args[1].shape
    small = jax.ShapeDtypeStruct((RHS, RHS), F32)
    outs = [jax.ShapeDtypeStruct((RHS, cols), F32)]
    if first:
        outs.append(jax.ShapeDtypeStruct((8, cols), F32))
    outs += [small, small]
    if not first:
        outs.append(small)
    outs.append(jax.ShapeDtypeStruct((parts, 4 if last else RHS + 4, 256), F32))
    return pl.pallas_call(
        functools.partial(panel_kernel, total, first, last, parts),
        out_shape=outs,
        compiler_params=PARAMS,
        name="panel",
    )(*args)


def solve_kernel(markers, first, *refs):
    if first:
        ridge_ref, got_ref, pp_ref, norm_ref, resid_ref, send_ref, alpha_ref, inv_ref, sol_ref, base_ref = refs
    else:
        (ridge_ref, got_ref, pp_ref, norm_ref, resid_ref, beta_ref, olddir_ref, oldsol_ref,
         send_ref, alpha_ref, inv_ref, sol_ref, base_ref, dir_ref) = refs
    lam = ridge_ref[0]
    norm = norm_ref[...]
    parts = got_ref.shape[0]
    got = got_ref[0]
    for j in range(1, parts):
        got = got + got_ref[j]
    eye = (lax.broadcasted_iota(jnp.int32, norm.shape, 0) == lax.broadcasted_iota(jnp.int32, norm.shape, 1)).astype(F32)
    curvature = symmetric(unpack(got[RHS:]) * (1.0 / markers) + lam * pp_ref[...])
    alpha = left_divide(curvature, norm).T
    inv_ref[...] = left_divide(norm, eye)
    alpha_ref[...] = alpha * (1.0 / markers)
    for j in range(parts):
        send_ref[j, :, :] = got[:RHS]
    resid = resid_ref[...]
    if first:
        direction = resid
    else:
        direction = resid + small_dot(beta_ref[...], olddir_ref[...])
        dir_ref[...] = direction
    move = small_dot(alpha, direction)
    sol_ref[...] = move if first else oldsol_ref[...] + move
    base_ref[...] = resid - lam * move


def solve(markers, first, *args):
    vmem = pl.BlockSpec(memory_space=pltpu.VMEM)
    long = jax.ShapeDtypeStruct(args[4].shape, F32)
    small = jax.ShapeDtypeStruct((RHS, RHS), F32)
    parts, _, width = args[1].shape
    return pl.pallas_call(
        functools.partial(solve_kernel, markers, first),
        in_specs=[pl.BlockSpec(memory_space=pltpu.SMEM)] + [vmem] * (len(args) - 1),
        out_shape=[jax.ShapeDtypeStruct((parts, RHS, width), F32), small, small, long, long] + ([] if first else [long]),
        compiler_params=PARAMS,
        name="solve",
    )(*args)


def step_kernel(held_too, *refs):
    if held_too:
        image_ref, alpha_ref, base_ref, dir_ref, codes_ref, sol_ref, held_ref, resid_ref, pay_ref = refs
    else:
        image_ref, alpha_ref, base_ref, dir_ref, codes_ref, resid_ref, pay_ref = refs
    half = codes_ref.shape[1] // 2
    image = jnp.concatenate([image_ref[j] for j in range(image_ref.shape[0])], axis=1)
    resid = base_ref[...] - small_dot(alpha_ref[...], image)
    resid_ref[...] = resid
    pieces = stacked(resid)
    dpieces = stacked(dir_ref[...])
    panel_ = fold(jnp.dot(pieces, codes_ref[...], preferred_element_type=F32))
    for c in range(2):
        pay_ref[c, :, :half] = panel_[:, c * half:(c + 1) * half]
        pay_ref[c, :, half:] = jnp.zeros((RHS, 128), F32)
    put(pay_ref, "norm", gram(pieces, pieces))
    put(pay_ref, "sums", jnp.sum(resid, axis=1, keepdims=True))
    put(pay_ref, "cross", gram(dpieces, pieces))
    if held_too:
        place = lax.broadcasted_iota(jnp.int32, resid.shape, 1)
        chosen = (place == held_ref[...]).astype(BF16)
        for name, value in (("held_resid", pieces), ("held_dir", dpieces), ("held_sol", stacked(sol_ref[...]))):
            put(pay_ref, name, fold(lax.dot_general(value, chosen, NT, preferred_element_type=F32)))


def step(held_too, *args):
    rows, cols = args[4].shape
    return pl.pallas_call(
        functools.partial(step_kernel, held_too),
        out_shape=[jax.ShapeDtypeStruct((RHS, rows), F32), jax.ShapeDtypeStruct((2, RHS, cols // 2 + 128), F32)],
        compiler_params=PARAMS,
        name="step",
    )(*args)


def last_kernel(markers, ridge_ref, got_ref, pp_ref, norm_ref, beta_ref, resid_ref, olddir_ref, sol_ref, red_ref,
                out_ref, held_ref):
    got = got_ref[0]
    for j in range(1, got_ref.shape[0]):
        got = got + got_ref[j]
    alpha = left_divide(symmetric(unpack(got) * (1.0 / markers) + ridge_ref[0] * pp_ref[...]), norm_ref[...]).T
    beta = beta_ref[...]
    out_ref[...] = sol_ref[...] + small_dot(alpha, resid_ref[...] + small_dot(beta, olddir_ref[...]))
    direction = take(red_ref, "held_resid") + small_dot(beta, take(red_ref, "held_dir"))
    rows = take(red_ref, "held_sol") + small_dot(alpha, direction)
    eye = lax.broadcasted_iota(jnp.int32, rows.shape, 0) == lax.broadcasted_iota(jnp.int32, rows.shape, 1)
    held_ref[...] = jnp.sum(jnp.where(eye, rows, 0.0), axis=0, keepdims=True)


def last_step(markers, *args):
    vmem = pl.BlockSpec(memory_space=pltpu.VMEM)
    return pl.pallas_call(
        functools.partial(last_kernel, markers),
        in_specs=[pl.BlockSpec(memory_space=pltpu.SMEM)] + [vmem] * (len(args) - 1),
        out_shape=[jax.ShapeDtypeStruct(args[5].shape, F32), jax.ShapeDtypeStruct((1, RHS), F32)],
        compiler_params=PARAMS,
        name="last",
    )(*args)


def on_ind(move):
    pairs = []
    for y in range(YSIZE):
        for x in range(XSIZE):
            for c in range(CORES):
                ty, tx, tc = move(y, x, c)
                pairs.append(((y * XSIZE + x) * CORES + c, (ty * XSIZE + tx) * CORES + tc))
    return pairs


def swap_cores(value):
    return lax.ppermute(value, "ind", on_ind(lambda y, x, c: (y, x, 1 - c)))


def sum_ind(value):
    odd = lax.axis_index("ind") % CORES == 1
    mine = jnp.where(odd, value[1], value[0])
    mine = mine + swap_cores(jnp.where(odd, value[0], value[1]))
    for along in ("x", "y"):
        moved = []
        for d in (1, 2, 3):
            if along == "x":
                pairs = on_ind(lambda y, x, c, d=d: (y, (x + d) % XSIZE, c))
            else:
                pairs = on_ind(lambda y, x, c, d=d: ((y + d) % YSIZE, x, c))
            moved.append(lax.ppermute(mine, "ind", pairs))
        mine = (mine + moved[1]) + (moved[0] + moved[2])
    other = swap_cores(mine)
    return jnp.stack([jnp.where(odd, other, mine), jnp.where(odd, mine, other)])


def exchange(value):
    return lax.all_to_all(value, "snp", 0, 0)


def shards(genotypes, targets, ridge, held_out):
    rows, cols = genotypes.shape
    parts = lax.axis_size("snp")
    total = rows * lax.axis_size("ind")
    markers = cols * parts
    place = (held_out - lax.axis_index("ind") * rows)[:, None]

    resid = targets.T
    codes, pay = prep(genotypes, resid)
    for k in range(ITERS):
        first, last = k == 0, k == ITERS - 1
        red = sum_ind(pay)
        if first:
            u, stat, norm, pp, out = panel(total, True, False, parts, red, codes)
        else:
            u, norm, pp, beta, out = panel(total, False, last, parts, red, codes, u, stat, inv, pp)
        got = exchange(out)
        if last:
            break
        args = [ridge, got, pp, norm, resid]
        if first:
            direction = resid
            send, alpha, inv, sol, base = solve(markers, True, *args)
        else:
            send, alpha, inv, sol, base, direction = solve(markers, False, *args, beta, direction, sol)
        image = exchange(send)
        held_too = k == ITERS - 2
        resid, pay = step(held_too, image, alpha, base, direction, codes, *([sol, place] if held_too else []))
    sol, held = last_step(markers, ridge, got, pp, norm, beta, resid, direction, sol, red)
    return sol.T, held[0]


def solution(mesh):
    return jax.shard_map(
        shards,
        mesh=mesh,
        in_specs=(P("ind", "snp"), P("ind", None), P(), P()),
        out_specs=(P("ind", None), P()),
        check_vma=False,
    )
```

time: 235 us -> 209 us (0.89)
  waiting for transfers between devices: 80.1 us -> 68.3 us
  local copies, waits for them, and re-layouts: 6.06 us -> 0.1 us
  other arithmetic: 2.96 us -> 0.28 us
  starting transfers between devices: 42.9 us -> 40.3 us
    all_to_all x3 -> x2, waiting for transfers between devices: 34.2 us -> 24.6 us  [exchange(): return lax.all_to_all(value, 'snp', 0, 0)]
    ppermute x28 -> x32, starting transfers between devices: 32.7 us -> 28.2 us  [the longest x24 27.5 us: sum_ind(): moved.append(lax.ppermute(mine, 'ind', pairs))]
    unnamed x18 -> x4, local copies, waits for them, and re-layouts: 3.77 us -> 0.01 us
    pallas_call x5 -> x8, Pallas kernels: 19.8 us -> 17.4 us  [the longest x3 8 us: solve(): pl.pallas_call(functools.partial(solve_kernel, markers, first), in_specs=...]
    ppermute x28 -> x32, waiting for transfers between devices: 46 us -> 43.7 us  [the longest x24 33.9 us: sum_ind(): moved.append(lax.ppermute(mine, 'ind', pairs))]
    all_to_all x3 -> x2, starting transfers between devices: 10.2 us -> 12.1 us  [exchange(): return lax.all_to_all(value, 'snp', 0, 0)]
    all_to_all x4 -> x5, blocking collectives: 72 us -> 72.3 us  [exchange(): return lax.all_to_all(value, 'snp', 0, 0)]
  transfers between devices with their start and end apart: 31 -> 34, of which waited for: 30 -> 30; matrix products, arithmetic and copies ran while one was open for 0% -> 0% of each run, Pallas kernels for 0% -> 0%
where the time goes in v2:
time: 209 us; the launch traced here: 206 us
  blocking collectives  72.3 us (35%)
  waiting for transfers between devices  68.3 us (33%)
  starting transfers between devices  40.3 us (19%)
  Pallas kernels  22.7 us (11%)
    all_to_all x5, blocking collectives, exchange(): return lax.all_to_all(value, 'snp', 0, 0)  72.3 us
    ppermute x24, waiting for transfers between devices, sum_ind(): moved.append(lax.ppermute(mine, 'ind', pairs))  33.9 us
    ppermute x24, starting transfers between devices, sum_ind(): moved.append(lax.ppermute(mine, 'ind', pairs))  27.5 us
    all_to_all x2, waiting for transfers between devices, exchange(): return lax.all_to_all(value, 'snp', 0, 0)  24.6 us
    all_to_all x2, starting transfers between devices, exchange(): return lax.all_to_all(value, 'snp', 0, 0)  12.1 us
    ppermute x8, waiting for transfers between devices, swap_cores(): return lax.ppermute(value, 'ind', on_ind(lambda y, x, c: (y, x, 1 - c)))  9.77 us
    pallas_call x3, Pallas kernels, solve(): pl.pallas_call(functools.partial(solve_kernel, markers, first), in_specs=...  8 us
    pallas_call x4, Pallas kernels, panel(): pl.pallas_call(functools.partial(panel_kernel, total, first, last, parts)...  5.23 us
  transfers between devices with their start and end apart: 34, of which 30 were waited for; matrix products, arithmetic and copies ran while one was open for 0% of the time, Pallas kernels for 0%

profile of v2, /device:TPU:22, one launch (start us, length us, event | category | flops | bytes accessed | tf_op | source)
XLA Modules:
  0.0 205.5 jit_solution(2293739348920538737)
XLA Ops:
  0.7 2.9 %prep.1 = (bf16[2048,512]{1,0:T(8,128)(2,1)S(1)}, f32[2,40,384]{2,1,0:T(8,128)S(1)}) custom-call(s32[2048,512]{1,0:T(8,128)} %geno_hbm.1, f32[32,2048]{1,0:T(8,128)} %bitcast.37), custom_call_target="tpu_custom_call" | custom-call | tf_op jit(solution)/shard_map/prep/pallas_call | solution.py:128
  3.7 1.2 collective-permute-done
  4.9 1.5 collective-permute-start.1
  6.4 2.1 %collective-permute-start.2 = (f32[40,384]{1,0:T(8,128)S(1)}, f32[40,384]{1,0:T(8,128)S(1)}, u32[]{:S(2)}, u32[]{:S(2)}) collective-permute-start(f32[40,384]{1,0:T(8,128)S(1)} %bitcast_add_fusion), channel_id=1, source_target_pairs={{0,16},{8,24},{16,32},{24,40},{32,48},{40,56},{48,0},{56,8},{64,80... | collective-permute-start | bytes 184328 | tf_op jit(solution)/shard_map/ppermute | solution.py:337
  8.5 2.2 %collective-permute-done.1 = f32[40,384]{1,0:T(8,128)S(1)} collective-permute-done((f32[40,384]{1,0:T(8,128)S(1)}, f32[40,384]{1,0:T(8,128)S(1)}, u32[]{:S(2)}, u32[]{:S(2)}) %collective-permute-start.1) | collective-permute-done | bytes 61472 | tf_op jit(solution)/shard_map/ppermute | solution.py:337
  10.7 3.2 %collective-permute-done.3 = f32[40,384]{1,0:T(8,128)S(1)} collective-permute-done((f32[40,384]{1,0:T(8,128)S(1)}, f32[40,384]{1,0:T(8,128)S(1)}, u32[]{:S(2)}, u32[]{:S(2)}) %collective-permute-start.3) | collective-permute-done | bytes 61472 | tf_op jit(solution)/shard_map/ppermute | solution.py:337
  14.4 2.2 %collective-permute-start.5 = (f32[40,384]{1,0:T(8,128)S(1)}, f32[40,384]{1,0:T(8,128)S(1)}, u32[]{:S(2)}, u32[]{:S(2)}) collective-permute-start(f32[40,384]{1,0:T(8,128)S(1)} %add_add_fusion.1), channel_id=1, source_target_pairs={{0,64},{8,72},{16,80},{24,88},{32,96},{40,104},{48,112},{56,120},{... | collective-permute-start | bytes 184328 | tf_op jit(solution)/shard_map/ppermute | solution.py:337
  16.8 3.0 %collective-permute-done.4 = f32[40,384]{1,0:T(8,128)S(1)} collective-permute-done((f32[40,384]{1,0:T(8,128)S(1)}, f32[40,384]{1,0:T(8,128)S(1)}, u32[]{:S(2)}, u32[]{:S(2)}) %collective-permute-start.4) | collective-permute-done | bytes 61472 | tf_op jit(solution)/shard_map/ppermute | solution.py:337
  21.0 1.2 collective-permute-done.7
  22.3 1.6 panel.4
  23.9 8.5 %all-to-all-start = ((f32[8,36,256]{2,1,0:T(8,128)}), f32[8,36,256]{2,1,0:T(8,128)S(1)}, u32[]{:S(2)}, u32[]{:S(2)}) async-start(f32[8,36,256]{2,1,0:T(8,128)} %get-tuple-element.50), calls=%async_computation | async-start | bytes 655360 | tf_op jit(solution)/shard_map/all_to_all | solution.py:344
  33.0 13.0 %all-to-all-done.refs_1_ = f32[8,36,256]{2,1,0:T(8,128)S(1)} async-done(((f32[8,36,256]{2,1,0:T(8,128)}), f32[8,36,256]{2,1,0:T(8,128)S(1)}, u32[]{:S(2)}, u32[]{:S(2)}) %all-to-all-start) | async-done | bytes 294944 | tf_op jit(solution)/shard_map/all_to_all | solution.py:344
  46.0 2.4 %solve.3 = (f32[8,32,256]{2,1,0:T(8,128)S(1)}, f32[32,32]{1,0:T(8,128)S(1)}, f32[32,32]{1,0:T(8,128)S(1)}, f32[32,2048]{1,0:T(8,128)S(1)}, f32[32,2048]{1,0:T(8,128)S(1)}) custom-call(f32[1]{0:T(128)S(6)} %copy.7.refs_0_.ridge_ref, f32[8,36,256]{2,1,0:T(8,128)S(1)} %all-to-all-done.refs_1_, f32[32,32]{1,0:T(8,128)S(1)} %get-tuple-element.51.refs_2_.refs_5_, ...), custom_call_target="tpu_custom_call" | custom-call | tf_op jit(solution)/shard_map/solve/pallas_call | solution.py:243
  48.4 14.6 %all_to_all.35.refs_0_ = f32[8,32,256]{2,1,0:T(8,128)S(1)} all-to-all(f32[8,32,256]{2,1,0:T(8,128)S(1)} %get-tuple-element.53), channel_id=1, replica_groups=mesh['ind'=32,'snp'=8] {'snp'}, dimensions={0} | all-to-all | bytes 524288 | tf_op jit(solution)/shard_map/all_to_all | solution.py:344
  64.3 1.2 collective-permute-done.8
  65.6 2.0 collective-permute-start.11
  67.6 2.1 %collective-permute-done.10 = f32[32,384]{1,0:T(8,128)S(1)} collective-permute-done((f32[32,384]{1,0:T(8,128)S(1)}, f32[32,384]{1,0:T(8,128)S(1)}, u32[]{:S(2)}, u32[]{:S(2)}) %collective-permute-start.10) | collective-permute-done | bytes 49184 | tf_op jit(solution)/shard_map/ppermute | solution.py:337
  69.6 1.3 collective-permute-done.11
  71.0 2.2 %collective-permute-done.9 = f32[32,384]{1,0:T(8,128)S(1)} collective-permute-done((f32[32,384]{1,0:T(8,128)S(1)}, f32[32,384]{1,0:T(8,128)S(1)}, u32[]{:S(2)}, u32[]{:S(2)}) %collective-permute-start.9) | collective-permute-done | bytes 49184 | tf_op jit(solution)/shard_map/ppermute | solution.py:337
  73.2 2.2 %collective-permute-start.12 = (f32[32,384]{1,0:T(8,128)S(1)}, f32[32,384]{1,0:T(8,128)S(1)}, u32[]{:S(2)}, u32[]{:S(2)}) collective-permute-start(f32[32,384]{1,0:T(8,128)S(1)} %add_add_fusion.7), channel_id=1, source_target_pairs={{0,128},{8,136},{16,144},{24,152},{32,160},{40,168},{48,176},{56,1... | collective-permute-start | bytes 147464 | tf_op jit(solution)/shard_map/ppermute | solution.py:337
  75.4 1.4 collective-permute-start.13
  78.0 1.3 collective-permute-done.12
  81.0 1.2 collective-permute-done.15
  82.2 1.3 panel.5
  83.5 16.3 %all_to_all.36.refs_1_ = f32[8,36,256]{2,1,0:T(8,128)S(1)} all-to-all(f32[8,36,256]{2,1,0:T(8,128)S(1)} %get-tuple-element.60), channel_id=1, replica_groups=mesh['ind'=32,'snp'=8] {'snp'}, dimensions={0} | all-to-all | bytes 589824 | tf_op jit(solution)/shard_map/all_to_all | solution.py:344
  99.8 2.5 %solve.4 = (f32[8,32,256]{2,1,0:T(8,128)S(1)}, f32[32,32]{1,0:T(8,128)S(1)}, f32[32,32]{1,0:T(8,128)S(1)}, f32[32,2048]{1,0:T(8,128)S(1)}, f32[32,2048]{1,0:T(8,128)S(1)}, /*index=5*/f32[32,2048]{1,0:T(8,128)S(1)}) custom-call(f32[1]{0:T(128)S(6)} %copy.7.refs_0_.ridge_ref, f32[8,36,256]{2,1,0:T(8,128)S(1)} %all_to_all.36.refs_1_, ...), custom_call_target="tpu_custom_call" | custom-call | tf_op jit(solution)/shard_map/solve/pallas_call | solution.py:243
  102.2 14.8 %all_to_all.37.refs_0_ = f32[8,32,256]{2,1,0:T(8,128)S(1)} all-to-all(f32[8,32,256]{2,1,0:T(8,128)S(1)} %get-tuple-element.66), channel_id=1, replica_groups=mesh['ind'=32,'snp'=8] {'snp'}, dimensions={0} | all-to-all | bytes 524288 | tf_op jit(solution)/shard_map/all_to_all | solution.py:344
  118.2 1.2 collective-permute-done.16
  120.0 2.1 %collective-permute-start.18 = (f32[32,384]{1,0:T(8,128)S(1)}, f32[32,384]{1,0:T(8,128)S(1)}, u32[]{:S(2)}, u32[]{:S(2)}) collective-permute-start(f32[32,384]{1,0:T(8,128)S(1)} %bitcast_add_fusion.2), channel_id=1, source_target_pairs={{0,16},{8,24},{16,32},{24,40},{32,48},{40,56},{48,0},{56,8},{64,80... | collective-permute-start | bytes 147464 | tf_op jit(solution)/shard_map/ppermute | solution.py:337
  122.2 2.9 %collective-permute-done.17 = f32[32,384]{1,0:T(8,128)S(1)} collective-permute-done((f32[32,384]{1,0:T(8,128)S(1)}, f32[32,384]{1,0:T(8,128)S(1)}, u32[]{:S(2)}, u32[]{:S(2)}) %collective-permute-start.17) | collective-permute-done | bytes 49184 | tf_op jit(solution)/shard_map/ppermute | solution.py:337
  125.1 2.4 %collective-permute-done.19 = f32[32,384]{1,0:T(8,128)S(1)} collective-permute-done((f32[32,384]{1,0:T(8,128)S(1)}, f32[32,384]{1,0:T(8,128)S(1)}, u32[]{:S(2)}, u32[]{:S(2)}) %collective-permute-start.19) | collective-permute-done | bytes 49184 | tf_op jit(solution)/shard_map/ppermute | solution.py:337
  127.5 2.7 %collective-permute-start.20 = (f32[32,384]{1,0:T(8,128)S(1)}, f32[32,384]{1,0:T(8,128)S(1)}, u32[]{:S(2)}, u32[]{:S(2)}) collective-permute-start(f32[32,384]{1,0:T(8,128)S(1)} %add_add_fusion.5), channel_id=1, source_target_pairs={{0,128},{8,136},{16,144},{24,152},{32,160},{40,168},{48,176},{56,1... | collective-permute-start | bytes 147464 | tf_op jit(solution)/shard_map/ppermute | solution.py:337
  130.8 1.4 collective-permute-start.22
  135.0 1.2 collective-permute-done.23
  136.3 1.3 panel.6
  137.6 16.3 %all_to_all.38.refs_1_ = f32[8,36,256]{2,1,0:T(8,128)S(1)} all-to-all(f32[8,36,256]{2,1,0:T(8,128)S(1)} %get-tuple-element.73), channel_id=1, replica_groups=mesh['ind'=32,'snp'=8] {'snp'}, dimensions={0} | all-to-all | bytes 589824 | tf_op jit(solution)/shard_map/all_to_all | solution.py:344
  153.8 3.1 %solve.5 = (f32[8,32,256]{2,1,0:T(8,128)}, f32[32,32]{1,0:T(8,128)S(1)}, f32[32,32]{1,0:T(8,128)S(1)}, f32[32,2048]{1,0:T(8,128)S(1)}, f32[32,2048]{1,0:T(8,128)S(1)}, /*index=5*/f32[32,2048]{1,0:T(8,128)S(1)}) custom-call(f32[1]{0:T(128)S(6)} %copy.7.refs_0_.ridge_ref, f32[8,36,256]{2,1,0:T(8,128)S(1)} %all_to_all.38.refs_1_, ...), custom_call_target="tpu_custom_call" | custom-call | tf_op jit(solution)/shard_map/solve/pallas_call | solution.py:243
  156.9 3.6 %all-to-all-start.5 = ((f32[8,32,256]{2,1,0:T(8,128)}), f32[8,32,256]{2,1,0:T(8,128)S(1)}, u32[]{:S(2)}, u32[]{:S(2)}) async-start(f32[8,32,256]{2,1,0:T(8,128)} %get-tuple-element.79), calls=%async_computation.5 | async-start | bytes 524288 | tf_op jit(solution)/shard_map/all_to_all | solution.py:344
  160.7 11.7 %all-to-all-done.5.refs_0_ = f32[8,32,256]{2,1,0:T(8,128)S(1)} async-done(((f32[8,32,256]{2,1,0:T(8,128)}), f32[8,32,256]{2,1,0:T(8,128)S(1)}, u32[]{:S(2)}, u32[]{:S(2)}) %all-to-all-start.5) | async-done | bytes 262176 | tf_op jit(solution)/shard_map/all_to_all | solution.py:344
  172.4 1.2 step.5
  173.7 1.2 collective-permute-done.24
  177.4 3.3 %collective-permute-done.25 = f32[32,384]{1,0:T(8,128)S(1)} collective-permute-done((f32[32,384]{1,0:T(8,128)S(1)}, f32[32,384]{1,0:T(8,128)S(1)}, u32[]{:S(2)}, u32[]{:S(2)}) %collective-permute-start.25) | collective-permute-done | bytes 49184 | tf_op jit(solution)/shard_map/ppermute | solution.py:337
  181.8 2.2 %collective-permute-start.28 = (f32[32,384]{1,0:T(8,128)S(1)}, f32[32,384]{1,0:T(8,128)S(1)}, u32[]{:S(2)}, u32[]{:S(2)}) collective-permute-start(f32[32,384]{1,0:T(8,128)S(1)} %add_add_fusion.3), channel_id=1, source_target_pairs={{0,128},{8,136},{16,144},{24,152},{32,160},{40,168},{48,176},{56,1... | collective-permute-start | bytes 147464 | tf_op jit(solution)/shard_map/ppermute | solution.py:337
  184.0 1.4 collective-permute-start.29
  186.0 1.9 collective-permute-done.28
  189.6 1.2 collective-permute-done.31
  191.9 10.4 %all_to_all.39.got_ref = f32[8,4,256]{2,1,0:T(4,128)S(1)} all-to-all(f32[8,4,256]{2,1,0:T(4,128)S(1)} %get-tuple-element.87), channel_id=1, replica_groups=mesh['ind'=32,'snp'=8] {'snp'}, dimensions={0} | all-to-all | bytes 65536 | tf_op jit(solution)/shard_map/all_to_all | solution.py:344
  202.3 3.2 %last.1 = (f32[32,2048]{1,0:T(8,128)}, f32[1,32]{1,0:T(1,128)}) custom-call(f32[1]{0:T(128)S(6)} %copy.7.refs_0_.ridge_ref, f32[8,4,256]{2,1,0:T(4,128)S(1)} %all_to_all.39.got_ref, f32[32,32]{1,0:T(8,128)S(1)} %get-tuple-element.88.pp_ref, f32[32,32]{1,0:T(8,128)S(1)} %get-tuple-element.89.norm_ref, f32[32,32]{1,0:T(8,128)S(1)} %get-tuple-element.90.beta_ref, ...), custom_call_target="tpu_custom_call" | custom-call | tf_op jit(solution)/shard_map/last/pallas_call | solution.py:303
  (67 shorter events, 18.7 us)
Async XLA Ops:
  0.6 45.4 %copy-start = (f32[2048,32]{0,1:T(8,128)S(1)}, f32[2048,32]{0,1:T(8,128)}, u32[]{:S(2)}) copy-start(f32[2048,32]{0,1:T(8,128)} %param.5) | copy-start | bytes 786436
  3.6 1.3 collective-permute-start
  4.9 5.8 %collective-permute-start.1 = (f32[40,384]{1,0:T(8,128)S(1)}, f32[40,384]{1,0:T(8,128)S(1)}, u32[]{:S(2)}, u32[]{:S(2)}) collective-permute-start(f32[40,384]{1,0:T(8,128)S(1)} %bitcast_add_fusion), channel_id=1, source_target_pairs={{0,32},{8,40},{16,48},{24,56},{32,0},{40,8},{48,16},{56,24},{64,96... | collective-permute-start | bytes 184328 | tf_op jit(solution)/shard_map/ppermute | solution.py:337
  6.4 4.3 %collective-permute-start.2 = (f32[40,384]{1,0:T(8,128)S(1)}, f32[40,384]{1,0:T(8,128)S(1)}, u32[]{:S(2)}, u32[]{:S(2)}) collective-permute-start(f32[40,384]{1,0:T(8,128)S(1)} %bitcast_add_fusion), channel_id=1, source_target_pairs={{0,16},{8,24},{16,32},{24,40},{32,48},{40,56},{48,0},{56,8},{64,80... | collective-permute-start | bytes 184328 | tf_op jit(solution)/shard_map/ppermute | solution.py:337
  8.5 5.4 %collective-permute-start.3 = (f32[40,384]{1,0:T(8,128)S(1)}, f32[40,384]{1,0:T(8,128)S(1)}, u32[]{:S(2)}, u32[]{:S(2)}) collective-permute-start(f32[40,384]{1,0:T(8,128)S(1)} %bitcast_add_fusion), channel_id=1, source_target_pairs={{0,48},{8,56},{16,0},{24,8},{32,16},{40,24},{48,32},{56,40},{64,11... | collective-permute-start | bytes 184328 | tf_op jit(solution)/shard_map/ppermute | solution.py:337
  13.9 5.8 %collective-permute-start.4 = (f32[40,384]{1,0:T(8,128)S(1)}, f32[40,384]{1,0:T(8,128)S(1)}, u32[]{:S(2)}, u32[]{:S(2)}) collective-permute-start(f32[40,384]{1,0:T(8,128)S(1)} %add_add_fusion.1), channel_id=1, source_target_pairs={{0,128},{8,136},{16,144},{24,152},{32,160},{40,168},{48,176},{56,1... | collective-permute-start | bytes 184328 | tf_op jit(solution)/shard_map/ppermute | solution.py:337
  14.4 5.4 %collective-permute-start.5 = (f32[40,384]{1,0:T(8,128)S(1)}, f32[40,384]{1,0:T(8,128)S(1)}, u32[]{:S(2)}, u32[]{:S(2)}) collective-permute-start(f32[40,384]{1,0:T(8,128)S(1)} %add_add_fusion.1), channel_id=1, source_target_pairs={{0,64},{8,72},{16,80},{24,88},{32,96},{40,104},{48,112},{56,120},{... | collective-permute-start | bytes 184328 | tf_op jit(solution)/shard_map/ppermute | solution.py:337
  16.5 4.4 %collective-permute-start.6 = (f32[40,384]{1,0:T(8,128)S(1)}, f32[40,384]{1,0:T(8,128)S(1)}, u32[]{:S(2)}, u32[]{:S(2)}) collective-permute-start(f32[40,384]{1,0:T(8,128)S(1)} %add_add_fusion.1), channel_id=1, source_target_pairs={{0,192},{8,200},{16,208},{24,216},{32,224},{40,232},{48,240},{56,2... | collective-permute-start | bytes 184328 | tf_op jit(solution)/shard_map/ppermute | solution.py:337
  20.9 1.3 collective-permute-start.7
  23.9 22.1 %all-to-all-start = ((f32[8,36,256]{2,1,0:T(8,128)}), f32[8,36,256]{2,1,0:T(8,128)S(1)}, u32[]{:S(2)}, u32[]{:S(2)}) async-start(f32[8,36,256]{2,1,0:T(8,128)} %get-tuple-element.50), calls=%async_computation | async-start | bytes 655360 | tf_op jit(solution)/shard_map/all_to_all | solution.py:344
  64.2 1.3 collective-permute-start.8
  65.5 4.2 %collective-permute-start.10 = (f32[32,384]{1,0:T(8,128)S(1)}, f32[32,384]{1,0:T(8,128)S(1)}, u32[]{:S(2)}, u32[]{:S(2)}) collective-permute-start(f32[32,384]{1,0:T(8,128)S(1)} %bitcast_add_fusion.3), channel_id=1, source_target_pairs={{0,16},{8,24},{16,32},{24,40},{32,48},{40,56},{48,0},{56,8},{64,80... | collective-permute-start | bytes 147464 | tf_op jit(solution)/shard_map/ppermute | solution.py:337
  65.6 5.4 %collective-permute-start.11 = (f32[32,384]{1,0:T(8,128)S(1)}, f32[32,384]{1,0:T(8,128)S(1)}, u32[]{:S(2)}, u32[]{:S(2)}) collective-permute-start(f32[32,384]{1,0:T(8,128)S(1)} %bitcast_add_fusion.3), channel_id=1, source_target_pairs={{0,48},{8,56},{16,0},{24,8},{32,16},{40,24},{48,32},{56,40},{64,11... | collective-permute-start | bytes 147464 | tf_op jit(solution)/shard_map/ppermute | solution.py:337
  67.6 5.6 %collective-permute-start.9 = (f32[32,384]{1,0:T(8,128)S(1)}, f32[32,384]{1,0:T(8,128)S(1)}, u32[]{:S(2)}, u32[]{:S(2)}) collective-permute-start(f32[32,384]{1,0:T(8,128)S(1)} %bitcast_add_fusion.3), channel_id=1, source_target_pairs={{0,32},{8,40},{16,48},{24,56},{32,0},{40,8},{48,16},{56,24},{64,96... | collective-permute-start | bytes 147464 | tf_op jit(solution)/shard_map/ppermute | solution.py:337
  73.2 6.0 %collective-permute-start.12 = (f32[32,384]{1,0:T(8,128)S(1)}, f32[32,384]{1,0:T(8,128)S(1)}, u32[]{:S(2)}, u32[]{:S(2)}) collective-permute-start(f32[32,384]{1,0:T(8,128)S(1)} %add_add_fusion.7), channel_id=1, source_target_pairs={{0,128},{8,136},{16,144},{24,152},{32,160},{40,168},{48,176},{56,1... | collective-permute-start | bytes 147464 | tf_op jit(solution)/shard_map/ppermute | solution.py:337
  75.4 4.7 %collective-permute-start.13 = (f32[32,384]{1,0:T(8,128)S(1)}, f32[32,384]{1,0:T(8,128)S(1)}, u32[]{:S(2)}, u32[]{:S(2)}) collective-permute-start(f32[32,384]{1,0:T(8,128)S(1)} %add_add_fusion.7), channel_id=1, source_target_pairs={{0,64},{8,72},{16,80},{24,88},{32,96},{40,104},{48,112},{56,120},{... | collective-permute-start | bytes 147464 | tf_op jit(solution)/shard_map/ppermute | solution.py:337
  76.8 4.1 %collective-permute-start.14 = (f32[32,384]{1,0:T(8,128)S(1)}, f32[32,384]{1,0:T(8,128)S(1)}, u32[]{:S(2)}, u32[]{:S(2)}) collective-permute-start(f32[32,384]{1,0:T(8,128)S(1)} %add_add_fusion.7), channel_id=1, source_target_pairs={{0,192},{8,200},{16,208},{24,216},{32,224},{40,232},{48,240},{56,2... | collective-permute-start | bytes 147464 | tf_op jit(solution)/shard_map/ppermute | solution.py:337
  80.9 1.3 collective-permute-start.15
  117.0 43.6 %copy-start.1 = (s32[32]{0:T(128)S(1)}, s32[32]{0:T(128)}, u32[]{:S(2)}) copy-start(s32[32]{0:T(128)} %param.7) | copy-start | bytes 388
  118.1 1.3 collective-permute-start.16
  119.4 5.7 %collective-permute-start.17 = (f32[32,384]{1,0:T(8,128)S(1)}, f32[32,384]{1,0:T(8,128)S(1)}, u32[]{:S(2)}, u32[]{:S(2)}) collective-permute-start(f32[32,384]{1,0:T(8,128)S(1)} %bitcast_add_fusion.2), channel_id=1, source_target_pairs={{0,32},{8,40},{16,48},{24,56},{32,0},{40,8},{48,16},{56,24},{64,96... | collective-permute-start | bytes 147464 | tf_op jit(solution)/shard_map/ppermute | solution.py:337
  120.0 5.1 %collective-permute-start.18 = (f32[32,384]{1,0:T(8,128)S(1)}, f32[32,384]{1,0:T(8,128)S(1)}, u32[]{:S(2)}, u32[]{:S(2)}) collective-permute-start(f32[32,384]{1,0:T(8,128)S(1)} %bitcast_add_fusion.2), channel_id=1, source_target_pairs={{0,16},{8,24},{16,32},{24,40},{32,48},{40,56},{48,0},{56,8},{64,80... | collective-permute-start | bytes 147464 | tf_op jit(solution)/shard_map/ppermute | solution.py:337
  122.2 5.3 %collective-permute-start.19 = (f32[32,384]{1,0:T(8,128)S(1)}, f32[32,384]{1,0:T(8,128)S(1)}, u32[]{:S(2)}, u32[]{:S(2)}) collective-permute-start(f32[32,384]{1,0:T(8,128)S(1)} %bitcast_add_fusion.2), channel_id=1, source_target_pairs={{0,48},{8,56},{16,0},{24,8},{32,16},{40,24},{48,32},{56,40},{64,11... | collective-permute-start | bytes 147464 | tf_op jit(solution)/shard_map/ppermute | solution.py:337
  127.5 5.7 %collective-permute-start.20 = (f32[32,384]{1,0:T(8,128)S(1)}, f32[32,384]{1,0:T(8,128)S(1)}, u32[]{:S(2)}, u32[]{:S(2)}) collective-permute-start(f32[32,384]{1,0:T(8,128)S(1)} %add_add_fusion.5), channel_id=1, source_target_pairs={{0,128},{8,136},{16,144},{24,152},{32,160},{40,168},{48,176},{56,1... | collective-permute-start | bytes 147464 | tf_op jit(solution)/shard_map/ppermute | solution.py:337
  130.2 4.1 %collective-permute-start.21 = (f32[32,384]{1,0:T(8,128)S(1)}, f32[32,384]{1,0:T(8,128)S(1)}, u32[]{:S(2)}, u32[]{:S(2)}) collective-permute-start(f32[32,384]{1,0:T(8,128)S(1)} %add_add_fusion.5), channel_id=1, source_target_pairs={{0,64},{8,72},{16,80},{24,88},{32,96},{40,104},{48,112},{56,120},{... | collective-permute-start | bytes 147464 | tf_op jit(solution)/shard_map/ppermute | solution.py:337
  130.8 4.1 %collective-permute-start.22 = (f32[32,384]{1,0:T(8,128)S(1)}, f32[32,384]{1,0:T(8,128)S(1)}, u32[]{:S(2)}, u32[]{:S(2)}) collective-permute-start(f32[32,384]{1,0:T(8,128)S(1)} %add_add_fusion.5), channel_id=1, source_target_pairs={{0,192},{8,200},{16,208},{24,216},{32,224},{40,232},{48,240},{56,2... | collective-permute-start | bytes 147464 | tf_op jit(solution)/shard_map/ppermute | solution.py:337
  134.9 1.3 collective-permute-start.23
  156.9 15.4 %all-to-all-start.5 = ((f32[8,32,256]{2,1,0:T(8,128)}), f32[8,32,256]{2,1,0:T(8,128)S(1)}, u32[]{:S(2)}, u32[]{:S(2)}) async-start(f32[8,32,256]{2,1,0:T(8,128)} %get-tuple-element.79), calls=%async_computation.5 | async-start | bytes 524288 | tf_op jit(solution)/shard_map/all_to_all | solution.py:344
  173.6 1.3 collective-permute-start.24
  175.0 5.8 %collective-permute-start.25 = (f32[32,384]{1,0:T(8,128)S(1)}, f32[32,384]{1,0:T(8,128)S(1)}, u32[]{:S(2)}, u32[]{:S(2)}) collective-permute-start(f32[32,384]{1,0:T(8,128)S(1)} %bitcast_add_fusion.1), channel_id=1, source_target_pairs={{0,32},{8,40},{16,48},{24,56},{32,0},{40,8},{48,16},{56,24},{64,96... | collective-permute-start | bytes 147464 | tf_op jit(solution)/shard_map/ppermute | solution.py:337
  175.4 5.4 %collective-permute-start.26 = (f32[32,384]{1,0:T(8,128)S(1)}, f32[32,384]{1,0:T(8,128)S(1)}, u32[]{:S(2)}, u32[]{:S(2)}) collective-permute-start(f32[32,384]{1,0:T(8,128)S(1)} %bitcast_add_fusion.1), channel_id=1, source_target_pairs={{0,16},{8,24},{16,32},{24,40},{32,48},{40,56},{48,0},{56,8},{64,80... | collective-permute-start | bytes 147464 | tf_op jit(solution)/shard_map/ppermute | solution.py:337
  176.5 5.3 %collective-permute-start.27 = (f32[32,384]{1,0:T(8,128)S(1)}, f32[32,384]{1,0:T(8,128)S(1)}, u32[]{:S(2)}, u32[]{:S(2)}) collective-permute-start(f32[32,384]{1,0:T(8,128)S(1)} %bitcast_add_fusion.1), channel_id=1, source_target_pairs={{0,48},{8,56},{16,0},{24,8},{32,16},{40,24},{48,32},{56,40},{64,11... | collective-permute-start | bytes 147464 | tf_op jit(solution)/shard_map/ppermute | solution.py:337
  181.8 6.1 %collective-permute-start.28 = (f32[32,384]{1,0:T(8,128)S(1)}, f32[32,384]{1,0:T(8,128)S(1)}, u32[]{:S(2)}, u32[]{:S(2)}) collective-permute-start(f32[32,384]{1,0:T(8,128)S(1)} %add_add_fusion.3), channel_id=1, source_target_pairs={{0,128},{8,136},{16,144},{24,152},{32,160},{40,168},{48,176},{56,1... | collective-permute-start | bytes 147464 | tf_op jit(solution)/shard_map/ppermute | solution.py:337
  184.0 4.3 %collective-permute-start.29 = (f32[32,384]{1,0:T(8,128)S(1)}, f32[32,384]{1,0:T(8,128)S(1)}, u32[]{:S(2)}, u32[]{:S(2)}) collective-permute-start(f32[32,384]{1,0:T(8,128)S(1)} %add_add_fusion.3), channel_id=1, source_target_pairs={{0,64},{8,72},{16,80},{24,88},{32,96},{40,104},{48,112},{56,120},{... | collective-permute-start | bytes 147464 | tf_op jit(solution)/shard_map/ppermute | solution.py:337
  185.4 4.1 %collective-permute-start.30 = (f32[32,384]{1,0:T(8,128)S(1)}, f32[32,384]{1,0:T(8,128)S(1)}, u32[]{:S(2)}, u32[]{:S(2)}) collective-permute-start(f32[32,384]{1,0:T(8,128)S(1)} %add_add_fusion.3), channel_id=1, source_target_pairs={{0,192},{8,200},{16,208},{24,216},{32,224},{40,232},{48,240},{56,2... | collective-permute-start | bytes 147464 | tf_op jit(solution)/shard_map/ppermute | solution.py:337
  189.5 1.3 collective-permute-start.31

commit v3 on v2

v3 whole, which is shorter than its diff:
```python
import functools

import jax
import jax.numpy as jnp
from jax import lax
from jax.experimental import pallas as pl
from jax.experimental.pallas import tpu as pltpu
from jax.sharding import PartitionSpec as P

ITERS = 4
RHS = 32
XSIZE, YSIZE, CORES = 4, 4, 2
F32, BF16 = jnp.float32, jnp.bfloat16
NT = (((1,), (1,)), ((), ()))
PARAMS = pltpu.CompilerParams(vmem_limit_bytes=12 * 1024 * 1024)


def split(x):
    high = x.astype(BF16)
    rest = x - high.astype(F32)
    mid = rest.astype(BF16)
    low = (rest - mid.astype(F32)).astype(BF16)
    return high, mid, low


def stacked(x):
    return jnp.concatenate(split(x), axis=0)


def fold(x):
    n = x.shape[0] // 3
    return x[:n] + (x[n:2 * n] + x[2 * n:])


def gram(left, right):
    full = fold(lax.dot_general(left, right, NT, preferred_element_type=F32))
    n = full.shape[1] // 3
    return full[:, :n] + (full[:, n:2 * n] + full[:, 2 * n:])


def small_dot(left, right):
    lh, lm, ll = split(left)
    rh, rm, rl = split(right)
    lhs = jnp.concatenate([lh, lh, lm, lm, lh, ll], axis=1)
    rhs = jnp.concatenate([rh, rm, rh, rm, rl, rh], axis=0)
    return jnp.dot(lhs, rhs, preferred_element_type=F32)


def symmetric(x):
    return 0.5 * (x + x.T)


GROUP = 4


def left_divide(gram_, right):
    n = gram_.shape[0]
    diag = lax.broadcasted_iota(jnp.int32, (n, n), 0) == lax.broadcasted_iota(jnp.int32, (n, n), 1)
    only = jnp.where(diag, gram_, 0.0)
    down = lax.rsqrt(jnp.sum(only, axis=1, keepdims=True))
    across = lax.rsqrt(jnp.sum(only, axis=0, keepdims=True))
    m = jnp.concatenate([gram_ * across, right], axis=1) * down
    sub = lax.broadcasted_iota(jnp.int32, (n, 1), 0)
    for k in range(0, n, GROUP):
        wide = [jnp.broadcast_to(m[:, k + i:k + i + 1], m.shape) for i in range(GROUP)]
        for i in range(0, GROUP, 2):
            a, b = k + i, k + i + 1
            c0, c1 = wide[i], wide[i + 1]
            p, q, r = c0[a:a + 1, :], c0[b:b + 1, :], c1[b:b + 1, :]
            inverse = 1.0 / (p * r - q * q)

            def eliminate(v):
                r0, r1 = v[a:a + 1, :], v[b:b + 1, :]
                n0 = (r * r0 - q * r1) * inverse
                n1 = (p * r1 - q * r0) * inverse
                return jnp.where(sub == a, n0, jnp.where(sub == b, n1, v - c0 * n0 - c1 * n1))

            for j in range(i + 2, GROUP):
                wide[j] = eliminate(wide[j])
            m = eliminate(m)
    return m[:, n:] * down


FLAT = {"norm": 0, "cross": 32, "sums": 64, "stats": 96}
HALVED = {"norm": (0, 0), "sums": (0, 32), "held_resid": (0, 64), "cross": (1, 0), "held_dir": (1, 32), "held_sol": (1, 64)}


def slot(half):
    return (half + lax.axis_index("ind")) % CORES


def place(ref, name, lanes):
    start = ref.shape[-1] - 128
    if len(ref.shape) == 2:
        start += FLAT[name]
        return slice(0, RHS), slice(start, start + lanes)
    half, lane = HALVED[name]
    start += lane
    return slot(half), slice(0, RHS), slice(start, start + lanes)


def put(ref, name, value):
    ref[place(ref, name, value.shape[1])] = value


def take(ref, name, lanes=RHS):
    return ref[place(ref, name, lanes)]


def put_panel(ref, value):
    width = ref.shape[-1] - 128
    if len(ref.shape) == 2:
        ref[0:RHS, :width] = value
        ref[0:RHS, width:] = jnp.zeros((RHS, 128), F32)
    else:
        for c in range(2):
            ref[slot(c), :, :width] = value[:, c * width:(c + 1) * width]
            ref[slot(c), :, width:] = jnp.zeros((RHS, 128), F32)


def take_panel(ref):
    width = ref.shape[-1] - 128
    if len(ref.shape) == 2:
        return ref[0:RHS, :width]
    return jnp.concatenate([ref[slot(c), :, :width] for c in range(2)], axis=1)


QUARTERS = 4


def prep_kernel(geno_hbm, rhs_hbm, held_hbm, ridge_ref, codes_ref, pay_ref, rhs_ref, lam_ref, chosen_ref,
                geno_ref, held_ref, sems):
    rows, cols = geno_ref.shape
    chunk = rows // QUARTERS
    rhs_copy = pltpu.make_async_copy(rhs_hbm, rhs_ref, sems.at[QUARTERS])
    rhs_copy.start()
    held_copy = pltpu.make_async_copy(held_hbm, held_ref, sems.at[QUARTERS + 1])
    held_copy.start()
    copies = []
    for q in range(QUARTERS):
        part = pl.ds(q * chunk, chunk)
        copies.append(pltpu.make_async_copy(geno_hbm.at[part, :], geno_ref.at[part, :], sems.at[q]))
        copies[-1].start()
    rhs_copy.wait()
    held_copy.wait()
    rhs = rhs_ref[...]
    pieces = stacked(rhs)
    lam_ref[...] = jnp.full(lam_ref.shape, ridge_ref[0], F32)
    norm = gram(pieces, pieces)
    place = lax.broadcasted_iota(jnp.int32, (1, rows), 1) + lax.axis_index("ind") * rows
    chosen_ref[...] = jnp.concatenate([(place == held_ref[:, k:k + 1]).astype(F32) for k in range(RHS)], axis=0).astype(BF16)
    lhs = jnp.concatenate([pieces, jnp.ones((32, rows), BF16)], axis=0)
    panel_, sums, squares = 0.0, 0.0, 0.0
    for q in range(QUARTERS):
        copies[q].wait()
        centred = (geno_ref[q * chunk:(q + 1) * chunk, :] - 1).astype(F32)
        codes = centred.astype(BF16)
        codes_ref[q * chunk:(q + 1) * chunk, :] = codes
        squares = squares + jnp.sum(centred * centred, axis=0, keepdims=True)
        acc = jnp.dot(lhs[:, q * chunk:(q + 1) * chunk], codes, preferred_element_type=F32)
        panel_ = panel_ + fold(acc[:96])
        sums = sums + acc[96:97]
    put_panel(pay_ref, panel_)
    put(pay_ref, "norm", norm)
    put(pay_ref, "sums", jnp.sum(rhs, axis=1, keepdims=True))
    put(pay_ref, "stats", jnp.concatenate([row[:, i:i + 32] for row in (sums, squares) for i in range(0, cols, 32)], axis=0))


def prep(genotypes, rhs, held, ridge):
    rows, cols = genotypes.shape
    hbm = pl.BlockSpec(memory_space=pltpu.HBM)
    return pl.pallas_call(
        prep_kernel,
        in_specs=[hbm, hbm, hbm, pl.BlockSpec(memory_space=pltpu.SMEM)],
        out_shape=[jax.ShapeDtypeStruct((rows, cols), BF16), jax.ShapeDtypeStruct((RHS, cols + 128), F32),
                   jax.ShapeDtypeStruct((RHS, rows), F32), jax.ShapeDtypeStruct((RHS, 128), F32),
                   jax.ShapeDtypeStruct((RHS, rows), BF16)],
        scratch_shapes=[pltpu.VMEM((rows, cols), jnp.int32), pltpu.VMEM(held.shape, jnp.int32),
                        pltpu.SemaphoreType.DMA((QUARTERS + 2,))],
        compiler_params=PARAMS,
        name="prep",
    )(*[pltpu.with_memory_space_constraint(arg, pltpu.HBM) for arg in (genotypes, rhs, held)], ridge)


def panel_kernel(total, first, last, parts, *refs):
    if first:
        red_ref, codes_ref, u_ref, stat_ref, norm_ref, pp_ref, out_ref = refs
    else:
        red_ref, codes_ref, oldu_ref, stat_in_ref, inv_ref, oldpp_ref, u_ref, norm_ref, pp_ref, beta_ref, out_ref = refs
    cols = codes_ref.shape[1]
    if first:
        stats = take(red_ref, "stats")
        sums, squares = [jnp.concatenate([stats[i:i + 1] for i in range(j, j + cols // 32)], axis=1)
                         for j in (0, cols // 32)]
        mean = sums * (1.0 / total)
        scale = 1.0 / jnp.sqrt(squares * (1.0 / total) - mean * mean + 1e-05)
        stat_ref[0:1, :] = mean
        stat_ref[1:2, :] = scale
    else:
        mean, scale = stat_in_ref[0:1, :], stat_in_ref[1:2, :]
    norm = symmetric(take(red_ref, "norm"))
    u = (take_panel(red_ref) - take(red_ref, "sums", 1) * mean) * scale
    norm_ref[...] = norm
    if first:
        pp = norm
    else:
        beta = small_dot(norm, inv_ref[...])
        u = u + small_dot(beta, oldu_ref[...])
        cross = small_dot(beta, take(red_ref, "cross"))
        pp = norm + (cross + cross.T) + symmetric(small_dot(small_dot(beta, oldpp_ref[...]), beta.T))
        beta_ref[...] = beta
    pp_ref[...] = pp
    u_ref[...] = u
    pieces = stacked(u)
    uu = gram(pieces, pieces)
    packed = jnp.concatenate([uu[4 * i:4 * i + 4] for i in range(8)], axis=1)
    if last:
        for j in range(parts):
            out_ref[j, :, :] = packed
        return
    weight = u * scale
    image = fold(lax.dot_general(stacked(weight), codes_ref[...], NT, preferred_element_type=F32))
    image = image - jnp.sum(weight * mean, axis=1, keepdims=True)
    width = image.shape[1] // parts
    for j in range(parts):
        out_ref[j, 0:RHS, :] = image[:, j * width:(j + 1) * width]
        out_ref[j, RHS:, :] = packed


def unpack(block):
    return jnp.concatenate([block[0:4, 32 * i:32 * i + 32] for i in range(8)], axis=0)


def panel(total, first, last, parts, *args):
    rows, cols = args[1].shape
    small = jax.ShapeDtypeStruct((RHS, RHS), F32)
    outs = [jax.ShapeDtypeStruct((RHS, cols), F32)]
    if first:
        outs.append(jax.ShapeDtypeStruct((8, cols), F32))
    outs += [small, small]
    if not first:
        outs.append(small)
    outs.append(jax.ShapeDtypeStruct((parts, 4 if last else RHS + 4, 256), F32))
    return pl.pallas_call(
        functools.partial(panel_kernel, total, first, last, parts),
        out_shape=outs,
        compiler_params=PARAMS,
        name="panel",
    )(*args)


def solve_kernel(markers, first, *refs):
    if first:
        lam_ref, got_ref, pp_ref, norm_ref, resid_ref, send_ref, alpha_ref, inv_ref, sol_ref, base_ref = refs
    else:
        (lam_ref, got_ref, pp_ref, norm_ref, resid_ref, beta_ref, olddir_ref, oldsol_ref,
         send_ref, alpha_ref, inv_ref, sol_ref, base_ref, dir_ref) = refs
    norm = norm_ref[...]
    parts = got_ref.shape[0]
    got = got_ref[0]
    for j in range(1, parts):
        got = got + got_ref[j]
    eye = (lax.broadcasted_iota(jnp.int32, norm.shape, 0) == lax.broadcasted_iota(jnp.int32, norm.shape, 1)).astype(F32)
    curvature = symmetric(unpack(got[RHS:]) * (1.0 / markers) + lam_ref[:, 0:RHS] * pp_ref[...])
    alpha = left_divide(curvature, norm).T
    inv_ref[...] = left_divide(norm, eye)
    alpha_ref[...] = alpha * (1.0 / markers)
    for j in range(parts):
        send_ref[j, :, :] = got[:RHS]
    resid = resid_ref[...]
    if first:
        direction = resid
    else:
        direction = resid + small_dot(beta_ref[...], olddir_ref[...])
        dir_ref[...] = direction
    move = small_dot(alpha, direction)
    sol_ref[...] = move if first else oldsol_ref[...] + move
    base_ref[...] = resid - lam_ref[:, 0:1] * move


def solve(markers, first, *args):
    long = jax.ShapeDtypeStruct(args[4].shape, F32)
    small = jax.ShapeDtypeStruct((RHS, RHS), F32)
    parts, _, width = args[1].shape
    return pl.pallas_call(
        functools.partial(solve_kernel, markers, first),
        out_shape=[jax.ShapeDtypeStruct((parts, RHS, width), F32), small, small, long, long] + ([] if first else [long]),
        compiler_params=PARAMS,
        name="solve",
    )(*args)


def step_kernel(held_too, *refs):
    if held_too:
        image_ref, alpha_ref, base_ref, dir_ref, codes_ref, sol_ref, chosen_ref, resid_ref, pay_ref = refs
    else:
        image_ref, alpha_ref, base_ref, dir_ref, codes_ref, resid_ref, pay_ref = refs
    image = jnp.concatenate([image_ref[j] for j in range(image_ref.shape[0])], axis=1)
    resid = base_ref[...] - small_dot(alpha_ref[...], image)
    resid_ref[...] = resid
    pieces = stacked(resid)
    dpieces = stacked(dir_ref[...])
    put_panel(pay_ref, fold(jnp.dot(pieces, codes_ref[...], preferred_element_type=F32)))
    put(pay_ref, "norm", gram(pieces, pieces))
    put(pay_ref, "sums", jnp.sum(resid, axis=1, keepdims=True))
    put(pay_ref, "cross", gram(dpieces, pieces))
    if held_too:
        chosen = chosen_ref[...]
        for name, value in (("held_resid", pieces), ("held_dir", dpieces), ("held_sol", stacked(sol_ref[...]))):
            put(pay_ref, name, fold(lax.dot_general(value, chosen, NT, preferred_element_type=F32)))


def step(held_too, *args):
    rows, cols = args[4].shape
    return pl.pallas_call(
        functools.partial(step_kernel, held_too),
        out_shape=[jax.ShapeDtypeStruct((RHS, rows), F32),
                   jax.ShapeDtypeStruct((2, RHS, cols // 2 + 128) if held_too else (RHS, cols + 128), F32)],
        compiler_params=PARAMS,
        name="step",
    )(*args)


def last_kernel(markers, lam_ref, got_ref, pp_ref, norm_ref, beta_ref, resid_ref, olddir_ref, sol_ref, red_ref,
                out_ref, held_ref):
    got = got_ref[0]
    for j in range(1, got_ref.shape[0]):
        got = got + got_ref[j]
    alpha = left_divide(symmetric(unpack(got) * (1.0 / markers) + lam_ref[:, 0:RHS] * pp_ref[...]), norm_ref[...]).T
    beta = beta_ref[...]
    out_ref[...] = sol_ref[...] + small_dot(alpha, resid_ref[...] + small_dot(beta, olddir_ref[...]))
    direction = take(red_ref, "held_resid") + small_dot(beta, take(red_ref, "held_dir"))
    rows = take(red_ref, "held_sol") + small_dot(alpha, direction)
    eye = lax.broadcasted_iota(jnp.int32, rows.shape, 0) == lax.broadcasted_iota(jnp.int32, rows.shape, 1)
    held_ref[...] = jnp.sum(jnp.where(eye, rows, 0.0), axis=0, keepdims=True)


def last_step(markers, *args):
    return pl.pallas_call(
        functools.partial(last_kernel, markers),
        out_shape=[jax.ShapeDtypeStruct(args[5].shape, F32), jax.ShapeDtypeStruct((1, RHS), F32)],
        compiler_params=PARAMS,
        name="last",
    )(*args)


def on_ind(move):
    pairs = []
    for y in range(YSIZE):
        for x in range(XSIZE):
            for c in range(CORES):
                ty, tx, tc = move(y, x, c)
                pairs.append(((y * XSIZE + x) * CORES + c, (ty * XSIZE + tx) * CORES + tc))
    return pairs


def swap_cores(value):
    return lax.ppermute(value, "ind", on_ind(lambda y, x, c: (y, x, 1 - c)))


def sum_chips(value):
    for along in ("x", "y"):
        moved = {}
        for d in (1, 3, 2):
            if along == "x":
                pairs = on_ind(lambda y, x, c, d=d: (y, (x + d) % XSIZE, c))
            else:
                pairs = on_ind(lambda y, x, c, d=d: ((y + d) % YSIZE, x, c))
            moved[d] = lax.ppermute(value, "ind", pairs)
        value = (moved[3] + moved[1]) + (moved[2] + value)
    return value


def sum_ind(value):
    if value.ndim == 2:
        return sum_chips(value + swap_cores(value))
    mine = sum_chips(value[0] + swap_cores(value[1]))
    return jnp.stack([mine, swap_cores(mine)])


def exchange(value):
    return lax.all_to_all(value, "snp", 0, 0)


def shards(genotypes, targets, ridge, held_out):
    rows, cols = genotypes.shape
    parts = lax.axis_size("snp")
    total = rows * lax.axis_size("ind")
    markers = cols * parts

    codes, pay, resid, lam, chosen = prep(genotypes, targets.T, held_out[None, :], ridge)
    for k in range(ITERS):
        first, last = k == 0, k == ITERS - 1
        red = sum_ind(pay)
        if first:
            u, stat, norm, pp, out = panel(total, True, False, parts, red, codes)
        else:
            u, norm, pp, beta, out = panel(total, False, last, parts, red, codes, u, stat, inv, pp)
        got = exchange(out)
        if last:
            break
        args = [lam, got, pp, norm, resid]
        if first:
            direction = resid
            send, alpha, inv, sol, base = solve(markers, True, *args)
        else:
            send, alpha, inv, sol, base, direction = solve(markers, False, *args, beta, direction, sol)
        image = exchange(send)
        held_too = k == ITERS - 2
        resid, pay = step(held_too, image, alpha, base, direction, codes, *([sol, chosen] if held_too else []))
    sol, held = last_step(markers, lam, got, pp, norm, beta, resid, direction, sol, red)
    return sol.T, held[0]


def solution(mesh):
    return jax.shard_map(
        shards,
        mesh=mesh,
        in_specs=(P("ind", "snp"), P("ind", None), P(), P()),
        out_specs=(P("ind", None), P()),
        check_vma=False,
    )
```

time: 209 us -> 194 us (0.928); the launches traced: 206 us -> 193 us
  waiting for transfers between devices: 68.3 us -> 41.2 us
  blocking collectives: 72.3 us -> 97.7 us
  starting transfers between devices: 40.3 us -> 33 us
  Pallas kernels: 22.7 us -> 19.9 us
    all_to_all x5 -> x7, blocking collectives: 72.3 us -> 97.7 us  [exchange(): return lax.all_to_all(value, 'snp', 0, 0)]
    all_to_all x2 -> x0, waiting for transfers between devices: 24.6 us -> none  [exchange(): return lax.all_to_all(value, 'snp', 0, 0)]
    all_to_all x2 -> x0, starting transfers between devices: 12.1 us -> none  [exchange(): return lax.all_to_all(value, 'snp', 0, 0)]
    ppermute x24, starting transfers between devices: 27.5 us -> 32.5 us  [sum_chips(): moved[d] = lax.ppermute(value, 'ind', pairs)]
    ppermute x8 -> x5, waiting for transfers between devices: 9.77 us -> 6.23 us  [swap_cores(): return lax.ppermute(value, 'ind', on_ind(lambda y, x, c: (y, x, 1 - c)))]
    pallas_call x5, Pallas kernels: 14.1 us -> 12 us  [the longest x3 6.16 us: solve(): pl.pallas_call(functools.partial(solve_kernel, markers, first), out_shape...]
  transfers between devices with their start and end apart: 34 -> 29, of which waited for: 30 -> 25; matrix products, arithmetic and copies ran while one was open for 0% -> 0% of each run, Pallas kernels for 0% -> 0%
where the time goes in v3:
time: 194 us; the launch traced here: 193 us
  blocking collectives  97.7 us (50%)
  waiting for transfers between devices  41.2 us (21%)
  starting transfers between devices  33 us (17%)
  Pallas kernels  19.9 us (10%)
    all_to_all x7, blocking collectives, exchange(): return lax.all_to_all(value, 'snp', 0, 0)  97.7 us
    ppermute x24, waiting for transfers between devices, sum_chips(): moved[d] = lax.ppermute(value, 'ind', pairs)  35 us
    ppermute x24, starting transfers between devices, sum_chips(): moved[d] = lax.ppermute(value, 'ind', pairs)  32.5 us
    ppermute x5, waiting for transfers between devices, swap_cores(): return lax.ppermute(value, 'ind', on_ind(lambda y, x, c: (y, x, 1 - c)))  6.23 us
    pallas_call x3, Pallas kernels, solve(): pl.pallas_call(functools.partial(solve_kernel, markers, first), out_shape...  6.16 us
    pallas_call x4, Pallas kernels, panel(): pl.pallas_call(functools.partial(panel_kernel, total, first, last, parts)...  4.55 us
  transfers between devices with their start and end apart: 29, of which 25 were waited for; matrix products, arithmetic and copies ran while one was open for 0% of the time, Pallas kernels for 0%

profile of v3, /device:TPU:22, one launch (start us, length us, event | category | flops | bytes accessed | tf_op | source)
XLA Modules:
  0.0 193.4 jit_solution(8279840036430032668)
XLA Ops:
  1.3 3.1 %prep.1 = (bf16[2048,512]{1,0:T(8,128)(2,1)S(1)}, f32[32,640]{1,0:T(8,128)S(1)}, f32[32,2048]{1,0:T(8,128)S(1)}, f32[32,128]{1,0:T(8,128)S(1)}, bf16[32,2048]{1,0:T(8,128)(2,1)S(1)}) custom-call(s32[2048,512]{1,0:T(8,128)} %geno_hbm.1, f32[32,2048]{1,0:T(8,128)} %bitcast.10, s32[1,32]{1,0:T(1,128)} %bitcast.13, f32[1]{0:T(128)S(6)} %copy.6.ridge_ref), custom_call_target="tpu_custom_call" | custom-call | tf_op jit(solution)/shard_map/prep/pallas_call | solution.py:172
  4.5 1.3 collective-permute-done
  5.8 1.5 collective-permute-start.3
  7.3 2.1 %collective-permute-start.2 = (f32[32,640]{1,0:T(8,128)S(1)}, f32[32,640]{1,0:T(8,128)S(1)}, u32[]{:S(2)}, u32[]{:S(2)}) collective-permute-start(f32[32,640]{1,0:T(8,128)S(1)} %add.84), channel_id=1, source_target_pairs={{0,16},{8,24},{16,32},{24,40},{32,48},{40,56},{48,0},{56,8},{64,80... | collective-permute-start | bytes 245768 | tf_op jit(solution)/shard_map/ppermute | solution.py:369
  9.4 2.8 %collective-permute-done.3 = f32[32,640]{1,0:T(8,128)S(1)} collective-permute-done((f32[32,640]{1,0:T(8,128)S(1)}, f32[32,640]{1,0:T(8,128)S(1)}, u32[]{:S(2)}, u32[]{:S(2)}) %collective-permute-start.3) | collective-permute-done | bytes 81952 | tf_op jit(solution)/shard_map/ppermute | solution.py:369
  12.2 2.8 %collective-permute-done.1 = f32[32,640]{1,0:T(8,128)S(1)} collective-permute-done((f32[32,640]{1,0:T(8,128)S(1)}, f32[32,640]{1,0:T(8,128)S(1)}, u32[]{:S(2)}, u32[]{:S(2)}) %collective-permute-start.1) | collective-permute-done | bytes 81952 | tf_op jit(solution)/shard_map/ppermute | solution.py:369
  15.4 2.2 %collective-permute-start.5 = (f32[32,640]{1,0:T(8,128)S(1)}, f32[32,640]{1,0:T(8,128)S(1)}, u32[]{:S(2)}, u32[]{:S(2)}) collective-permute-start(f32[32,640]{1,0:T(8,128)S(1)} %add_add_fusion.5), channel_id=1, source_target_pairs={{0,64},{8,72},{16,80},{24,88},{32,96},{40,104},{48,112},{56,120},{... | collective-permute-start | bytes 245768 | tf_op jit(solution)/shard_map/ppermute | solution.py:369
  17.9 3.3 %collective-permute-done.6 = f32[32,640]{1,0:T(8,128)S(1)} collective-permute-done((f32[32,640]{1,0:T(8,128)S(1)}, f32[32,640]{1,0:T(8,128)S(1)}, u32[]{:S(2)}, u32[]{:S(2)}) %collective-permute-start.6) | collective-permute-done | bytes 81952 | tf_op jit(solution)/shard_map/ppermute | solution.py:369
  23.2 19.5 %all_to_all.35.refs_1_ = f32[8,36,256]{2,1,0:T(8,128)S(1)} all-to-all(f32[8,36,256]{2,1,0:T(8,128)S(1)} %get-tuple-element.54), channel_id=1, replica_groups=mesh['ind'=32,'snp'=8] {'snp'}, dimensions={0} | all-to-all | bytes 589824 | tf_op jit(solution)/shard_map/all_to_all | solution.py:382
  42.6 2.0 %solve.3 = (f32[8,32,256]{2,1,0:T(8,128)S(1)}, f32[32,32]{1,0:T(8,128)S(1)}, f32[32,32]{1,0:T(8,128)S(1)}, f32[32,2048]{1,0:T(8,128)S(1)}, f32[32,2048]{1,0:T(8,128)S(1)}) custom-call(f32[32,128]{1,0:T(8,128)S(1)} %get-tuple-element.51.refs_0_.lam_ref, f32[8,36,256]{2,1,0:T(8,128)S(1)} %all_to_all.35.refs_1_, ...), custom_call_target="tpu_custom_call" | custom-call | tf_op jit(solution)/shard_map/solve/pallas_call | solution.py:285
  44.6 12.9 %all_to_all.36.refs_0_ = f32[8,32,256]{2,1,0:T(8,128)S(1)} all-to-all(f32[8,32,256]{2,1,0:T(8,128)S(1)} %get-tuple-element.58), channel_id=1, replica_groups=mesh['ind'=32,'snp'=8] {'snp'}, dimensions={0} | all-to-all | bytes 524288 | tf_op jit(solution)/shard_map/all_to_all | solution.py:382
  58.7 1.3 collective-permute-done.7
  60.0 1.3 collective-permute-start.10
  61.2 1.3 collective-permute-start.9
  63.3 3.1 %collective-permute-done.10 = f32[32,640]{1,0:T(8,128)S(1)} collective-permute-done((f32[32,640]{1,0:T(8,128)S(1)}, f32[32,640]{1,0:T(8,128)S(1)}, u32[]{:S(2)}, u32[]{:S(2)}) %collective-permute-start.10) | collective-permute-done | bytes 81952 | tf_op jit(solution)/shard_map/ppermute | solution.py:369
  66.4 1.7 collective-permute-done.8
  68.2 1.9 collective-permute-start.13
  70.1 1.4 collective-permute-start.12
  71.5 1.2 collective-permute-start.11
  72.6 1.7 collective-permute-done.13
  74.3 1.3 collective-permute-done.12
  75.9 1.3 panel.5
  77.2 15.5 %all_to_all.37.refs_1_ = f32[8,36,256]{2,1,0:T(8,128)S(1)} all-to-all(f32[8,36,256]{2,1,0:T(8,128)S(1)} %get-tuple-element.65), channel_id=1, replica_groups=mesh['ind'=32,'snp'=8] {'snp'}, dimensions={0} | all-to-all | bytes 589824 | tf_op jit(solution)/shard_map/all_to_all | solution.py:382
  92.7 2.1 %solve.4 = (f32[8,32,256]{2,1,0:T(8,128)S(1)}, f32[32,32]{1,0:T(8,128)S(1)}, f32[32,32]{1,0:T(8,128)S(1)}, f32[32,2048]{1,0:T(8,128)S(1)}, f32[32,2048]{1,0:T(8,128)S(1)}, /*index=5*/f32[32,2048]{1,0:T(8,128)S(1)}) custom-call(f32[32,128]{1,0:T(8,128)S(1)} %get-tuple-element.51.refs_0_.lam_ref, f32[8,36,256]{2,1,0:T(8,128)S(1)} %all_to_all.37.refs_1_, ...), custom_call_target="tpu_custom_call" | custom-call | tf_op jit(solution)/shard_map/solve/pallas_call | solution.py:285
  94.7 13.0 %all_to_all.38.refs_0_ = f32[8,32,256]{2,1,0:T(8,128)S(1)} all-to-all(f32[8,32,256]{2,1,0:T(8,128)S(1)} %get-tuple-element.71), channel_id=1, replica_groups=mesh['ind'=32,'snp'=8] {'snp'}, dimensions={0} | all-to-all | bytes 524288 | tf_op jit(solution)/shard_map/all_to_all | solution.py:382
  109.0 1.3 collective-permute-done.14
  110.2 1.5 collective-permute-start.17
  113.7 2.9 %collective-permute-done.17 = f32[32,640]{1,0:T(8,128)S(1)} collective-permute-done((f32[32,640]{1,0:T(8,128)S(1)}, f32[32,640]{1,0:T(8,128)S(1)}, u32[]{:S(2)}, u32[]{:S(2)}) %collective-permute-start.17) | collective-permute-done | bytes 81952 | tf_op jit(solution)/shard_map/ppermute | solution.py:369
  116.7 1.8 collective-permute-done.15
  118.4 1.9 collective-permute-start.20
  120.3 2.2 %collective-permute-start.19 = (f32[32,640]{1,0:T(8,128)S(1)}, f32[32,640]{1,0:T(8,128)S(1)}, u32[]{:S(2)}, u32[]{:S(2)}) collective-permute-start(f32[32,640]{1,0:T(8,128)S(1)} %add_add_fusion.1), channel_id=1, source_target_pairs={{0,64},{8,72},{16,80},{24,88},{32,96},{40,104},{48,112},{56,120},{... | collective-permute-start | bytes 245768 | tf_op jit(solution)/shard_map/ppermute | solution.py:369
  122.5 2.2 %collective-permute-done.20 = f32[32,640]{1,0:T(8,128)S(1)} collective-permute-done((f32[32,640]{1,0:T(8,128)S(1)}, f32[32,640]{1,0:T(8,128)S(1)}, u32[]{:S(2)}, u32[]{:S(2)}) %collective-permute-start.20) | collective-permute-done | bytes 81952 | tf_op jit(solution)/shard_map/ppermute | solution.py:369
  125.5 1.5 collective-permute-done.18
  127.0 1.3 panel.6
  128.3 13.6 %all_to_all.39.refs_1_ = f32[8,36,256]{2,1,0:T(8,128)S(1)} all-to-all(f32[8,36,256]{2,1,0:T(8,128)S(1)} %get-tuple-element.78), channel_id=1, replica_groups=mesh['ind'=32,'snp'=8] {'snp'}, dimensions={0} | all-to-all | bytes 589824 | tf_op jit(solution)/shard_map/all_to_all | solution.py:382
  141.8 2.1 %solve.5 = (f32[8,32,256]{2,1,0:T(8,128)S(1)}, f32[32,32]{1,0:T(8,128)S(1)}, f32[32,32]{1,0:T(8,128)S(1)}, f32[32,2048]{1,0:T(8,128)S(1)}, f32[32,2048]{1,0:T(8,128)S(1)}, /*index=5*/f32[32,2048]{1,0:T(8,128)S(1)}) custom-call(f32[32,128]{1,0:T(8,128)S(1)} %get-tuple-element.51.refs_0_.lam_ref, f32[8,36,256]{2,1,0:T(8,128)S(1)} %all_to_all.39.refs_1_, ...), custom_call_target="tpu_custom_call" | custom-call | tf_op jit(solution)/shard_map/solve/pallas_call | solution.py:285
  143.9 12.9 %all_to_all.40.refs_0_ = f32[8,32,256]{2,1,0:T(8,128)S(1)} all-to-all(f32[8,32,256]{2,1,0:T(8,128)S(1)} %get-tuple-element.84), channel_id=1, replica_groups=mesh['ind'=32,'snp'=8] {'snp'}, dimensions={0} | all-to-all | bytes 524288 | tf_op jit(solution)/shard_map/all_to_all | solution.py:382
  156.8 1.2 step.5
  158.1 1.2 collective-permute-done.21
  159.4 3.6 %collective-permute-start.24 = (f32[32,384]{1,0:T(8,128)S(1)}, f32[32,384]{1,0:T(8,128)S(1)}, u32[]{:S(2)}, u32[]{:S(2)}) collective-permute-start(f32[32,384]{1,0:T(8,128)S(1)} %bitcast_add_fusion), channel_id=1, source_target_pairs={{0,32},{8,40},{16,48},{24,56},{32,0},{40,8},{48,16},{56,24},{64,96... | collective-permute-start | bytes 147464 | tf_op jit(solution)/shard_map/ppermute | solution.py:369
  163.4 1.7 collective-permute-start.22
  165.3 1.8 collective-permute-done.23
  167.1 1.6 collective-permute-done.22
  169.6 4.2 %collective-permute-start.26 = (f32[32,384]{1,0:T(8,128)S(1)}, f32[32,384]{1,0:T(8,128)S(1)}, u32[]{:S(2)}, u32[]{:S(2)}) collective-permute-start(f32[32,384]{1,0:T(8,128)S(1)} %add_add_fusion.7), channel_id=1, source_target_pairs={{0,64},{8,72},{16,80},{24,88},{32,96},{40,104},{48,112},{56,120},{... | collective-permute-start | bytes 147464 | tf_op jit(solution)/shard_map/ppermute | solution.py:369
  175.5 2.3 %collective-permute-done.25 = f32[32,384]{1,0:T(8,128)S(1)} collective-permute-done((f32[32,384]{1,0:T(8,128)S(1)}, f32[32,384]{1,0:T(8,128)S(1)}, u32[]{:S(2)}, u32[]{:S(2)}) %collective-permute-start.25) | collective-permute-done | bytes 49184 | tf_op jit(solution)/shard_map/ppermute | solution.py:369
  178.0 1.2 collective-permute-done.28
  180.3 10.4 %all_to_all.41.got_ref = f32[8,4,256]{2,1,0:T(4,128)S(1)} all-to-all(f32[8,4,256]{2,1,0:T(4,128)S(1)} %get-tuple-element.93), channel_id=1, replica_groups=mesh['ind'=32,'snp'=8] {'snp'}, dimensions={0} | all-to-all | bytes 65536 | tf_op jit(solution)/shard_map/all_to_all | solution.py:382
  190.7 2.7 %last.1 = (f32[32,2048]{1,0:T(8,128)}, f32[1,32]{1,0:T(1,128)}) custom-call(f32[32,128]{1,0:T(8,128)S(1)} %get-tuple-element.51.refs_0_.lam_ref, f32[8,4,256]{2,1,0:T(4,128)S(1)} %all_to_all.41.got_ref, f32[32,32]{1,0:T(8,128)S(1)} %get-tuple-element.94.pp_ref, f32[32,32]{1,0:T(8,128)S(1)} %get-tuple-element.95.norm_ref, ...), custom_call_target="tpu_custom_call" | custom-call | tf_op jit(solution)/shard_map/last/pallas_call | solution.py:339
  (43 shorter events, 13.7 us)
Async XLA Ops:
  4.4 1.4 collective-permute-start
  5.8 6.4 %collective-permute-start.3 = (f32[32,640]{1,0:T(8,128)S(1)}, f32[32,640]{1,0:T(8,128)S(1)}, u32[]{:S(2)}, u32[]{:S(2)}) collective-permute-start(f32[32,640]{1,0:T(8,128)S(1)} %add.84), channel_id=1, source_target_pairs={{0,32},{8,40},{16,48},{24,56},{32,0},{40,8},{48,16},{56,24},{64,96... | collective-permute-start | bytes 245768 | tf_op jit(solution)/shard_map/ppermute | solution.py:369
  7.3 4.9 %collective-permute-start.2 = (f32[32,640]{1,0:T(8,128)S(1)}, f32[32,640]{1,0:T(8,128)S(1)}, u32[]{:S(2)}, u32[]{:S(2)}) collective-permute-start(f32[32,640]{1,0:T(8,128)S(1)} %add.84), channel_id=1, source_target_pairs={{0,16},{8,24},{16,32},{24,40},{32,48},{40,56},{48,0},{56,8},{64,80... | collective-permute-start | bytes 245768 | tf_op jit(solution)/shard_map/ppermute | solution.py:369
  9.4 5.7 %collective-permute-start.1 = (f32[32,640]{1,0:T(8,128)S(1)}, f32[32,640]{1,0:T(8,128)S(1)}, u32[]{:S(2)}, u32[]{:S(2)}) collective-permute-start(f32[32,640]{1,0:T(8,128)S(1)} %add.84), channel_id=1, source_target_pairs={{0,48},{8,56},{16,0},{24,8},{32,16},{40,24},{48,32},{56,40},{64,11... | collective-permute-start | bytes 245768 | tf_op jit(solution)/shard_map/ppermute | solution.py:369
  15.0 6.1 %collective-permute-start.6 = (f32[32,640]{1,0:T(8,128)S(1)}, f32[32,640]{1,0:T(8,128)S(1)}, u32[]{:S(2)}, u32[]{:S(2)}) collective-permute-start(f32[32,640]{1,0:T(8,128)S(1)} %add_add_fusion.5), channel_id=1, source_target_pairs={{0,128},{8,136},{16,144},{24,152},{32,160},{40,168},{48,176},{56,1... | collective-permute-start | bytes 245768 | tf_op jit(solution)/shard_map/ppermute | solution.py:369
  15.4 5.7 %collective-permute-start.5 = (f32[32,640]{1,0:T(8,128)S(1)}, f32[32,640]{1,0:T(8,128)S(1)}, u32[]{:S(2)}, u32[]{:S(2)}) collective-permute-start(f32[32,640]{1,0:T(8,128)S(1)} %add_add_fusion.5), channel_id=1, source_target_pairs={{0,64},{8,72},{16,80},{24,88},{32,96},{40,104},{48,112},{56,120},{... | collective-permute-start | bytes 245768 | tf_op jit(solution)/shard_map/ppermute | solution.py:369
  17.6 4.6 %collective-permute-start.4 = (f32[32,640]{1,0:T(8,128)S(1)}, f32[32,640]{1,0:T(8,128)S(1)}, u32[]{:S(2)}, u32[]{:S(2)}) collective-permute-start(f32[32,640]{1,0:T(8,128)S(1)} %add_add_fusion.5), channel_id=1, source_target_pairs={{0,192},{8,200},{16,208},{24,216},{32,224},{40,232},{48,240},{56,2... | collective-permute-start | bytes 245768 | tf_op jit(solution)/shard_map/ppermute | solution.py:369
  58.6 1.4 collective-permute-start.7
  60.0 6.4 %collective-permute-start.10 = (f32[32,640]{1,0:T(8,128)S(1)}, f32[32,640]{1,0:T(8,128)S(1)}, u32[]{:S(2)}, u32[]{:S(2)}) collective-permute-start(f32[32,640]{1,0:T(8,128)S(1)} %add.91), channel_id=1, source_target_pairs={{0,32},{8,40},{16,48},{24,56},{32,0},{40,8},{48,16},{56,24},{64,96... | collective-permute-start | bytes 245768 | tf_op jit(solution)/shard_map/ppermute | solution.py:369
  61.2 5.2 %collective-permute-start.9 = (f32[32,640]{1,0:T(8,128)S(1)}, f32[32,640]{1,0:T(8,128)S(1)}, u32[]{:S(2)}, u32[]{:S(2)}) collective-permute-start(f32[32,640]{1,0:T(8,128)S(1)} %add.91), channel_id=1, source_target_pairs={{0,16},{8,24},{16,32},{24,40},{32,48},{40,56},{48,0},{56,8},{64,80... | collective-permute-start | bytes 245768 | tf_op jit(solution)/shard_map/ppermute | solution.py:369
  62.5 5.7 %collective-permute-start.8 = (f32[32,640]{1,0:T(8,128)S(1)}, f32[32,640]{1,0:T(8,128)S(1)}, u32[]{:S(2)}, u32[]{:S(2)}) collective-permute-start(f32[32,640]{1,0:T(8,128)S(1)} %add.91), channel_id=1, source_target_pairs={{0,48},{8,56},{16,0},{24,8},{32,16},{40,24},{48,32},{56,40},{64,11... | collective-permute-start | bytes 245768 | tf_op jit(solution)/shard_map/ppermute | solution.py:369
  68.2 6.1 %collective-permute-start.13 = (f32[32,640]{1,0:T(8,128)S(1)}, f32[32,640]{1,0:T(8,128)S(1)}, u32[]{:S(2)}, u32[]{:S(2)}) collective-permute-start(f32[32,640]{1,0:T(8,128)S(1)} %add_add_fusion.3), channel_id=1, source_target_pairs={{0,128},{8,136},{16,144},{24,152},{32,160},{40,168},{48,176},{56,1... | collective-permute-start | bytes 245768 | tf_op jit(solution)/shard_map/ppermute | solution.py:369
  70.1 5.5 %collective-permute-start.12 = (f32[32,640]{1,0:T(8,128)S(1)}, f32[32,640]{1,0:T(8,128)S(1)}, u32[]{:S(2)}, u32[]{:S(2)}) collective-permute-start(f32[32,640]{1,0:T(8,128)S(1)} %add_add_fusion.3), channel_id=1, source_target_pairs={{0,64},{8,72},{16,80},{24,88},{32,96},{40,104},{48,112},{56,120},{... | collective-permute-start | bytes 245768 | tf_op jit(solution)/shard_map/ppermute | solution.py:369
  71.5 4.4 %collective-permute-start.11 = (f32[32,640]{1,0:T(8,128)S(1)}, f32[32,640]{1,0:T(8,128)S(1)}, u32[]{:S(2)}, u32[]{:S(2)}) collective-permute-start(f32[32,640]{1,0:T(8,128)S(1)} %add_add_fusion.3), channel_id=1, source_target_pairs={{0,192},{8,200},{16,208},{24,216},{32,224},{40,232},{48,240},{56,2... | collective-permute-start | bytes 245768 | tf_op jit(solution)/shard_map/ppermute | solution.py:369
  108.9 1.4 collective-permute-start.14
  110.2 6.4 %collective-permute-start.17 = (f32[32,640]{1,0:T(8,128)S(1)}, f32[32,640]{1,0:T(8,128)S(1)}, u32[]{:S(2)}, u32[]{:S(2)}) collective-permute-start(f32[32,640]{1,0:T(8,128)S(1)} %add.98), channel_id=1, source_target_pairs={{0,32},{8,40},{16,48},{24,56},{32,0},{40,8},{48,16},{56,24},{64,96... | collective-permute-start | bytes 245768 | tf_op jit(solution)/shard_map/ppermute | solution.py:369
  111.7 5.0 %collective-permute-start.16 = (f32[32,640]{1,0:T(8,128)S(1)}, f32[32,640]{1,0:T(8,128)S(1)}, u32[]{:S(2)}, u32[]{:S(2)}) collective-permute-start(f32[32,640]{1,0:T(8,128)S(1)} %add.98), channel_id=1, source_target_pairs={{0,16},{8,24},{16,32},{24,40},{32,48},{40,56},{48,0},{56,8},{64,80... | collective-permute-start | bytes 245768 | tf_op jit(solution)/shard_map/ppermute | solution.py:369
  112.8 5.7 %collective-permute-start.15 = (f32[32,640]{1,0:T(8,128)S(1)}, f32[32,640]{1,0:T(8,128)S(1)}, u32[]{:S(2)}, u32[]{:S(2)}) collective-permute-start(f32[32,640]{1,0:T(8,128)S(1)} %add.98), channel_id=1, source_target_pairs={{0,48},{8,56},{16,0},{24,8},{32,16},{40,24},{48,32},{56,40},{64,11... | collective-permute-start | bytes 245768 | tf_op jit(solution)/shard_map/ppermute | solution.py:369
  118.4 6.3 %collective-permute-start.20 = (f32[32,640]{1,0:T(8,128)S(1)}, f32[32,640]{1,0:T(8,128)S(1)}, u32[]{:S(2)}, u32[]{:S(2)}) collective-permute-start(f32[32,640]{1,0:T(8,128)S(1)} %add_add_fusion.1), channel_id=1, source_target_pairs={{0,128},{8,136},{16,144},{24,152},{32,160},{40,168},{48,176},{56,1... | collective-permute-start | bytes 245768 | tf_op jit(solution)/shard_map/ppermute | solution.py:369
  120.3 5.2 %collective-permute-start.19 = (f32[32,640]{1,0:T(8,128)S(1)}, f32[32,640]{1,0:T(8,128)S(1)}, u32[]{:S(2)}, u32[]{:S(2)}) collective-permute-start(f32[32,640]{1,0:T(8,128)S(1)} %add_add_fusion.1), channel_id=1, source_target_pairs={{0,64},{8,72},{16,80},{24,88},{32,96},{40,104},{48,112},{56,120},{... | collective-permute-start | bytes 245768 | tf_op jit(solution)/shard_map/ppermute | solution.py:369
  122.5 4.4 %collective-permute-start.18 = (f32[32,640]{1,0:T(8,128)S(1)}, f32[32,640]{1,0:T(8,128)S(1)}, u32[]{:S(2)}, u32[]{:S(2)}) collective-permute-start(f32[32,640]{1,0:T(8,128)S(1)} %add_add_fusion.1), channel_id=1, source_target_pairs={{0,192},{8,200},{16,208},{24,216},{32,224},{40,232},{48,240},{56,2... | collective-permute-start | bytes 245768 | tf_op jit(solution)/shard_map/ppermute | solution.py:369
  158.0 1.3 collective-permute-start.21
  159.4 5.9 %collective-permute-start.24 = (f32[32,384]{1,0:T(8,128)S(1)}, f32[32,384]{1,0:T(8,128)S(1)}, u32[]{:S(2)}, u32[]{:S(2)}) collective-permute-start(f32[32,384]{1,0:T(8,128)S(1)} %bitcast_add_fusion), channel_id=1, source_target_pairs={{0,32},{8,40},{16,48},{24,56},{32,0},{40,8},{48,16},{56,24},{64,96... | collective-permute-start | bytes 147464 | tf_op jit(solution)/shard_map/ppermute | solution.py:369
  163.0 4.1 %collective-permute-start.23 = (f32[32,384]{1,0:T(8,128)S(1)}, f32[32,384]{1,0:T(8,128)S(1)}, u32[]{:S(2)}, u32[]{:S(2)}) collective-permute-start(f32[32,384]{1,0:T(8,128)S(1)} %bitcast_add_fusion), channel_id=1, source_target_pairs={{0,16},{8,24},{16,32},{24,40},{32,48},{40,56},{48,0},{56,8},{64,80... | collective-permute-start | bytes 147464 | tf_op jit(solution)/shard_map/ppermute | solution.py:369
  163.4 5.3 %collective-permute-start.22 = (f32[32,384]{1,0:T(8,128)S(1)}, f32[32,384]{1,0:T(8,128)S(1)}, u32[]{:S(2)}, u32[]{:S(2)}) collective-permute-start(f32[32,384]{1,0:T(8,128)S(1)} %bitcast_add_fusion), channel_id=1, source_target_pairs={{0,48},{8,56},{16,0},{24,8},{32,16},{40,24},{48,32},{56,40},{64,11... | collective-permute-start | bytes 147464 | tf_op jit(solution)/shard_map/ppermute | solution.py:369
  168.7 5.7 %collective-permute-start.27 = (f32[32,384]{1,0:T(8,128)S(1)}, f32[32,384]{1,0:T(8,128)S(1)}, u32[]{:S(2)}, u32[]{:S(2)}) collective-permute-start(f32[32,384]{1,0:T(8,128)S(1)} %add_add_fusion.7), channel_id=1, source_target_pairs={{0,128},{8,136},{16,144},{24,152},{32,160},{40,168},{48,176},{56,1... | collective-permute-start | bytes 147464 | tf_op jit(solution)/shard_map/ppermute | solution.py:369
  169.6 5.9 %collective-permute-start.26 = (f32[32,384]{1,0:T(8,128)S(1)}, f32[32,384]{1,0:T(8,128)S(1)}, u32[]{:S(2)}, u32[]{:S(2)}) collective-permute-start(f32[32,384]{1,0:T(8,128)S(1)} %add_add_fusion.7), channel_id=1, source_target_pairs={{0,64},{8,72},{16,80},{24,88},{32,96},{40,104},{48,112},{56,120},{... | collective-permute-start | bytes 147464 | tf_op jit(solution)/shard_map/ppermute | solution.py:369
  173.8 4.1 %collective-permute-start.25 = (f32[32,384]{1,0:T(8,128)S(1)}, f32[32,384]{1,0:T(8,128)S(1)}, u32[]{:S(2)}, u32[]{:S(2)}) collective-permute-start(f32[32,384]{1,0:T(8,128)S(1)} %add_add_fusion.7), channel_id=1, source_target_pairs={{0,192},{8,200},{16,208},{24,216},{32,224},{40,232},{48,240},{56,2... | collective-permute-start | bytes 147464 | tf_op jit(solution)/shard_map/ppermute | solution.py:369
  177.9 1.3 collective-permute-start.28

commit v4 on v3

--- a/solution.py
+++ b/solution.py
@@ -81,48 +81,27 @@
     return m[:, n:] * down
 
 
-FLAT = {"norm": 0, "cross": 32, "sums": 64, "stats": 96}
-HALVED = {"norm": (0, 0), "sums": (0, 32), "held_resid": (0, 64), "cross": (1, 0), "held_dir": (1, 32), "held_sol": (1, 64)}
-
-
-def slot(half):
-    return (half + lax.axis_index("ind")) % CORES
-
-
-def place(ref, name, lanes):
-    start = ref.shape[-1] - 128
-    if len(ref.shape) == 2:
-        start += FLAT[name]
-        return slice(0, RHS), slice(start, start + lanes)
-    half, lane = HALVED[name]
-    start += lane
-    return slot(half), slice(0, RHS), slice(start, start + lanes)
+SIDE = {"norm": 0, "held": 32, "sums": 64, "cross": 96, "stats": 96}
 
 
 def put(ref, name, value):
-    ref[place(ref, name, value.shape[1])] = value
+    lane = ref.shape[1] - 128 + SIDE[name]
+    ref[:, lane:lane + value.shape[1]] = value
 
 
 def take(ref, name, lanes=RHS):
-    return ref[place(ref, name, lanes)]
+    lane = ref.shape[1] - 128 + SIDE[name]
+    return ref[:, lane:lane + lanes]
 
 
 def put_panel(ref, value):
-    width = ref.shape[-1] - 128
-    if len(ref.shape) == 2:
-        ref[0:RHS, :width] = value
-        ref[0:RHS, width:] = jnp.zeros((RHS, 128), F32)
-    else:
-        for c in range(2):
-            ref[slot(c), :, :width] = value[:, c * width:(c + 1) * width]
-            ref[slot(c), :, width:] = jnp.zeros((RHS, 128), F32)
-
-
-def take_panel(ref):
-    width = ref.shape[-1] - 128
-    if len(ref.shape) == 2:
-        return ref[0:RHS, :width]
-    return jnp.concatenate([ref[slot(c), :, :width] for c in range(2)], axis=1)
+    cols = value.shape[1]
+    ref[:, :cols] = value
+    ref[:, cols:] = jnp.zeros((RHS, ref.shape[1] - cols), F32)
+
+
+def rows_at(pieces, chosen):
+    return fold(lax.dot_general(pieces, chosen, NT, preferred_element_type=F32))
 
 
 QUARTERS = 4
@@ -163,6 +142,7 @@
     put_panel(pay_ref, panel_)
     put(pay_ref, "norm", norm)
     put(pay_ref, "sums", jnp.sum(rhs, axis=1, keepdims=True))
+    put(pay_ref, "held", rows_at(pieces, chosen_ref[...]))
     put(pay_ref, "stats", jnp.concatenate([row[:, i:i + 32] for row in (sums, squares) for i in range(0, cols, 32)], axis=0))
 
 
@@ -184,9 +164,11 @@
 
 def panel_kernel(total, first, last, parts, *refs):
     if first:
-        red_ref, codes_ref, u_ref, stat_ref, norm_ref, pp_ref, out_ref = refs
-    else:
-        red_ref, codes_ref, oldu_ref, stat_in_ref, inv_ref, oldpp_ref, u_ref, norm_ref, pp_ref, beta_ref, out_ref = refs
+        red_ref, codes_ref, u_ref, stat_ref, norm_ref, pp_ref, heldp_ref, out_ref = refs
+    else:
+        red_ref, codes_ref, oldu_ref, stat_in_ref, inv_ref, oldpp_ref, oldheldp_ref = refs[:7]
+        norm_ref, pp_ref, heldp_ref, beta_ref, out_ref = refs[-5:]
+        u_ref = None if last else refs[7]
     cols = codes_ref.shape[1]
     if first:
         stats = take(red_ref, "stats")
@@ -199,18 +181,22 @@
     else:
         mean, scale = stat_in_ref[0:1, :], stat_in_ref[1:2, :]
     norm = symmetric(take(red_ref, "norm"))
-    u = (take_panel(red_ref) - take(red_ref, "sums", 1) * mean) * scale
+    u = (red_ref[:, :cols] - take(red_ref, "sums", 1) * mean) * scale
     norm_ref[...] = norm
+    held = take(red_ref, "held")
     if first:
         pp = norm
+        heldp_ref[...] = held
     else:
         beta = small_dot(norm, inv_ref[...])
         u = u + small_dot(beta, oldu_ref[...])
         cross = small_dot(beta, take(red_ref, "cross"))
         pp = norm + (cross + cross.T) + symmetric(small_dot(small_dot(beta, oldpp_ref[...]), beta.T))
+        heldp_ref[...] = held + small_dot(beta, oldheldp_ref[...])
         beta_ref[...] = beta
     pp_ref[...] = pp
-    u_ref[...] = u
+    if not last:
+        u_ref[...] = u
     pieces = stacked(u)
     uu = gram(pieces, pieces)
     packed = jnp.concatenate([uu[4 * i:4 * i + 4] for i in range(8)], axis=1)
@@ -234,10 +220,10 @@
 def panel(total, first, last, parts, *args):
     rows, cols = args[1].shape
     small = jax.ShapeDtypeStruct((RHS, RHS), F32)
-    outs = [jax.ShapeDtypeStruct((RHS, cols), F32)]
+    outs = [] if last else [jax.ShapeDtypeStruct((RHS, cols), F32)]
     if first:
         outs.append(jax.ShapeDtypeStruct((8, cols), F32))
-    outs += [small, small]
+    outs += [small, small, small]
     if not first:
         outs.append(small)
     outs.append(jax.ShapeDtypeStruct((parts, 4 if last else RHS + 4, 256), F32))
@@ -251,10 +237,11 @@
 
 def solve_kernel(markers, first, *refs):
     if first:
-        lam_ref, got_ref, pp_ref, norm_ref, resid_ref, send_ref, alpha_ref, inv_ref, sol_ref, base_ref = refs
-    else:
-        (lam_ref, got_ref, pp_ref, norm_ref, resid_ref, beta_ref, olddir_ref, oldsol_ref,
-         send_ref, alpha_ref, inv_ref, sol_ref, base_ref, dir_ref) = refs
+        (lam_ref, got_ref, pp_ref, norm_ref, resid_ref, heldp_ref,
+         send_ref, alpha_ref, inv_ref, heldx_ref, sol_ref, base_ref) = refs
+    else:
+        (lam_ref, got_ref, pp_ref, norm_ref, resid_ref, heldp_ref, oldheldx_ref, beta_ref, olddir_ref, oldsol_ref,
+         send_ref, alpha_ref, inv_ref, heldx_ref, sol_ref, base_ref, dir_ref) = refs
     norm = norm_ref[...]
     parts = got_ref.shape[0]
     got = got_ref[0]
@@ -273,6 +260,8 @@
     else:
         direction = resid + small_dot(beta_ref[...], olddir_ref[...])
         dir_ref[...] = direction
+    heldx = small_dot(alpha, heldp_ref[...])
+    heldx_ref[...] = heldx if first else oldheldx_ref[...] + heldx
     move = small_dot(alpha, direction)
     sol_ref[...] = move if first else oldsol_ref[...] + move
     base_ref[...] = resid - lam_ref[:, 0:1] * move
@@ -284,17 +273,13 @@
     parts, _, width = args[1].shape
     return pl.pallas_call(
         functools.partial(solve_kernel, markers, first),
-        out_shape=[jax.ShapeDtypeStruct((parts, RHS, width), F32), small, small, long, long] + ([] if first else [long]),
+        out_shape=[jax.ShapeDtypeStruct((parts, RHS, width), F32), small, small, small, long, long] + ([] if first else [long]),
         compiler_params=PARAMS,
         name="solve",
     )(*args)
 
 
-def step_kernel(held_too, *refs):
-    if held_too:
-        image_ref, alpha_ref, base_ref, dir_ref, codes_ref, sol_ref, chosen_ref, resid_ref, pay_ref = refs
-    else:
-        image_ref, alpha_ref, base_ref, dir_ref, codes_ref, resid_ref, pay_ref = refs
+def step_kernel(image_ref, alpha_ref, base_ref, dir_ref, codes_ref, chosen_ref, resid_ref, pay_ref):
     image = jnp.concatenate([image_ref[j] for j in range(image_ref.shape[0])], axis=1)
     resid = base_ref[...] - small_dot(alpha_ref[...], image)
     resid_ref[...] = resid
@@ -304,33 +289,28 @@
     put(pay_ref, "norm", gram(pieces, pieces))
     put(pay_ref, "sums", jnp.sum(resid, axis=1, keepdims=True))
     put(pay_ref, "cross", gram(dpieces, pieces))
-    if held_too:
-        chosen = chosen_ref[...]
-        for name, value in (("held_resid", pieces), ("held_dir", dpieces), ("held_sol", stacked(sol_ref[...]))):
-            put(pay_ref, name, fold(lax.dot_general(value, chosen, NT, preferred_element_type=F32)))
-
-
-def step(held_too, *args):
+    put(pay_ref, "held", rows_at(pieces, chosen_ref[...]))
+
+
+def step(*args):
     rows, cols = args[4].shape
     return pl.pallas_call(
-        functools.partial(step_kernel, held_too),
-        out_shape=[jax.ShapeDtypeStruct((RHS, rows), F32),
-                   jax.ShapeDtypeStruct((2, RHS, cols // 2 + 128) if held_too else (RHS, cols + 128), F32)],
+        step_kernel,
+        out_shape=[jax.ShapeDtypeStruct((RHS, rows), F32), jax.ShapeDtypeStruct((RHS, cols + 128), F32)],
         compiler_params=PARAMS,
         name="step",
     )(*args)
 
 
-def last_kernel(markers, lam_ref, got_ref, pp_ref, norm_ref, beta_ref, resid_ref, olddir_ref, sol_ref, red_ref,
-                out_ref, held_ref):
+def last_kernel(markers, lam_ref, got_ref, pp_ref, norm_ref, beta_ref, resid_ref, olddir_ref, sol_ref, heldp_ref,
+                heldx_ref, out_ref, held_ref):
     got = got_ref[0]
     for j in range(1, got_ref.shape[0]):
         got = got + got_ref[j]
     alpha = left_divide(symmetric(unpack(got) * (1.0 / markers) + lam_ref[:, 0:RHS] * pp_ref[...]), norm_ref[...]).T
     beta = beta_ref[...]
     out_ref[...] = sol_ref[...] + small_dot(alpha, resid_ref[...] + small_dot(beta, olddir_ref[...]))
-    direction = take(red_ref, "held_resid") + small_dot(beta, take(red_ref, "held_dir"))
-    rows = take(red_ref, "held_sol") + small_dot(alpha, direction)
+    rows = heldx_ref[...] + small_dot(alpha, heldp_ref[...])
     eye = lax.broadcasted_iota(jnp.int32, rows.shape, 0) == lax.broadcasted_iota(jnp.int32, rows.shape, 1)
     held_ref[...] = jnp.sum(jnp.where(eye, rows, 0.0), axis=0, keepdims=True)
 
@@ -358,7 +338,8 @@
     return lax.ppermute(value, "ind", on_ind(lambda y, x, c: (y, x, 1 - c)))
 
 
-def sum_chips(value):
+def sum_ind(value):
+    value = value + swap_cores(value)
     for along in ("x", "y"):
         moved = {}
         for d in (1, 3, 2):
@@ -371,13 +352,6 @@
     return value
 
 
-def sum_ind(value):
-    if value.ndim == 2:
-        return sum_chips(value + swap_cores(value))
-    mine = sum_chips(value[0] + swap_cores(value[1]))
-    return jnp.stack([mine, swap_cores(mine)])
-
-
 def exchange(value):
     return lax.all_to_all(value, "snp", 0, 0)
 
@@ -393,22 +367,23 @@
         first, last = k == 0, k == ITERS - 1
         red = sum_ind(pay)
         if first:
-            u, stat, norm, pp, out = panel(total, True, False, parts, red, codes)
+            u, stat, norm, pp, heldp, out = panel(total, True, False, parts, red, codes)
         else:
-            u, norm, pp, beta, out = panel(total, False, last, parts, red, codes, u, stat, inv, pp)
+            *new_u, norm, pp, heldp, beta, out = panel(total, False, last, parts, red, codes, u, stat, inv, pp, heldp)
+            u = new_u[0] if new_u else None
         got = exchange(out)
         if last:
             break
-        args = [lam, got, pp, norm, resid]
+        args = [lam, got, pp, norm, resid, heldp]
         if first:
             direction = resid
-            send, alpha, inv, sol, base = solve(markers, True, *args)
+            send, alpha, inv, heldx, sol, base = solve(markers, True, *args)
         else:
-            send, alpha, inv, sol, base, direction = solve(markers, False, *args, beta, direction, sol)
+            send, alpha, inv, heldx, sol, base, direction = solve(
+                markers, False, *args, heldx, beta, direction, sol)
         image = exchange(send)
-        held_too = k == ITERS - 2
-        resid, pay = step(held_too, image, alpha, base, direction, codes, *([sol, chosen] if held_too else []))
-    sol, held = last_step(markers, lam, got, pp, norm, beta, resid, direction, sol, red)
+        resid, pay = step(image, alpha, base, direction, codes, chosen)
+    sol, held = last_step(markers, lam, got, pp, norm, beta, resid, direction, sol, heldp, heldx)
     return sol.T, held[0]
 
 

time: 194 us -> 194 us (level)
    ppermute x5 -> x4, waiting for transfers between devices: 6.23 us -> 5.06 us  [swap_cores(): return lax.ppermute(value, 'ind', on_ind(lambda y, x, c: (y, x, 1 - c)))]
  transfers between devices with their start and end apart: 29 -> 28, of which waited for: 25 -> 24; matrix products, arithmetic and copies ran while one was open for 0% -> 0% of each run, Pallas kernels for 0% -> 0%
where the time goes in v4:
time: 194 us; the launch traced here: 193 us
  blocking collectives  97.7 us (50%)
  waiting for transfers between devices  40.8 us (21%)
  starting transfers between devices  32.8 us (17%)
  Pallas kernels  19.7 us (10%)
    all_to_all x7, blocking collectives, exchange(): return lax.all_to_all(value, 'snp', 0, 0)  97.7 us
    ppermute x24, waiting for transfers between devices, sum_ind(): moved[d] = lax.ppermute(value, 'ind', pairs)  35.8 us
    ppermute x24, starting transfers between devices, sum_ind(): moved[d] = lax.ppermute(value, 'ind', pairs)  32.5 us
    pallas_call x3, Pallas kernels, solve(): pl.pallas_call(functools.partial(solve_kernel, markers, first), out_shape...  6.12 us
    ppermute x4, waiting for transfers between devices, swap_cores(): return lax.ppermute(value, 'ind', on_ind(lambda y, x, c: (y, x, 1 - c)))  5.06 us
    pallas_call x4, Pallas kernels, panel(): pl.pallas_call(functools.partial(panel_kernel, total, first, last, parts)...  4.63 us
  transfers between devices with their start and end apart: 28, of which 24 were waited for; matrix products, arithmetic and copies ran while one was open for 0% of the time, Pallas kernels for 0%

profile of v4, /device:TPU:22, one launch (start us, length us, event | category | flops | bytes accessed | tf_op | source)
XLA Modules:
  0.0 192.7 jit_solution(1005450837812985606)
XLA Ops:
  1.3 3.1 %prep.1 = (bf16[2048,512]{1,0:T(8,128)(2,1)S(1)}, f32[32,640]{1,0:T(8,128)S(1)}, f32[32,2048]{1,0:T(8,128)S(1)}, f32[32,128]{1,0:T(8,128)S(1)}, bf16[32,2048]{1,0:T(8,128)(2,1)S(1)}) custom-call(s32[2048,512]{1,0:T(8,128)} %geno_hbm.1, f32[32,2048]{1,0:T(8,128)} %bitcast.4, s32[1,32]{1,0:T(1,128)} %bitcast.5, f32[1]{0:T(128)S(6)} %copy.6.ridge_ref), custom_call_target="tpu_custom_call" | custom-call | tf_op jit(solution)/shard_map/prep/pallas_call | solution.py:152
  4.5 1.3 collective-permute-done
  5.8 1.5 collective-permute-start.3
  7.3 2.1 %collective-permute-start.2 = (f32[32,640]{1,0:T(8,128)S(1)}, f32[32,640]{1,0:T(8,128)S(1)}, u32[]{:S(2)}, u32[]{:S(2)}) collective-permute-start(f32[32,640]{1,0:T(8,128)S(1)} %add.84), channel_id=1, source_target_pairs={{0,16},{8,24},{16,32},{24,40},{32,48},{40,56},{48,0},{56,8},{64,80... | collective-permute-start | bytes 245768 | tf_op jit(solution)/shard_map/ppermute | solution.py:350
  9.4 2.8 %collective-permute-done.3 = f32[32,640]{1,0:T(8,128)S(1)} collective-permute-done((f32[32,640]{1,0:T(8,128)S(1)}, f32[32,640]{1,0:T(8,128)S(1)}, u32[]{:S(2)}, u32[]{:S(2)}) %collective-permute-start.3) | collective-permute-done | bytes 81952 | tf_op jit(solution)/shard_map/ppermute | solution.py:350
  12.2 2.8 %collective-permute-done.1 = f32[32,640]{1,0:T(8,128)S(1)} collective-permute-done((f32[32,640]{1,0:T(8,128)S(1)}, f32[32,640]{1,0:T(8,128)S(1)}, u32[]{:S(2)}, u32[]{:S(2)}) %collective-permute-start.1) | collective-permute-done | bytes 81952 | tf_op jit(solution)/shard_map/ppermute | solution.py:350
  15.5 2.2 %collective-permute-start.5 = (f32[32,640]{1,0:T(8,128)S(1)}, f32[32,640]{1,0:T(8,128)S(1)}, u32[]{:S(2)}, u32[]{:S(2)}) collective-permute-start(f32[32,640]{1,0:T(8,128)S(1)} %add_add_fusion.7), channel_id=1, source_target_pairs={{0,64},{8,72},{16,80},{24,88},{32,96},{40,104},{48,112},{56,120},{... | collective-permute-start | bytes 245768 | tf_op jit(solution)/shard_map/ppermute | solution.py:350
  17.9 3.3 %collective-permute-done.6 = f32[32,640]{1,0:T(8,128)S(1)} collective-permute-done((f32[32,640]{1,0:T(8,128)S(1)}, f32[32,640]{1,0:T(8,128)S(1)}, u32[]{:S(2)}, u32[]{:S(2)}) %collective-permute-start.6) | collective-permute-done | bytes 81952 | tf_op jit(solution)/shard_map/ppermute | solution.py:350
  23.2 19.5 %all_to_all.35.refs_1_ = f32[8,36,256]{2,1,0:T(8,128)S(1)} all-to-all(f32[8,36,256]{2,1,0:T(8,128)S(1)} %get-tuple-element.61), channel_id=1, replica_groups=mesh['ind'=32,'snp'=8] {'snp'}, dimensions={0} | all-to-all | bytes 589824 | tf_op jit(solution)/shard_map/all_to_all | solution.py:356
  42.7 2.0 %solve.3 = (f32[8,32,256]{2,1,0:T(8,128)S(1)}, f32[32,32]{1,0:T(8,128)S(1)}, f32[32,32]{1,0:T(8,128)S(1)}, f32[32,32]{1,0:T(8,128)S(1)}, f32[32,2048]{1,0:T(8,128)S(1)}, /*index=5*/f32[32,2048]{1,0:T(8,128)S(1)}) custom-call(f32[32,128]{1,0:T(8,128)S(1)} %get-tuple-element.58.refs_0_.lam_ref, f32[8,36,256]{2,1,0:T(8,128)S(1)} %all_to_all.35.refs_1_, ...), custom_call_target="tpu_custom_call" | custom-call | tf_op jit(solution)/shard_map/solve/pallas_call | solution.py:274
  44.7 12.9 %all_to_all.36.image_ref = f32[8,32,256]{2,1,0:T(8,128)S(1)} all-to-all(f32[8,32,256]{2,1,0:T(8,128)S(1)} %get-tuple-element.66), channel_id=1, replica_groups=mesh['ind'=32,'snp'=8] {'snp'}, dimensions={0} | all-to-all | bytes 524288 | tf_op jit(solution)/shard_map/all_to_all | solution.py:356
  58.8 1.3 collective-permute-done.7
  60.1 1.3 collective-permute-start.10
  61.3 1.3 collective-permute-start.9
  63.4 3.1 %collective-permute-done.10 = f32[32,640]{1,0:T(8,128)S(1)} collective-permute-done((f32[32,640]{1,0:T(8,128)S(1)}, f32[32,640]{1,0:T(8,128)S(1)}, u32[]{:S(2)}, u32[]{:S(2)}) %collective-permute-start.10) | collective-permute-done | bytes 81952 | tf_op jit(solution)/shard_map/ppermute | solution.py:350
  66.5 1.8 collective-permute-done.8
  68.3 1.9 collective-permute-start.13
  70.2 1.4 collective-permute-start.12
  71.5 1.2 collective-permute-start.11
  72.7 1.7 collective-permute-done.13
  74.4 1.3 collective-permute-done.12
  76.0 1.4 panel.5
  77.4 15.5 %all_to_all.37.refs_1_ = f32[8,36,256]{2,1,0:T(8,128)S(1)} all-to-all(f32[8,36,256]{2,1,0:T(8,128)S(1)} %get-tuple-element.74), channel_id=1, replica_groups=mesh['ind'=32,'snp'=8] {'snp'}, dimensions={0} | all-to-all | bytes 589824 | tf_op jit(solution)/shard_map/all_to_all | solution.py:356
  92.8 2.0 %solve.4 = (f32[8,32,256]{2,1,0:T(8,128)S(1)}, f32[32,32]{1,0:T(8,128)S(1)}, f32[32,32]{1,0:T(8,128)S(1)}, f32[32,32]{1,0:T(8,128)S(1)}, f32[32,2048]{1,0:T(8,12...) custom-call(f32[32,128]{1,0:T(8,128)S(1)} %get-tuple-element.58.refs_0_.lam_ref, ...), custom_call_target="tpu_custom_call" | custom-call | tf_op jit(solution)/shard_map/solve/pallas_call | solution.py:274
  94.9 13.0 %all_to_all.38.image_ref = f32[8,32,256]{2,1,0:T(8,128)S(1)} all-to-all(f32[8,32,256]{2,1,0:T(8,128)S(1)} %get-tuple-element.82), channel_id=1, replica_groups=mesh['ind'=32,'snp'=8] {'snp'}, dimensions={0} | all-to-all | bytes 524288 | tf_op jit(solution)/shard_map/all_to_all | solution.py:356
  107.9 1.1 step.4
  109.2 1.3 collective-permute-done.14
  110.4 1.5 collective-permute-start.17
  114.0 2.9 %collective-permute-done.17 = f32[32,640]{1,0:T(8,128)S(1)} collective-permute-done((f32[32,640]{1,0:T(8,128)S(1)}, f32[32,640]{1,0:T(8,128)S(1)}, u32[]{:S(2)}, u32[]{:S(2)}) %collective-permute-start.17) | collective-permute-done | bytes 81952 | tf_op jit(solution)/shard_map/ppermute | solution.py:350
  116.9 1.8 collective-permute-done.15
  118.7 1.9 collective-permute-start.20
  120.5 2.2 %collective-permute-start.19 = (f32[32,640]{1,0:T(8,128)S(1)}, f32[32,640]{1,0:T(8,128)S(1)}, u32[]{:S(2)}, u32[]{:S(2)}) collective-permute-start(f32[32,640]{1,0:T(8,128)S(1)} %add_add_fusion.3), channel_id=1, source_target_pairs={{0,64},{8,72},{16,80},{24,88},{32,96},{40,104},{48,112},{56,120},{... | collective-permute-start | bytes 245768 | tf_op jit(solution)/shard_map/ppermute | solution.py:350
  122.8 2.1 %collective-permute-done.20 = f32[32,640]{1,0:T(8,128)S(1)} collective-permute-done((f32[32,640]{1,0:T(8,128)S(1)}, f32[32,640]{1,0:T(8,128)S(1)}, u32[]{:S(2)}, u32[]{:S(2)}) %collective-permute-start.20) | collective-permute-done | bytes 81952 | tf_op jit(solution)/shard_map/ppermute | solution.py:350
  125.7 1.5 collective-permute-done.18
  127.2 1.4 panel.6
  128.6 13.6 %all_to_all.39.refs_1_ = f32[8,36,256]{2,1,0:T(8,128)S(1)} all-to-all(f32[8,36,256]{2,1,0:T(8,128)S(1)} %get-tuple-element.89), channel_id=1, replica_groups=mesh['ind'=32,'snp'=8] {'snp'}, dimensions={0} | all-to-all | bytes 589824 | tf_op jit(solution)/shard_map/all_to_all | solution.py:356
  142.2 2.0 %solve.5 = (f32[8,32,256]{2,1,0:T(8,128)S(1)}, f32[32,32]{1,0:T(8,128)S(1)}, f32[32,32]{1,0:T(8,128)S(1)}, f32[32,32]{1,0:T(8,128)S(1)}, f32[32,2048]{1,0:T(8,12...) custom-call(f32[32,128]{1,0:T(8,128)S(1)} %get-tuple-element.58.refs_0_.lam_ref, ...), custom_call_target="tpu_custom_call" | custom-call | tf_op jit(solution)/shard_map/solve/pallas_call | solution.py:274
  144.2 12.9 %all_to_all.40.image_ref = f32[8,32,256]{2,1,0:T(8,128)S(1)} all-to-all(f32[8,32,256]{2,1,0:T(8,128)S(1)} %get-tuple-element.97), channel_id=1, replica_groups=mesh['ind'=32,'snp'=8] {'snp'}, dimensions={0} | all-to-all | bytes 524288 | tf_op jit(solution)/shard_map/all_to_all | solution.py:356
  157.1 1.1 step.5
  158.3 1.3 collective-permute-done.21
  159.6 3.6 %collective-permute-start.24 = (f32[32,640]{1,0:T(8,128)S(1)}, f32[32,640]{1,0:T(8,128)S(1)}, u32[]{:S(2)}, u32[]{:S(2)}) collective-permute-start(f32[32,640]{1,0:T(8,128)S(1)} %add.105), channel_id=1, source_target_pairs={{0,32},{8,40},{16,48},{24,56},{32,0},{40,8},{48,16},{56,24},{64,96... | collective-permute-start | bytes 245768 | tf_op jit(solution)/shard_map/ppermute | solution.py:350
  163.6 1.6 collective-permute-start.22
  166.2 1.4 collective-permute-done.23
  167.7 1.6 collective-permute-done.22
  170.2 4.2 %collective-permute-start.26 = (f32[32,640]{1,0:T(8,128)S(1)}, f32[32,640]{1,0:T(8,128)S(1)}, u32[]{:S(2)}, u32[]{:S(2)}) collective-permute-start(f32[32,640]{1,0:T(8,128)S(1)} %add_add_fusion.1), channel_id=1, source_target_pairs={{0,64},{8,72},{16,80},{24,88},{32,96},{40,104},{48,112},{56,120},{... | collective-permute-start | bytes 245768 | tf_op jit(solution)/shard_map/ppermute | solution.py:350
  176.4 2.4 %collective-permute-done.25 = f32[32,640]{1,0:T(8,128)S(1)} collective-permute-done((f32[32,640]{1,0:T(8,128)S(1)}, f32[32,640]{1,0:T(8,128)S(1)}, u32[]{:S(2)}, u32[]{:S(2)}) %collective-permute-start.25) | collective-permute-done | bytes 81952 | tf_op jit(solution)/shard_map/ppermute | solution.py:350
  179.8 10.4 %all_to_all.41.got_ref = f32[8,4,256]{2,1,0:T(4,128)S(1)} all-to-all(f32[8,4,256]{2,1,0:T(4,128)S(1)} %get-tuple-element.104), channel_id=1, replica_groups=mesh['ind'=32,'snp'=8] {'snp'}, dimensions={0} | all-to-all | bytes 65536 | tf_op jit(solution)/shard_map/all_to_all | solution.py:356
  190.2 2.4 %last.1 = (f32[32,2048]{1,0:T(8,128)}, f32[1,32]{1,0:T(1,128)}) custom-call(f32[32,128]{1,0:T(8,128)S(1)} %get-tuple-element.58.refs_0_.lam_ref, f32[8,4,256]{2,1,0:T(4,128)S(1)} %all_to_all.41.got_ref, f32[32,32]{1,0:T(8,128)S(1)} %get-tuple-element.105.pp_ref, f32[32,32]{1,0:T(8,128)S(1)} %get-tuple-element.106.norm_ref, ...), custom_call_target="tpu_custom_call" | custom-call | tf_op jit(solution)/shard_map/last/pallas_call | solution.py:319
  (39 shorter events, 13.5 us)
Async XLA Ops:
  4.4 1.4 collective-permute-start
  5.8 6.4 %collective-permute-start.3 = (f32[32,640]{1,0:T(8,128)S(1)}, f32[32,640]{1,0:T(8,128)S(1)}, u32[]{:S(2)}, u32[]{:S(2)}) collective-permute-start(f32[32,640]{1,0:T(8,128)S(1)} %add.84), channel_id=1, source_target_pairs={{0,32},{8,40},{16,48},{24,56},{32,0},{40,8},{48,16},{56,24},{64,96... | collective-permute-start | bytes 245768 | tf_op jit(solution)/shard_map/ppermute | solution.py:350
  7.3 4.9 %collective-permute-start.2 = (f32[32,640]{1,0:T(8,128)S(1)}, f32[32,640]{1,0:T(8,128)S(1)}, u32[]{:S(2)}, u32[]{:S(2)}) collective-permute-start(f32[32,640]{1,0:T(8,128)S(1)} %add.84), channel_id=1, source_target_pairs={{0,16},{8,24},{16,32},{24,40},{32,48},{40,56},{48,0},{56,8},{64,80... | collective-permute-start | bytes 245768 | tf_op jit(solution)/shard_map/ppermute | solution.py:350
  9.4 5.7 %collective-permute-start.1 = (f32[32,640]{1,0:T(8,128)S(1)}, f32[32,640]{1,0:T(8,128)S(1)}, u32[]{:S(2)}, u32[]{:S(2)}) collective-permute-start(f32[32,640]{1,0:T(8,128)S(1)} %add.84), channel_id=1, source_target_pairs={{0,48},{8,56},{16,0},{24,8},{32,16},{40,24},{48,32},{56,40},{64,11... | collective-permute-start | bytes 245768 | tf_op jit(solution)/shard_map/ppermute | solution.py:350
  15.1 6.1 %collective-permute-start.6 = (f32[32,640]{1,0:T(8,128)S(1)}, f32[32,640]{1,0:T(8,128)S(1)}, u32[]{:S(2)}, u32[]{:S(2)}) collective-permute-start(f32[32,640]{1,0:T(8,128)S(1)} %add_add_fusion.7), channel_id=1, source_target_pairs={{0,128},{8,136},{16,144},{24,152},{32,160},{40,168},{48,176},{56,1... | collective-permute-start | bytes 245768 | tf_op jit(solution)/shard_map/ppermute | solution.py:350
  15.5 5.7 %collective-permute-start.5 = (f32[32,640]{1,0:T(8,128)S(1)}, f32[32,640]{1,0:T(8,128)S(1)}, u32[]{:S(2)}, u32[]{:S(2)}) collective-permute-start(f32[32,640]{1,0:T(8,128)S(1)} %add_add_fusion.7), channel_id=1, source_target_pairs={{0,64},{8,72},{16,80},{24,88},{32,96},{40,104},{48,112},{56,120},{... | collective-permute-start | bytes 245768 | tf_op jit(solution)/shard_map/ppermute | solution.py:350
  17.7 4.6 %collective-permute-start.4 = (f32[32,640]{1,0:T(8,128)S(1)}, f32[32,640]{1,0:T(8,128)S(1)}, u32[]{:S(2)}, u32[]{:S(2)}) collective-permute-start(f32[32,640]{1,0:T(8,128)S(1)} %add_add_fusion.7), channel_id=1, source_target_pairs={{0,192},{8,200},{16,208},{24,216},{32,224},{40,232},{48,240},{56,2... | collective-permute-start | bytes 245768 | tf_op jit(solution)/shard_map/ppermute | solution.py:350
  58.7 1.4 collective-permute-start.7
  60.1 6.4 %collective-permute-start.10 = (f32[32,640]{1,0:T(8,128)S(1)}, f32[32,640]{1,0:T(8,128)S(1)}, u32[]{:S(2)}, u32[]{:S(2)}) collective-permute-start(f32[32,640]{1,0:T(8,128)S(1)} %add.91), channel_id=1, source_target_pairs={{0,32},{8,40},{16,48},{24,56},{32,0},{40,8},{48,16},{56,24},{64,96... | collective-permute-start | bytes 245768 | tf_op jit(solution)/shard_map/ppermute | solution.py:350
  61.3 5.2 %collective-permute-start.9 = (f32[32,640]{1,0:T(8,128)S(1)}, f32[32,640]{1,0:T(8,128)S(1)}, u32[]{:S(2)}, u32[]{:S(2)}) collective-permute-start(f32[32,640]{1,0:T(8,128)S(1)} %add.91), channel_id=1, source_target_pairs={{0,16},{8,24},{16,32},{24,40},{32,48},{40,56},{48,0},{56,8},{64,80... | collective-permute-start | bytes 245768 | tf_op jit(solution)/shard_map/ppermute | solution.py:350
  62.6 5.7 %collective-permute-start.8 = (f32[32,640]{1,0:T(8,128)S(1)}, f32[32,640]{1,0:T(8,128)S(1)}, u32[]{:S(2)}, u32[]{:S(2)}) collective-permute-start(f32[32,640]{1,0:T(8,128)S(1)} %add.91), channel_id=1, source_target_pairs={{0,48},{8,56},{16,0},{24,8},{32,16},{40,24},{48,32},{56,40},{64,11... | collective-permute-start | bytes 245768 | tf_op jit(solution)/shard_map/ppermute | solution.py:350
  68.3 6.1 %collective-permute-start.13 = (f32[32,640]{1,0:T(8,128)S(1)}, f32[32,640]{1,0:T(8,128)S(1)}, u32[]{:S(2)}, u32[]{:S(2)}) collective-permute-start(f32[32,640]{1,0:T(8,128)S(1)} %add_add_fusion.5), channel_id=1, source_target_pairs={{0,128},{8,136},{16,144},{24,152},{32,160},{40,168},{48,176},{56,1... | collective-permute-start | bytes 245768 | tf_op jit(solution)/shard_map/ppermute | solution.py:350
  70.2 5.5 %collective-permute-start.12 = (f32[32,640]{1,0:T(8,128)S(1)}, f32[32,640]{1,0:T(8,128)S(1)}, u32[]{:S(2)}, u32[]{:S(2)}) collective-permute-start(f32[32,640]{1,0:T(8,128)S(1)} %add_add_fusion.5), channel_id=1, source_target_pairs={{0,64},{8,72},{16,80},{24,88},{32,96},{40,104},{48,112},{56,120},{... | collective-permute-start | bytes 245768 | tf_op jit(solution)/shard_map/ppermute | solution.py:350
  71.5 4.4 %collective-permute-start.11 = (f32[32,640]{1,0:T(8,128)S(1)}, f32[32,640]{1,0:T(8,128)S(1)}, u32[]{:S(2)}, u32[]{:S(2)}) collective-permute-start(f32[32,640]{1,0:T(8,128)S(1)} %add_add_fusion.5), channel_id=1, source_target_pairs={{0,192},{8,200},{16,208},{24,216},{32,224},{40,232},{48,240},{56,2... | collective-permute-start | bytes 245768 | tf_op jit(solution)/shard_map/ppermute | solution.py:350
  109.1 1.4 collective-permute-start.14
  110.4 6.4 %collective-permute-start.17 = (f32[32,640]{1,0:T(8,128)S(1)}, f32[32,640]{1,0:T(8,128)S(1)}, u32[]{:S(2)}, u32[]{:S(2)}) collective-permute-start(f32[32,640]{1,0:T(8,128)S(1)} %add.98), channel_id=1, source_target_pairs={{0,32},{8,40},{16,48},{24,56},{32,0},{40,8},{48,16},{56,24},{64,96... | collective-permute-start | bytes 245768 | tf_op jit(solution)/shard_map/ppermute | solution.py:350
  111.9 4.9 %collective-permute-start.16 = (f32[32,640]{1,0:T(8,128)S(1)}, f32[32,640]{1,0:T(8,128)S(1)}, u32[]{:S(2)}, u32[]{:S(2)}) collective-permute-start(f32[32,640]{1,0:T(8,128)S(1)} %add.98), channel_id=1, source_target_pairs={{0,16},{8,24},{16,32},{24,40},{32,48},{40,56},{48,0},{56,8},{64,80... | collective-permute-start | bytes 245768 | tf_op jit(solution)/shard_map/ppermute | solution.py:350
  113.0 5.7 %collective-permute-start.15 = (f32[32,640]{1,0:T(8,128)S(1)}, f32[32,640]{1,0:T(8,128)S(1)}, u32[]{:S(2)}, u32[]{:S(2)}) collective-permute-start(f32[32,640]{1,0:T(8,128)S(1)} %add.98), channel_id=1, source_target_pairs={{0,48},{8,56},{16,0},{24,8},{32,16},{40,24},{48,32},{56,40},{64,11... | collective-permute-start | bytes 245768 | tf_op jit(solution)/shard_map/ppermute | solution.py:350
  118.7 6.2 %collective-permute-start.20 = (f32[32,640]{1,0:T(8,128)S(1)}, f32[32,640]{1,0:T(8,128)S(1)}, u32[]{:S(2)}, u32[]{:S(2)}) collective-permute-start(f32[32,640]{1,0:T(8,128)S(1)} %add_add_fusion.3), channel_id=1, source_target_pairs={{0,128},{8,136},{16,144},{24,152},{32,160},{40,168},{48,176},{56,1... | collective-permute-start | bytes 245768 | tf_op jit(solution)/shard_map/ppermute | solution.py:350
  120.5 5.2 %collective-permute-start.19 = (f32[32,640]{1,0:T(8,128)S(1)}, f32[32,640]{1,0:T(8,128)S(1)}, u32[]{:S(2)}, u32[]{:S(2)}) collective-permute-start(f32[32,640]{1,0:T(8,128)S(1)} %add_add_fusion.3), channel_id=1, source_target_pairs={{0,64},{8,72},{16,80},{24,88},{32,96},{40,104},{48,112},{56,120},{... | collective-permute-start | bytes 245768 | tf_op jit(solution)/shard_map/ppermute | solution.py:350
  122.8 4.4 %collective-permute-start.18 = (f32[32,640]{1,0:T(8,128)S(1)}, f32[32,640]{1,0:T(8,128)S(1)}, u32[]{:S(2)}, u32[]{:S(2)}) collective-permute-start(f32[32,640]{1,0:T(8,128)S(1)} %add_add_fusion.3), channel_id=1, source_target_pairs={{0,192},{8,200},{16,208},{24,216},{32,224},{40,232},{48,240},{56,2... | collective-permute-start | bytes 245768 | tf_op jit(solution)/shard_map/ppermute | solution.py:350
  158.2 1.4 collective-permute-start.21
  159.6 6.6 %collective-permute-start.24 = (f32[32,640]{1,0:T(8,128)S(1)}, f32[32,640]{1,0:T(8,128)S(1)}, u32[]{:S(2)}, u32[]{:S(2)}) collective-permute-start(f32[32,640]{1,0:T(8,128)S(1)} %add.105), channel_id=1, source_target_pairs={{0,32},{8,40},{16,48},{24,56},{32,0},{40,8},{48,16},{56,24},{64,96... | collective-permute-start | bytes 245768 | tf_op jit(solution)/shard_map/ppermute | solution.py:350
  163.2 4.4 %collective-permute-start.23 = (f32[32,640]{1,0:T(8,128)S(1)}, f32[32,640]{1,0:T(8,128)S(1)}, u32[]{:S(2)}, u32[]{:S(2)}) collective-permute-start(f32[32,640]{1,0:T(8,128)S(1)} %add.105), channel_id=1, source_target_pairs={{0,16},{8,24},{16,32},{24,40},{32,48},{40,56},{48,0},{56,8},{64,80... | collective-permute-start | bytes 245768 | tf_op jit(solution)/shard_map/ppermute | solution.py:350
  163.6 5.7 %collective-permute-start.22 = (f32[32,640]{1,0:T(8,128)S(1)}, f32[32,640]{1,0:T(8,128)S(1)}, u32[]{:S(2)}, u32[]{:S(2)}) collective-permute-start(f32[32,640]{1,0:T(8,128)S(1)} %add.105), channel_id=1, source_target_pairs={{0,48},{8,56},{16,0},{24,8},{32,16},{40,24},{48,32},{56,40},{64,11... | collective-permute-start | bytes 245768 | tf_op jit(solution)/shard_map/ppermute | solution.py:350
  169.3 6.1 %collective-permute-start.27 = (f32[32,640]{1,0:T(8,128)S(1)}, f32[32,640]{1,0:T(8,128)S(1)}, u32[]{:S(2)}, u32[]{:S(2)}) collective-permute-start(f32[32,640]{1,0:T(8,128)S(1)} %add_add_fusion.1), channel_id=1, source_target_pairs={{0,128},{8,136},{16,144},{24,152},{32,160},{40,168},{48,176},{56,1... | collective-permute-start | bytes 245768 | tf_op jit(solution)/shard_map/ppermute | solution.py:350
  170.2 6.2 %collective-permute-start.26 = (f32[32,640]{1,0:T(8,128)S(1)}, f32[32,640]{1,0:T(8,128)S(1)}, u32[]{:S(2)}, u32[]{:S(2)}) collective-permute-start(f32[32,640]{1,0:T(8,128)S(1)} %add_add_fusion.1), channel_id=1, source_target_pairs={{0,64},{8,72},{16,80},{24,88},{32,96},{40,104},{48,112},{56,120},{... | collective-permute-start | bytes 245768 | tf_op jit(solution)/shard_map/ppermute | solution.py:350
  174.4 4.4 %collective-permute-start.25 = (f32[32,640]{1,0:T(8,128)S(1)}, f32[32,640]{1,0:T(8,128)S(1)}, u32[]{:S(2)}, u32[]{:S(2)}) collective-permute-start(f32[32,640]{1,0:T(8,128)S(1)} %add_add_fusion.1), channel_id=1, source_target_pairs={{0,192},{8,200},{16,208},{24,216},{32,224},{40,232},{48,240},{56,2... | collective-permute-start | bytes 245768 | tf_op jit(solution)/shard_map/ppermute | solution.py:350

commit v5 on v4

--- a/solution.py
+++ b/solution.py
@@ -104,19 +104,19 @@
     return fold(lax.dot_general(pieces, chosen, NT, preferred_element_type=F32))
 
 
-QUARTERS = 4
+CHUNKS = 8
 
 
 def prep_kernel(geno_hbm, rhs_hbm, held_hbm, ridge_ref, codes_ref, pay_ref, rhs_ref, lam_ref, chosen_ref,
                 geno_ref, held_ref, sems):
     rows, cols = geno_ref.shape
-    chunk = rows // QUARTERS
-    rhs_copy = pltpu.make_async_copy(rhs_hbm, rhs_ref, sems.at[QUARTERS])
+    chunk = rows // CHUNKS
+    rhs_copy = pltpu.make_async_copy(rhs_hbm, rhs_ref, sems.at[CHUNKS])
     rhs_copy.start()
-    held_copy = pltpu.make_async_copy(held_hbm, held_ref, sems.at[QUARTERS + 1])
+    held_copy = pltpu.make_async_copy(held_hbm, held_ref, sems.at[CHUNKS + 1])
     held_copy.start()
     copies = []
-    for q in range(QUARTERS):
+    for q in range(CHUNKS):
         part = pl.ds(q * chunk, chunk)
         copies.append(pltpu.make_async_copy(geno_hbm.at[part, :], geno_ref.at[part, :], sems.at[q]))
         copies[-1].start()
@@ -130,7 +130,7 @@
     chosen_ref[...] = jnp.concatenate([(place == held_ref[:, k:k + 1]).astype(F32) for k in range(RHS)], axis=0).astype(BF16)
     lhs = jnp.concatenate([pieces, jnp.ones((32, rows), BF16)], axis=0)
     panel_, sums, squares = 0.0, 0.0, 0.0
-    for q in range(QUARTERS):
+    for q in range(CHUNKS):
         copies[q].wait()
         centred = (geno_ref[q * chunk:(q + 1) * chunk, :] - 1).astype(F32)
         codes = centred.astype(BF16)
@@ -156,7 +156,7 @@
                    jax.ShapeDtypeStruct((RHS, rows), F32), jax.ShapeDtypeStruct((RHS, 128), F32),
                    jax.ShapeDtypeStruct((RHS, rows), BF16)],
         scratch_shapes=[pltpu.VMEM((rows, cols), jnp.int32), pltpu.VMEM(held.shape, jnp.int32),
-                        pltpu.SemaphoreType.DMA((QUARTERS + 2,))],
+                        pltpu.SemaphoreType.DMA((CHUNKS + 2,))],
         compiler_params=PARAMS,
         name="prep",
     )(*[pltpu.with_memory_space_constraint(arg, pltpu.HBM) for arg in (genotypes, rhs, held)], ridge)
@@ -344,9 +344,9 @@
         moved = {}
         for d in (1, 3, 2):
             if along == "x":
-                pairs = on_ind(lambda y, x, c, d=d: (y, (x + d) % XSIZE, c))
+                pairs = on_ind(lambda y, x, c, d=d: (y, x ^ d, c))
             else:
-                pairs = on_ind(lambda y, x, c, d=d: ((y + d) % YSIZE, x, c))
+                pairs = on_ind(lambda y, x, c, d=d: (y ^ d, x, c))
             moved[d] = lax.ppermute(value, "ind", pairs)
         value = (moved[3] + moved[1]) + (moved[2] + value)
     return value

time: 194 us -> 192 us (0.990)
  waiting for transfers between devices: 40.8 us -> 33.5 us
  blocking collectives: 97.7 us -> 100 us
    ppermute x24, waiting for transfers between devices: 35.8 us -> 28.4 us  [sum_ind(): moved[d] = lax.ppermute(value, 'ind', pairs)]
    all_to_all x7, blocking collectives: 97.7 us -> 100 us  [exchange(): return lax.all_to_all(value, 'snp', 0, 0)]
  transfers between devices with their start and end apart: 28 -> 28, of which waited for: 24 -> 21; matrix products, arithmetic and copies ran while one was open for 0% -> 0% of each run, Pallas kernels for 0% -> 0%
where the time goes in v5:
time: 192 us; the launch traced here: 190 us
  blocking collectives  100 us (52%)
  starting transfers between devices  33.8 us (18%)
  waiting for transfers between devices  33.5 us (17%)
  Pallas kernels  20.4 us (11%)
    all_to_all x7, blocking collectives, exchange(): return lax.all_to_all(value, 'snp', 0, 0)  100 us
    ppermute x24, starting transfers between devices, sum_ind(): moved[d] = lax.ppermute(value, 'ind', pairs)  33.4 us
    ppermute x24, waiting for transfers between devices, sum_ind(): moved[d] = lax.ppermute(value, 'ind', pairs)  28.4 us
    pallas_call x3, Pallas kernels, solve(): pl.pallas_call(functools.partial(solve_kernel, markers, first), out_shape...  6.13 us
    ppermute x4, waiting for transfers between devices, swap_cores(): return lax.ppermute(value, 'ind', on_ind(lambda y, x, c: (y, x, 1 - c)))  5.06 us
    pallas_call x4, Pallas kernels, panel(): pl.pallas_call(functools.partial(panel_kernel, total, first, last, parts)...  4.63 us
  transfers between devices with their start and end apart: 28, of which 21 were waited for; matrix products, arithmetic and copies ran while one was open for 0% of the time, Pallas kernels for 0%

profile of v5, /device:TPU:22, one launch (start us, length us, event | category | flops | bytes accessed | tf_op | source)
XLA Modules:
  0.0 189.7 jit_solution(16638007350016445457)
XLA Ops:
  1.3 3.8 %prep.1 = (bf16[2048,512]{1,0:T(8,128)(2,1)S(1)}, f32[32,640]{1,0:T(8,128)S(1)}, f32[32,2048]{1,0:T(8,128)S(1)}, f32[32,128]{1,0:T(8,128)S(1)}, bf16[32,2048]{1,0:T(8,128)(2,1)S(1)}) custom-call(s32[2048,512]{1,0:T(8,128)} %geno_hbm.1, f32[32,2048]{1,0:T(8,128)} %bitcast.4, s32[1,32]{1,0:T(1,128)} %bitcast.5, f32[1]{0:T(128)S(6)} %copy.6.ridge_ref), custom_call_target="tpu_custom_call" | custom-call | tf_op jit(solution)/shard_map/prep/pallas_call | solution.py:152
  5.2 1.3 collective-permute-done
  6.5 1.5 collective-permute-start.3
  8.0 2.7 %collective-permute-start.1 = (f32[32,640]{1,0:T(8,128)S(1)}, f32[32,640]{1,0:T(8,128)S(1)}, u32[]{:S(2)}, u32[]{:S(2)}) collective-permute-start(f32[32,640]{1,0:T(8,128)S(1)} %add.84), channel_id=1, source_target_pairs={{0,48},{8,56},{16,32},{24,40},{32,16},{40,24},{48,0},{56,8},{64,11... | collective-permute-start | bytes 245768 | tf_op jit(solution)/shard_map/ppermute | solution.py:350
  10.6 2.5 %collective-permute-done.3 = f32[32,640]{1,0:T(8,128)S(1)} collective-permute-done((f32[32,640]{1,0:T(8,128)S(1)}, f32[32,640]{1,0:T(8,128)S(1)}, u32[]{:S(2)}, u32[]{:S(2)}) %collective-permute-start.3) | collective-permute-done | bytes 81952 | tf_op jit(solution)/shard_map/ppermute | solution.py:350
  13.2 1.2 collective-permute-done.1
  14.3 1.4 collective-permute-start.6
  15.7 1.2 collective-permute-start.5
  16.9 1.6 collective-permute-start.4
  18.5 2.4 %collective-permute-done.6 = f32[32,640]{1,0:T(8,128)S(1)} collective-permute-done((f32[32,640]{1,0:T(8,128)S(1)}, f32[32,640]{1,0:T(8,128)S(1)}, u32[]{:S(2)}, u32[]{:S(2)}) %collective-permute-start.6) | collective-permute-done | bytes 81952 | tf_op jit(solution)/shard_map/ppermute | solution.py:350
  22.7 20.6 %all_to_all.35.refs_1_ = f32[8,36,256]{2,1,0:T(8,128)S(1)} all-to-all(f32[8,36,256]{2,1,0:T(8,128)S(1)} %get-tuple-element.61), channel_id=1, replica_groups=mesh['ind'=32,'snp'=8] {'snp'}, dimensions={0} | all-to-all | bytes 589824 | tf_op jit(solution)/shard_map/all_to_all | solution.py:356
  43.2 2.0 %solve.3 = (f32[8,32,256]{2,1,0:T(8,128)S(1)}, f32[32,32]{1,0:T(8,128)S(1)}, f32[32,32]{1,0:T(8,128)S(1)}, f32[32,32]{1,0:T(8,128)S(1)}, f32[32,2048]{1,0:T(8,128)S(1)}, /*index=5*/f32[32,2048]{1,0:T(8,128)S(1)}) custom-call(f32[32,128]{1,0:T(8,128)S(1)} %get-tuple-element.58.refs_0_.lam_ref, f32[8,36,256]{2,1,0:T(8,128)S(1)} %all_to_all.35.refs_1_, ...), custom_call_target="tpu_custom_call" | custom-call | tf_op jit(solution)/shard_map/solve/pallas_call | solution.py:274
  45.3 12.9 %all_to_all.36.image_ref = f32[8,32,256]{2,1,0:T(8,128)S(1)} all-to-all(f32[8,32,256]{2,1,0:T(8,128)S(1)} %get-tuple-element.66), channel_id=1, replica_groups=mesh['ind'=32,'snp'=8] {'snp'}, dimensions={0} | all-to-all | bytes 524288 | tf_op jit(solution)/shard_map/all_to_all | solution.py:356
  58.1 1.1 step.3
  59.4 1.3 collective-permute-done.7
  62.1 2.7 %collective-permute-start.8 = (f32[32,640]{1,0:T(8,128)S(1)}, f32[32,640]{1,0:T(8,128)S(1)}, u32[]{:S(2)}, u32[]{:S(2)}) collective-permute-start(f32[32,640]{1,0:T(8,128)S(1)} %add.91), channel_id=1, source_target_pairs={{0,48},{8,56},{16,32},{24,40},{32,16},{40,24},{48,0},{56,8},{64,11... | collective-permute-start | bytes 245768 | tf_op jit(solution)/shard_map/ppermute | solution.py:350
  64.8 2.7 %collective-permute-done.10 = f32[32,640]{1,0:T(8,128)S(1)} collective-permute-done((f32[32,640]{1,0:T(8,128)S(1)}, f32[32,640]{1,0:T(8,128)S(1)}, u32[]{:S(2)}, u32[]{:S(2)}) %collective-permute-start.10) | collective-permute-done | bytes 81952 | tf_op jit(solution)/shard_map/ppermute | solution.py:350
  68.5 2.3 %collective-permute-start.13 = (f32[32,640]{1,0:T(8,128)S(1)}, f32[32,640]{1,0:T(8,128)S(1)}, u32[]{:S(2)}, u32[]{:S(2)}) collective-permute-start(f32[32,640]{1,0:T(8,128)S(1)} %add_add_fusion.5), channel_id=1, source_target_pairs={{0,128},{8,136},{16,144},{24,152},{32,160},{40,168},{48,176},{56,1... | collective-permute-start | bytes 245768 | tf_op jit(solution)/shard_map/ppermute | solution.py:350
  70.8 1.3 collective-permute-start.12
  72.7 2.3 %collective-permute-done.13 = f32[32,640]{1,0:T(8,128)S(1)} collective-permute-done((f32[32,640]{1,0:T(8,128)S(1)}, f32[32,640]{1,0:T(8,128)S(1)}, u32[]{:S(2)}, u32[]{:S(2)}) %collective-permute-start.13) | collective-permute-done | bytes 81952 | tf_op jit(solution)/shard_map/ppermute | solution.py:350
  76.6 1.4 panel.5
  77.9 15.2 %all_to_all.37.refs_1_ = f32[8,36,256]{2,1,0:T(8,128)S(1)} all-to-all(f32[8,36,256]{2,1,0:T(8,128)S(1)} %get-tuple-element.74), channel_id=1, replica_groups=mesh['ind'=32,'snp'=8] {'snp'}, dimensions={0} | all-to-all | bytes 589824 | tf_op jit(solution)/shard_map/all_to_all | solution.py:356
  93.1 2.0 %solve.4 = (f32[8,32,256]{2,1,0:T(8,128)S(1)}, f32[32,32]{1,0:T(8,128)S(1)}, f32[32,32]{1,0:T(8,128)S(1)}, f32[32,32]{1,0:T(8,128)S(1)}, f32[32,2048]{1,0:T(8,12...) custom-call(f32[32,128]{1,0:T(8,128)S(1)} %get-tuple-element.58.refs_0_.lam_ref, ...), custom_call_target="tpu_custom_call" | custom-call | tf_op jit(solution)/shard_map/solve/pallas_call | solution.py:274
  95.1 13.0 %all_to_all.38.image_ref = f32[8,32,256]{2,1,0:T(8,128)S(1)} all-to-all(f32[8,32,256]{2,1,0:T(8,128)S(1)} %get-tuple-element.82), channel_id=1, replica_groups=mesh['ind'=32,'snp'=8] {'snp'}, dimensions={0} | all-to-all | bytes 524288 | tf_op jit(solution)/shard_map/all_to_all | solution.py:356
  108.1 1.1 step.4
  109.4 1.3 collective-permute-done.14
  110.6 1.2 collective-permute-start.17
  111.9 3.0 %collective-permute-start.15 = (f32[32,640]{1,0:T(8,128)S(1)}, f32[32,640]{1,0:T(8,128)S(1)}, u32[]{:S(2)}, u32[]{:S(2)}) collective-permute-start(f32[32,640]{1,0:T(8,128)S(1)} %add.98), channel_id=1, source_target_pairs={{0,48},{8,56},{16,32},{24,40},{32,16},{40,24},{48,0},{56,8},{64,11... | collective-permute-start | bytes 245768 | tf_op jit(solution)/shard_map/ppermute | solution.py:350
  114.8 2.7 %collective-permute-done.17 = f32[32,640]{1,0:T(8,128)S(1)} collective-permute-done((f32[32,640]{1,0:T(8,128)S(1)}, f32[32,640]{1,0:T(8,128)S(1)}, u32[]{:S(2)}, u32[]{:S(2)}) %collective-permute-start.17) | collective-permute-done | bytes 81952 | tf_op jit(solution)/shard_map/ppermute | solution.py:350
  118.5 1.8 collective-permute-start.20
  120.9 1.8 collective-permute-start.18
  122.7 2.4 %collective-permute-done.20 = f32[32,640]{1,0:T(8,128)S(1)} collective-permute-done((f32[32,640]{1,0:T(8,128)S(1)}, f32[32,640]{1,0:T(8,128)S(1)}, u32[]{:S(2)}, u32[]{:S(2)}) %collective-permute-start.20) | collective-permute-done | bytes 81952 | tf_op jit(solution)/shard_map/ppermute | solution.py:350
  126.0 1.4 panel.6
  127.3 15.4 %all_to_all.39.refs_1_ = f32[8,36,256]{2,1,0:T(8,128)S(1)} all-to-all(f32[8,36,256]{2,1,0:T(8,128)S(1)} %get-tuple-element.89), channel_id=1, replica_groups=mesh['ind'=32,'snp'=8] {'snp'}, dimensions={0} | all-to-all | bytes 589824 | tf_op jit(solution)/shard_map/all_to_all | solution.py:356
  142.8 2.0 %solve.5 = (f32[8,32,256]{2,1,0:T(8,128)S(1)}, f32[32,32]{1,0:T(8,128)S(1)}, f32[32,32]{1,0:T(8,128)S(1)}, f32[32,32]{1,0:T(8,128)S(1)}, f32[32,2048]{1,0:T(8,12...) custom-call(f32[32,128]{1,0:T(8,128)S(1)} %get-tuple-element.58.refs_0_.lam_ref, ...), custom_call_target="tpu_custom_call" | custom-call | tf_op jit(solution)/shard_map/solve/pallas_call | solution.py:274
  144.8 13.0 %all_to_all.40.image_ref = f32[8,32,256]{2,1,0:T(8,128)S(1)} all-to-all(f32[8,32,256]{2,1,0:T(8,128)S(1)} %get-tuple-element.97), channel_id=1, replica_groups=mesh['ind'=32,'snp'=8] {'snp'}, dimensions={0} | all-to-all | bytes 524288 | tf_op jit(solution)/shard_map/all_to_all | solution.py:356
  157.9 1.1 step.5
  159.1 1.3 collective-permute-done.21
  160.7 3.8 %collective-permute-start.22 = (f32[32,640]{1,0:T(8,128)S(1)}, f32[32,640]{1,0:T(8,128)S(1)}, u32[]{:S(2)}, u32[]{:S(2)}) collective-permute-start(f32[32,640]{1,0:T(8,128)S(1)} %add.105), channel_id=1, source_target_pairs={{0,48},{8,56},{16,32},{24,40},{32,16},{40,24},{48,0},{56,8},{64,11... | collective-permute-start | bytes 245768 | tf_op jit(solution)/shard_map/ppermute | solution.py:350
  164.5 2.7 %collective-permute-done.24 = f32[32,640]{1,0:T(8,128)S(1)} collective-permute-done((f32[32,640]{1,0:T(8,128)S(1)}, f32[32,640]{1,0:T(8,128)S(1)}, u32[]{:S(2)}, u32[]{:S(2)}) %collective-permute-start.24) | collective-permute-done | bytes 81952 | tf_op jit(solution)/shard_map/ppermute | solution.py:350
  167.2 1.0 collective-permute-done.22
  168.2 1.6 collective-permute-start.27
  169.9 1.1 collective-permute-start.26
  171.0 1.4 collective-permute-start.25
  172.4 2.6 %collective-permute-done.27 = f32[32,640]{1,0:T(8,128)S(1)} collective-permute-done((f32[32,640]{1,0:T(8,128)S(1)}, f32[32,640]{1,0:T(8,128)S(1)}, u32[]{:S(2)}, u32[]{:S(2)}) %collective-permute-start.27) | collective-permute-done | bytes 81952 | tf_op jit(solution)/shard_map/ppermute | solution.py:350
  175.9 1.0 panel.7
  176.9 10.4 %all_to_all.41.got_ref = f32[8,4,256]{2,1,0:T(4,128)S(1)} all-to-all(f32[8,4,256]{2,1,0:T(4,128)S(1)} %get-tuple-element.104), channel_id=1, replica_groups=mesh['ind'=32,'snp'=8] {'snp'}, dimensions={0} | all-to-all | bytes 65536 | tf_op jit(solution)/shard_map/all_to_all | solution.py:356
  187.3 2.4 %last.1 = (f32[32,2048]{1,0:T(8,128)}, f32[1,32]{1,0:T(1,128)}) custom-call(f32[32,128]{1,0:T(8,128)S(1)} %get-tuple-element.58.refs_0_.lam_ref, f32[8,4,256]{2,1,0:T(4,128)S(1)} %all_to_all.41.got_ref, f32[32,32]{1,0:T(8,128)S(1)} %get-tuple-element.105.pp_ref, f32[32,32]{1,0:T(8,128)S(1)} %get-tuple-element.106.norm_ref, ...), custom_call_target="tpu_custom_call" | custom-call | tf_op jit(solution)/shard_map/last/pallas_call | solution.py:319
  (39 shorter events, 10.5 us)
Async XLA Ops:
  5.1 1.4 collective-permute-start
  6.5 6.7 %collective-permute-start.3 = (f32[32,640]{1,0:T(8,128)S(1)}, f32[32,640]{1,0:T(8,128)S(1)}, u32[]{:S(2)}, u32[]{:S(2)}) collective-permute-start(f32[32,640]{1,0:T(8,128)S(1)} %add.84), channel_id=1, source_target_pairs={{0,32},{8,40},{16,48},{24,56},{32,0},{40,8},{48,16},{56,24},{64,96... | collective-permute-start | bytes 245768 | tf_op jit(solution)/shard_map/ppermute | solution.py:350
  8.0 5.2 %collective-permute-start.2 = (f32[32,640]{1,0:T(8,128)S(1)}, f32[32,640]{1,0:T(8,128)S(1)}, u32[]{:S(2)}, u32[]{:S(2)}) collective-permute-start(f32[32,640]{1,0:T(8,128)S(1)} %add.84), channel_id=1, source_target_pairs={{0,16},{8,24},{16,0},{24,8},{32,48},{40,56},{48,32},{56,40},{64,80... | collective-permute-start | bytes 245768 | tf_op jit(solution)/shard_map/ppermute | solution.py:350
  8.0 6.4 %collective-permute-start.1 = (f32[32,640]{1,0:T(8,128)S(1)}, f32[32,640]{1,0:T(8,128)S(1)}, u32[]{:S(2)}, u32[]{:S(2)}) collective-permute-start(f32[32,640]{1,0:T(8,128)S(1)} %add.84), channel_id=1, source_target_pairs={{0,48},{8,56},{16,32},{24,40},{32,16},{40,24},{48,0},{56,8},{64,11... | collective-permute-start | bytes 245768 | tf_op jit(solution)/shard_map/ppermute | solution.py:350
  14.3 6.6 %collective-permute-start.6 = (f32[32,640]{1,0:T(8,128)S(1)}, f32[32,640]{1,0:T(8,128)S(1)}, u32[]{:S(2)}, u32[]{:S(2)}) collective-permute-start(f32[32,640]{1,0:T(8,128)S(1)} %add_add_fusion.7), channel_id=1, source_target_pairs={{0,128},{8,136},{16,144},{24,152},{32,160},{40,168},{48,176},{56,1... | collective-permute-start | bytes 245768 | tf_op jit(solution)/shard_map/ppermute | solution.py:350
  15.7 5.2 %collective-permute-start.5 = (f32[32,640]{1,0:T(8,128)S(1)}, f32[32,640]{1,0:T(8,128)S(1)}, u32[]{:S(2)}, u32[]{:S(2)}) collective-permute-start(f32[32,640]{1,0:T(8,128)S(1)} %add_add_fusion.7), channel_id=1, source_target_pairs={{0,64},{8,72},{16,80},{24,88},{32,96},{40,104},{48,112},{56,120},{... | collective-permute-start | bytes 245768 | tf_op jit(solution)/shard_map/ppermute | solution.py:350
  16.9 4.8 %collective-permute-start.4 = (f32[32,640]{1,0:T(8,128)S(1)}, f32[32,640]{1,0:T(8,128)S(1)}, u32[]{:S(2)}, u32[]{:S(2)}) collective-permute-start(f32[32,640]{1,0:T(8,128)S(1)} %add_add_fusion.7), channel_id=1, source_target_pairs={{0,192},{8,200},{16,208},{24,216},{32,224},{40,232},{48,240},{56,2... | collective-permute-start | bytes 245768 | tf_op jit(solution)/shard_map/ppermute | solution.py:350
  59.3 1.4 collective-permute-start.7
  60.7 6.9 %collective-permute-start.10 = (f32[32,640]{1,0:T(8,128)S(1)}, f32[32,640]{1,0:T(8,128)S(1)}, u32[]{:S(2)}, u32[]{:S(2)}) collective-permute-start(f32[32,640]{1,0:T(8,128)S(1)} %add.91), channel_id=1, source_target_pairs={{0,32},{8,40},{16,48},{24,56},{32,0},{40,8},{48,16},{56,24},{64,96... | collective-permute-start | bytes 245768 | tf_op jit(solution)/shard_map/ppermute | solution.py:350
  61.5 6.1 %collective-permute-start.9 = (f32[32,640]{1,0:T(8,128)S(1)}, f32[32,640]{1,0:T(8,128)S(1)}, u32[]{:S(2)}, u32[]{:S(2)}) collective-permute-start(f32[32,640]{1,0:T(8,128)S(1)} %add.91), channel_id=1, source_target_pairs={{0,16},{8,24},{16,0},{24,8},{32,48},{40,56},{48,32},{56,40},{64,80... | collective-permute-start | bytes 245768 | tf_op jit(solution)/shard_map/ppermute | solution.py:350
  62.1 6.4 %collective-permute-start.8 = (f32[32,640]{1,0:T(8,128)S(1)}, f32[32,640]{1,0:T(8,128)S(1)}, u32[]{:S(2)}, u32[]{:S(2)}) collective-permute-start(f32[32,640]{1,0:T(8,128)S(1)} %add.91), channel_id=1, source_target_pairs={{0,48},{8,56},{16,32},{24,40},{32,16},{40,24},{48,0},{56,8},{64,11... | collective-permute-start | bytes 245768 | tf_op jit(solution)/shard_map/ppermute | solution.py:350
  68.5 6.5 %collective-permute-start.13 = (f32[32,640]{1,0:T(8,128)S(1)}, f32[32,640]{1,0:T(8,128)S(1)}, u32[]{:S(2)}, u32[]{:S(2)}) collective-permute-start(f32[32,640]{1,0:T(8,128)S(1)} %add_add_fusion.5), channel_id=1, source_target_pairs={{0,128},{8,136},{16,144},{24,152},{32,160},{40,168},{48,176},{56,1... | collective-permute-start | bytes 245768 | tf_op jit(solution)/shard_map/ppermute | solution.py:350
  70.8 5.0 %collective-permute-start.12 = (f32[32,640]{1,0:T(8,128)S(1)}, f32[32,640]{1,0:T(8,128)S(1)}, u32[]{:S(2)}, u32[]{:S(2)}) collective-permute-start(f32[32,640]{1,0:T(8,128)S(1)} %add_add_fusion.5), channel_id=1, source_target_pairs={{0,64},{8,72},{16,80},{24,88},{32,96},{40,104},{48,112},{56,120},{... | collective-permute-start | bytes 245768 | tf_op jit(solution)/shard_map/ppermute | solution.py:350
  72.1 4.4 %collective-permute-start.11 = (f32[32,640]{1,0:T(8,128)S(1)}, f32[32,640]{1,0:T(8,128)S(1)}, u32[]{:S(2)}, u32[]{:S(2)}) collective-permute-start(f32[32,640]{1,0:T(8,128)S(1)} %add_add_fusion.5), channel_id=1, source_target_pairs={{0,192},{8,200},{16,208},{24,216},{32,224},{40,232},{48,240},{56,2... | collective-permute-start | bytes 245768 | tf_op jit(solution)/shard_map/ppermute | solution.py:350
  109.3 1.4 collective-permute-start.14
  110.6 6.9 %collective-permute-start.17 = (f32[32,640]{1,0:T(8,128)S(1)}, f32[32,640]{1,0:T(8,128)S(1)}, u32[]{:S(2)}, u32[]{:S(2)}) collective-permute-start(f32[32,640]{1,0:T(8,128)S(1)} %add.98), channel_id=1, source_target_pairs={{0,32},{8,40},{16,48},{24,56},{32,0},{40,8},{48,16},{56,24},{64,96... | collective-permute-start | bytes 245768 | tf_op jit(solution)/shard_map/ppermute | solution.py:350
  111.9 5.7 %collective-permute-start.16 = (f32[32,640]{1,0:T(8,128)S(1)}, f32[32,640]{1,0:T(8,128)S(1)}, u32[]{:S(2)}, u32[]{:S(2)}) collective-permute-start(f32[32,640]{1,0:T(8,128)S(1)} %add.98), channel_id=1, source_target_pairs={{0,16},{8,24},{16,0},{24,8},{32,48},{40,56},{48,32},{56,40},{64,80... | collective-permute-start | bytes 245768 | tf_op jit(solution)/shard_map/ppermute | solution.py:350
  111.9 6.6 %collective-permute-start.15 = (f32[32,640]{1,0:T(8,128)S(1)}, f32[32,640]{1,0:T(8,128)S(1)}, u32[]{:S(2)}, u32[]{:S(2)}) collective-permute-start(f32[32,640]{1,0:T(8,128)S(1)} %add.98), channel_id=1, source_target_pairs={{0,48},{8,56},{16,32},{24,40},{32,16},{40,24},{48,0},{56,8},{64,11... | collective-permute-start | bytes 245768 | tf_op jit(solution)/shard_map/ppermute | solution.py:350
  118.5 6.6 %collective-permute-start.20 = (f32[32,640]{1,0:T(8,128)S(1)}, f32[32,640]{1,0:T(8,128)S(1)}, u32[]{:S(2)}, u32[]{:S(2)}) collective-permute-start(f32[32,640]{1,0:T(8,128)S(1)} %add_add_fusion.3), channel_id=1, source_target_pairs={{0,128},{8,136},{16,144},{24,152},{32,160},{40,168},{48,176},{56,1... | collective-permute-start | bytes 245768 | tf_op jit(solution)/shard_map/ppermute | solution.py:350
  120.3 4.9 %collective-permute-start.19 = (f32[32,640]{1,0:T(8,128)S(1)}, f32[32,640]{1,0:T(8,128)S(1)}, u32[]{:S(2)}, u32[]{:S(2)}) collective-permute-start(f32[32,640]{1,0:T(8,128)S(1)} %add_add_fusion.3), channel_id=1, source_target_pairs={{0,64},{8,72},{16,80},{24,88},{32,96},{40,104},{48,112},{56,120},{... | collective-permute-start | bytes 245768 | tf_op jit(solution)/shard_map/ppermute | solution.py:350
  120.9 5.1 %collective-permute-start.18 = (f32[32,640]{1,0:T(8,128)S(1)}, f32[32,640]{1,0:T(8,128)S(1)}, u32[]{:S(2)}, u32[]{:S(2)}) collective-permute-start(f32[32,640]{1,0:T(8,128)S(1)} %add_add_fusion.3), channel_id=1, source_target_pairs={{0,192},{8,200},{16,208},{24,216},{32,224},{40,232},{48,240},{56,2... | collective-permute-start | bytes 245768 | tf_op jit(solution)/shard_map/ppermute | solution.py:350
  159.0 1.4 collective-permute-start.21
  160.4 6.9 %collective-permute-start.24 = (f32[32,640]{1,0:T(8,128)S(1)}, f32[32,640]{1,0:T(8,128)S(1)}, u32[]{:S(2)}, u32[]{:S(2)}) collective-permute-start(f32[32,640]{1,0:T(8,128)S(1)} %add.105), channel_id=1, source_target_pairs={{0,32},{8,40},{16,48},{24,56},{32,0},{40,8},{48,16},{56,24},{64,96... | collective-permute-start | bytes 245768 | tf_op jit(solution)/shard_map/ppermute | solution.py:350
  160.5 6.8 %collective-permute-start.23 = (f32[32,640]{1,0:T(8,128)S(1)}, f32[32,640]{1,0:T(8,128)S(1)}, u32[]{:S(2)}, u32[]{:S(2)}) collective-permute-start(f32[32,640]{1,0:T(8,128)S(1)} %add.105), channel_id=1, source_target_pairs={{0,16},{8,24},{16,0},{24,8},{32,48},{40,56},{48,32},{56,40},{64,80... | collective-permute-start | bytes 245768 | tf_op jit(solution)/shard_map/ppermute | solution.py:350
  160.7 7.5 %collective-permute-start.22 = (f32[32,640]{1,0:T(8,128)S(1)}, f32[32,640]{1,0:T(8,128)S(1)}, u32[]{:S(2)}, u32[]{:S(2)}) collective-permute-start(f32[32,640]{1,0:T(8,128)S(1)} %add.105), channel_id=1, source_target_pairs={{0,48},{8,56},{16,32},{24,40},{32,16},{40,24},{48,0},{56,8},{64,11... | collective-permute-start | bytes 245768 | tf_op jit(solution)/shard_map/ppermute | solution.py:350
  168.2 6.7 %collective-permute-start.27 = (f32[32,640]{1,0:T(8,128)S(1)}, f32[32,640]{1,0:T(8,128)S(1)}, u32[]{:S(2)}, u32[]{:S(2)}) collective-permute-start(f32[32,640]{1,0:T(8,128)S(1)} %add_add_fusion.1), channel_id=1, source_target_pairs={{0,128},{8,136},{16,144},{24,152},{32,160},{40,168},{48,176},{56,1... | collective-permute-start | bytes 245768 | tf_op jit(solution)/shard_map/ppermute | solution.py:350
  169.9 5.1 %collective-permute-start.26 = (f32[32,640]{1,0:T(8,128)S(1)}, f32[32,640]{1,0:T(8,128)S(1)}, u32[]{:S(2)}, u32[]{:S(2)}) collective-permute-start(f32[32,640]{1,0:T(8,128)S(1)} %add_add_fusion.1), channel_id=1, source_target_pairs={{0,64},{8,72},{16,80},{24,88},{32,96},{40,104},{48,112},{56,120},{... | collective-permute-start | bytes 245768 | tf_op jit(solution)/shard_map/ppermute | solution.py:350
  171.0 4.8 %collective-permute-start.25 = (f32[32,640]{1,0:T(8,128)S(1)}, f32[32,640]{1,0:T(8,128)S(1)}, u32[]{:S(2)}, u32[]{:S(2)}) collective-permute-start(f32[32,640]{1,0:T(8,128)S(1)} %add_add_fusion.1), channel_id=1, source_target_pairs={{0,192},{8,200},{16,208},{24,216},{32,224},{40,232},{48,240},{56,2... | collective-permute-start | bytes 245768 | tf_op jit(solution)/shard_map/ppermute | solution.py:350
